TPU v7x, 32 devices: a whole 2x2x4 slice. The times are simulated.
32 devices in a mesh: lat: 4 (over x, core), lon: 8 (over z, y).
Axes of the slice: x: 2, y: 2, z: 4, core: 2. Of those that a mesh axis runs over, the one named last changes fastest.
Arguments:
- pre_act: bfloat16 [256, 256, 256], P('lat', 'lon'), may hold values from -8 to 8
- cotangent: bfloat16 [256, 256, 256], P('lat', 'lon'), may hold values from -6 to 6
- spec_weight: float32 [128, 2, 256], replicated, may hold values from -3 to 3
- disco_weight: bfloat16 [3, 256, 256], replicated, may hold values from -0.375 to 0.375
- disco_filter: float32 [3, 256, 5, 5], replicated, may hold values from -0.6 to 0.6
- support: int32 [256, 5], replicated, may hold values from 0 to 2
Outputs:
- grad_input: bfloat16 [256, 256, 256], P('lat', 'lon')
All inputs are finite; a program needn't handle non-finite values.
Results may differ from a plain program's by a relative error of at most 0.007.
Values may be sent and summed in bfloat16 or wider, within the bound.
No kernel may reach another device: no remote copies, remote signals or barrier semaphores. Data moves between devices by JAX's collectives and lax.ppermute only.
A program may use at most 192 MiB of HBM per device.

v0:
```python
import functools
import math

import jax
import jax.numpy as jnp
import numpy as np
from jax import lax
from jax.experimental import pallas as pl
from jax.experimental.pallas import tpu as pltpu
from jax.sharding import PartitionSpec as P

REACH = 2
TAPS = 2 * REACH + 1
LANES = 128
F32 = jnp.float32
BF16 = jnp.bfloat16
VMEM_LIMIT = 56 * 1024 * 1024


def params():
    return pltpu.CompilerParams(vmem_limit_bytes=VMEM_LIMIT)


def gelu_slope(pre_values):
    normal_cdf = 0.5 * (1.0 + lax.erf(pre_values * (1.0 / math.sqrt(2.0))))
    density = jnp.exp(-0.5 * pre_values * pre_values) * (1.0 / math.sqrt(2.0 * math.pi))
    return normal_cdf + pre_values * density


def grad_kernel(flip_ref, pre_ref, cot_ref, grad_ref, send_ref, rows_scr, chan_scr, *, group, q_count):
    step = pl.program_id(0)
    rows, cols, channels = pre_ref.shape
    flip = flip_ref[0]
    for row in range(rows):
        pre = pre_ref[row].astype(F32)
        grad = (cot_ref[row].astype(F32) * gelu_slope(pre)).astype(BF16)
        grad_ref[row] = grad
        rows_scr[row] = grad.astype(F32)
    for block in range(rows // group):
        q_index = step * (rows // group) + block
        q_out = jnp.where(flip == 1, q_count - 1 - q_index, q_index)
        parts = []
        for r in range(group):
            source = block * group + jnp.where(flip == 1, group - 1 - r, r)
            parts.append(rows_scr[source])
        stacked = jnp.concatenate(parts, axis=0)
        for tile in range(channels // LANES):
            turned = stacked[:, tile * LANES : (tile + 1) * LANES].T
            chan_scr[pl.ds(tile * LANES * q_count + q_out, LANES, stride=q_count), :] = turned

    @pl.when(step == pl.num_programs(0) - 1)
    def _():
        for dest in range(send_ref.shape[0]):
            count = send_ref.shape[1]
            send_ref[dest] = chan_scr[dest * count : (dest + 1) * count, :].astype(BF16)


def gradient(pre_act, cotangent, flip, devices, group):
    rows, cols, channels = pre_act.shape
    q_count = rows // group
    steps = 4
    block = (rows // steps, cols, channels)
    spec = pl.BlockSpec(block, lambda i: (i, 0, 0))
    send = (devices, channels // devices * q_count, LANES)
    return pl.pallas_call(
        functools.partial(grad_kernel, group=group, q_count=q_count),
        grid=(steps,),
        in_specs=[pl.BlockSpec(memory_space=pltpu.SMEM), spec, spec],
        out_specs=[spec, pl.BlockSpec(send, lambda i: (0, 0, 0))],
        out_shape=[
            jax.ShapeDtypeStruct(pre_act.shape, BF16),
            jax.ShapeDtypeStruct(send, BF16),
        ],
        scratch_shapes=[
            pltpu.VMEM(block, F32),
            pltpu.VMEM((channels * q_count, LANES), F32),
        ],
        compiler_params=params(),
        name="gradient",
    )(flip, pre_act, cotangent)


def legendre_kernel(cos_ref, start_ref, table_ref, scr, *, degrees, span):
    orders = table_ref.shape[0]
    groups = orders // 8
    first = pl.program_id(0) * orders
    cosine = jnp.broadcast_to(cos_ref[...], (8, LANES))
    sub = lax.broadcasted_iota(jnp.int32, (8, LANES), 0)
    order_vals = [(first + 8 * g + sub).astype(F32) for g in range(groups)]
    squares = [order * order for order in order_vals]
    zero = jnp.zeros((8, LANES), F32)

    def chunk(index, state):
        latest, earlier, scale = (list(part) for part in state)
        factor = [jnp.exp(value) for value in scale]
        for step in range(span):
            degree = index * span + step
            deg_val = degree.astype(F32)
            square = deg_val * deg_val
            prev = (deg_val - 1.0) * (deg_val - 1.0)
            upper = jnp.full((8, LANES), jnp.maximum(4.0 * square - 1.0, 0.0))
            lower = jnp.full((8, LANES), jnp.maximum(4.0 * prev - 1.0, 1.0))
            for g in range(groups):
                coef_a = jnp.sqrt(upper / jnp.maximum(square - squares[g], 1.0))
                coef_b = jnp.sqrt(jnp.maximum(prev - squares[g], 0.0) / lower)
                value = coef_a * (cosine * latest[g] - coef_b * earlier[g])
                value = jnp.where(order_vals[g] == deg_val, 1.0, value)
                earlier[g] = latest[g]
                latest[g] = value
                scr[pl.ds(g * 8 * degrees + degree, 8, stride=degrees), :] = value * factor[g]
        for g in range(groups):
            large = jnp.maximum(jnp.abs(latest[g]), jnp.abs(earlier[g])) > 2.0**20
            shrink = jnp.where(large, 2.0**-40, 1.0)
            latest[g] = latest[g] * shrink
            earlier[g] = earlier[g] * shrink
            scale[g] = scale[g] + jnp.where(large, 40.0 * math.log(2.0), 0.0)
        return (tuple(latest), tuple(earlier), tuple(scale))

    starts = tuple(start_ref[8 * g : 8 * g + 8, :] for g in range(groups))
    zeros = (zero,) * groups
    lax.fori_loop(0, degrees // span, chunk, (zeros, zeros, starts))
    for order in range(orders):
        table_ref[order] = scr[order * degrees : (order + 1) * degrees, :].astype(BF16)


def legendre(cosine, start, degrees):
    orders, points = start.shape
    block = math.gcd(orders, 32)
    return pl.pallas_call(
        functools.partial(legendre_kernel, degrees=degrees, span=8),
        grid=(orders // block, points // LANES),
        in_specs=[
            pl.BlockSpec((1, LANES), lambda i, j: (0, j)),
            pl.BlockSpec((block, LANES), lambda i, j: (i, j)),
        ],
        out_specs=pl.BlockSpec((block, degrees, LANES), lambda i, j: (i, 0, j)),
        out_shape=jax.ShapeDtypeStruct((orders, degrees, points), BF16),
        scratch_shapes=[pltpu.VMEM((block * degrees, LANES), F32)],
        compiler_params=params(),
        cost_estimate=pl.CostEstimate(
            flops=40 * orders * degrees * points,
            bytes_accessed=2 * orders * degrees * points,
            transcendentals=0,
        ),
        name="legendre",
    )(cosine, start)


def spectral_kernel(
    recv_ref, forward_ref, inverse_ref, table_ref, weight_ref, quad_ref, back_ref,
    grid_scr, even_scr, odd_scr, north_scr, south_scr, *, group, q_count, unroll,
):
    step = pl.program_id(0)
    bands, sectors = recv_ref.shape[:2]
    local, lats, lons = grid_scr.shape
    orders_here, degrees, half = table_ref.shape
    tiles = half // LANES
    modes = forward_ref.shape[0]
    orders = modes // 2
    band_rows = group * q_count
    width = LANES // group
    lane_group = lax.broadcasted_iota(jnp.int32, (q_count, LANES), 1) // width

    def place(band, r):
        if band < bands // 2:
            return band * band_rows + r * q_count
        return lats // 2 + (bands - 1 - band) * band_rows + r * q_count

    def rolled(value, places):
        shift = places * width % LANES
        return value if shift == 0 else pltpu.roll(value, shift, 1)

    @pl.when(step == 0)
    def _():
        for chan in range(local):
            at = chan * q_count
            for band in range(bands):
                for unit in range(sectors // group):
                    pieces = [
                        recv_ref[band, unit * group + k, at : at + q_count, :].astype(F32)
                        for k in range(group)
                    ]
                    for r in range(group):
                        value = rolled(pieces[0], -r)
                        for k in range(1, group):
                            value = jnp.where(lane_group == k, rolled(pieces[k], k - r), value)
                        row = place(band, r)
                        grid_scr[chan, row : row + q_count, unit * LANES : (unit + 1) * LANES] = (
                            value.astype(BF16)
                        )
            spectrum = lax.dot_general(
                forward_ref[...], grid_scr[chan], (((1,), (1,)), ((), ())), preferred_element_type=F32
            )
            for tile in range(tiles):
                north = spectrum[:, tile * LANES : (tile + 1) * LANES]
                south = spectrum[:, half + tile * LANES : half + (tile + 1) * LANES]
                even_scr[tile, chan * modes : (chan + 1) * modes, :] = north + south
                odd_scr[tile, chan * modes : (chan + 1) * modes, :] = north - south

    def lines(scr, tile, mode):
        if local == 1:
            return (tile, pl.ds(mode, 1), slice(None))
        return (tile, pl.ds(mode, local, stride=modes), slice(None))

    def load(scr, mode):
        parts = [scr[lines(scr, tile, mode)] for tile in range(tiles)]
        return parts[0] if tiles == 1 else jnp.concatenate(parts, axis=1)

    degree_lane = lax.broadcasted_iota(jnp.int32, (local, degrees), 1)
    real_w = weight_ref[0]
    imag_w = weight_ref[1]
    quad = quad_ref[...]

    def one_order(index):
        order = step * orders_here + index
        table = table_ref[index]
        even = (degree_lane + order) % 2 == 0
        stacked = jnp.concatenate(
            [
                load(even_scr, order),
                load(even_scr, orders + order),
                load(odd_scr, order),
                load(odd_scr, orders + order),
            ],
            axis=0,
        ).astype(BF16)
        analysed = lax.dot_general(
            stacked, table, (((1,), (1,)), ((), ())), preferred_element_type=F32
        )
        real_a = jnp.where(even, analysed[0:local], analysed[2 * local : 3 * local])
        imag_a = jnp.where(even, analysed[local : 2 * local], analysed[3 * local : 4 * local])
        real_m = real_w * real_a + imag_w * imag_a
        imag_m = real_w * imag_a - imag_w * real_a
        mixed = jnp.concatenate(
            [
                jnp.where(even, real_m, 0.0),
                jnp.where(even, imag_m, 0.0),
                jnp.where(even, 0.0, real_m),
                jnp.where(even, 0.0, imag_m),
            ],
            axis=0,
        ).astype(BF16)
        synth = jnp.dot(mixed, table, preferred_element_type=F32) * quad
        for part in range(2):
            even_part = synth[part * local : (part + 1) * local]
            odd_part = synth[(2 + part) * local : (3 + part) * local]
            for tile in range(tiles):
                lanes = slice(tile * LANES, (tile + 1) * LANES)
                where = lines(north_scr, tile, part * orders + order)
                north_scr[where] = even_part[:, lanes] + odd_part[:, lanes]
                south_scr[where] = even_part[:, lanes] - odd_part[:, lanes]

    def several(index, carry):
        for inner in range(unroll):
            one_order(index * unroll + inner)
        return carry

    lax.fori_loop(0, orders_here // unroll, several, 0)

    @pl.when(step == pl.num_programs(0) - 1)
    def _():
        for chan in range(local):
            rows = slice(chan * modes, (chan + 1) * modes)
            profile = jnp.concatenate(
                [scr[tile, rows, :].astype(BF16) for scr in (north_scr, south_scr) for tile in range(tiles)],
                axis=1,
            )
            field = lax.dot_general(
                profile, inverse_ref[...], (((0,), (0,)), ((), ())), preferred_element_type=F32
            )
            at = chan * q_count
            for band in range(bands):
                for unit in range(sectors // group):
                    pieces = []
                    for r in range(group):
                        row = place(band, r)
                        pieces.append(field[row : row + q_count, unit * LANES : (unit + 1) * LANES])
                    for k in range(group):
                        value = rolled(pieces[0], -k)
                        for r in range(1, group):
                            value = jnp.where(lane_group == r, rolled(pieces[r], r - k), value)
                        back_ref[band, unit * group + k, at : at + q_count, :] = value.astype(BF16)


def spectral(received, forward, inverse, table, weights, quad, group):
    bands, sectors, rows, _ = received.shape
    local = weights.shape[1]
    q_count = rows // local
    orders, degrees, half = table.shape
    lons = forward.shape[1]
    block = max(1, min(orders, 2**19 // (degrees * half)))
    tiles = half // LANES

    def whole(shape):
        return pl.BlockSpec(shape, lambda i: (0,) * len(shape))

    lines = pltpu.VMEM((tiles, local * forward.shape[0], LANES), F32)
    return pl.pallas_call(
        functools.partial(spectral_kernel, group=group, q_count=q_count, unroll=math.gcd(block, 8)),
        grid=(orders // block,),
        in_specs=[
            whole(received.shape),
            whole(forward.shape),
            whole(inverse.shape),
            pl.BlockSpec((block, degrees, half), lambda i: (i, 0, 0)),
            whole(weights.shape),
            whole(quad.shape),
        ],
        out_specs=whole(received.shape),
        out_shape=jax.ShapeDtypeStruct(received.shape, BF16),
        scratch_shapes=[pltpu.VMEM((local, 2 * half, lons), BF16), lines, lines, lines, lines],
        compiler_params=params(),
        name="spectral",
    )(received, forward, inverse, table, weights, quad)


def disco_kernel(tap_ref, grad_ref, low_ref, high_ref, left_ref, right_ref, mix_ref, out_ref, padded, taps_scr):
    step = pl.program_id(0)
    rows, cols, channels = grad_ref.shape
    rows_here = out_ref.shape[0]
    kernels = mix_ref.shape[0]
    halves = channels // LANES
    origin = 8

    @pl.when(step == 0)
    def _():
        for half in range(halves):
            lanes = slice(half * LANES, (half + 1) * LANES)
            padded[half, REACH : REACH + rows, origin : origin + cols, :] = grad_ref[:, :, lanes].astype(F32)
            padded[half, 0:REACH, origin : origin + cols, :] = low_ref[:, :, lanes].astype(F32)
            padded[half, REACH + rows :, origin : origin + cols, :] = high_ref[:, :, lanes].astype(F32)
            for side in range(REACH):
                padded[half, :, origin - REACH + side, :] = left_ref[side, :, lanes].astype(F32)
                padded[half, :, origin + cols + side, :] = right_ref[side, :, lanes].astype(F32)

    def one_row(row, carry):
        for half in range(halves):
            sums = [jnp.zeros((cols, LANES), F32) for _ in range(kernels)]
            for lat_tap in range(TAPS):
                source = step * rows_here + row + 2 * REACH - lat_tap
                for lon_tap in range(TAPS):
                    start = origin + REACH - lon_tap
                    slab = padded[half, source, start : start + cols, :]
                    for kernel in range(kernels):
                        tap = tap_ref[source, (kernel * TAPS + lat_tap) * TAPS + lon_tap]
                        sums[kernel] = sums[kernel] + tap * slab
            for kernel in range(kernels):
                taps_scr[kernel, row, :, half * LANES : (half + 1) * LANES] = sums[kernel].astype(BF16)
        return carry

    lax.fori_loop(0, rows_here, one_row, 0)
    total = None
    for kernel in range(kernels):
        flat = taps_scr[kernel].reshape(rows_here * cols, channels)
        term = lax.dot_general(
            flat, mix_ref[kernel], (((1,), (1,)), ((), ())), preferred_element_type=F32
        )
        total = term if total is None else total + term
    out_ref[...] = total.reshape(rows_here, cols, channels)


def disco(taps, grad, low, high, left, right, mix):
    rows, cols, channels = grad.shape
    kernels = mix.shape[0]
    steps = 4

    def whole(shape):
        return pl.BlockSpec(shape, lambda i: (0,) * len(shape))

    return pl.pallas_call(
        disco_kernel,
        grid=(steps,),
        in_specs=[pl.BlockSpec(memory_space=pltpu.SMEM)]
        + [whole(value.shape) for value in (grad, low, high, left, right, mix)],
        out_specs=pl.BlockSpec((rows // steps, cols, channels), lambda i: (i, 0, 0)),
        out_shape=jax.ShapeDtypeStruct(grad.shape, F32),
        scratch_shapes=[
            pltpu.VMEM((channels // LANES, rows + 2 * REACH, cols + 16, LANES), F32),
            pltpu.VMEM((kernels, rows // steps, cols, channels), BF16),
        ],
        compiler_params=params(),
        cost_estimate=pl.CostEstimate(
            flops=1000 * rows * cols * channels, bytes_accessed=8 * rows * cols * channels, transcendentals=0
        ),
        name="disco",
    )(taps, grad, low, high, left, right, mix)


def combine_kernel(flip_ref, back_ref, disco_ref, out_ref, chan_scr, *, group, q_count):
    step = pl.program_id(0)
    rows, cols, channels = out_ref.shape
    flip = flip_ref[0]

    @pl.when(step == 0)
    def _():
        count = back_ref.shape[1]
        for source in range(back_ref.shape[0]):
            chan_scr[source * count : (source + 1) * count, :] = back_ref[source].astype(F32)

    for block in range(rows // group):
        q_index = step * (rows // group) + block
        q_from = jnp.where(flip == 1, q_count - 1 - q_index, q_index)
        turned = jnp.concatenate(
            [
                chan_scr[pl.ds(tile * LANES * q_count + q_from, LANES, stride=q_count), :].T
                for tile in range(channels // LANES)
            ],
            axis=1,
        )
        for r in range(group):
            row = block * group + jnp.where(flip == 1, group - 1 - r, r)
            out_ref[row] = (disco_ref[row] + turned[r * cols : (r + 1) * cols]).astype(BF16)


def combine(back, local_part, flip, group):
    rows, cols, channels = local_part.shape
    q_count = rows // group
    steps = 4
    spec = pl.BlockSpec((rows // steps, cols, channels), lambda i: (i, 0, 0))
    return pl.pallas_call(
        functools.partial(combine_kernel, group=group, q_count=q_count),
        grid=(steps,),
        in_specs=[pl.BlockSpec(memory_space=pltpu.SMEM), pl.BlockSpec(back.shape, lambda i: (0, 0, 0)), spec],
        out_specs=spec,
        out_shape=jax.ShapeDtypeStruct(local_part.shape, BF16),
        scratch_shapes=[pltpu.VMEM((channels * q_count, LANES), F32)],
        compiler_params=params(),
        name="combine",
    )(flip, back, local_part)


def neighbours(axis, block_low, block_high):
    count = lax.axis_size(axis)
    forward = [(i, (i + 1) % count) for i in range(count)]
    backward = [(target, source) for source, target in forward]
    return (lax.ppermute(block_low, axis, forward), lax.ppermute(block_high, axis, backward))


def fourier_tables(order_count, points):
    order_list = jnp.arange(order_count, dtype=jnp.int32)[:, None]
    grid_pos = jnp.arange(points, dtype=jnp.int32)[None, :]
    angles = 2.0 * math.pi / points * (grid_pos * order_list % points).astype(F32)
    factor = jnp.where(order_list == 0, 1.0, 2.0).astype(F32)
    inverse = jnp.concatenate([jnp.cos(angles), -jnp.sin(angles)], axis=0)
    forward = jnp.concatenate([factor, factor], axis=0) * inverse
    return (forward.astype(BF16), inverse.astype(BF16))


def shards(pre_act, cotangent, spec_weight, disco_weight, disco_filter, support):
    lat_rows, lon_cols, channels = pre_act.shape
    lat_count = lax.axis_size("lat")
    lon_count = lax.axis_size("lon")
    devices = lat_count * lon_count
    band_index = lax.axis_index("lat")
    device_id = band_index * lon_count + lax.axis_index("lon")
    total_lat = lat_rows * lat_count
    total_lon = lon_cols * lon_count
    mode_count = spec_weight.shape[0]
    local = channels // devices
    group = LANES // lon_cols
    q_count = lat_rows // group
    flip = (2 * band_index >= lat_count).astype(jnp.int32).reshape(1)

    grad_pre, to_send = gradient(pre_act, cotangent, flip, devices, group)
    received = lax.all_to_all(to_send, ("lat", "lon"), 0, 0, tiled=True)

    low, high = neighbours("lat", grad_pre[-REACH:], grad_pre[:REACH])
    west = jnp.concatenate([part[:, :REACH] for part in (low, grad_pre, high)], axis=0)
    east = jnp.concatenate([part[:, -REACH:] for part in (low, grad_pre, high)], axis=0)
    left, right = neighbours("lon", jnp.transpose(east, (1, 0, 2)), jnp.transpose(west, (1, 0, 2)))

    lane = np.arange(total_lat // 2)
    lats = lane // lat_rows * lat_rows + lane % q_count * group + lane % lat_rows // q_count
    colatitude = math.pi / total_lat * (jnp.asarray(lats, F32) + 0.5)[None, :]
    order_vals = jnp.arange(mode_count, dtype=F32)[:, None]
    start = (
        0.5 * jnp.log((2.0 * order_vals + 1.0) / (4.0 * math.pi))
        + 0.5
        * (
            lax.lgamma(2.0 * order_vals + 1.0)
            - order_vals * math.log(4.0)
            - 2.0 * lax.lgamma(order_vals + 1.0)
        )
        + order_vals * jnp.log(jnp.sin(colatitude))
    )
    table = legendre(jnp.cos(colatitude), start, mode_count)
    forward, inverse = fourier_tables(mode_count, total_lon)
    quad = 2.0 * math.pi / total_lon * (math.pi / total_lat) * jnp.sin(colatitude)
    weights = jnp.transpose(
        lax.dynamic_slice_in_dim(spec_weight, device_id * local, local, 2), (1, 2, 0)
    )
    offsets = jnp.arange(TAPS, dtype=jnp.int32) - REACH
    allowed = (jnp.abs(offsets)[None, None, :] <= support[:, :, None]).astype(F32)
    tap_coef = jnp.pad(disco_filter * allowed[None], ((0, 0), (REACH, REACH), (0, 0), (0, 0)))
    tap_coef = lax.dynamic_slice_in_dim(tap_coef, band_index * lat_rows, lat_rows + 2 * REACH, 1)
    taps = jnp.transpose(tap_coef, (1, 0, 2, 3)).reshape(lat_rows + 2 * REACH, -1)

    blocks = received.reshape(lat_count, lon_count, local * q_count, LANES)
    back = spectral(blocks, forward, inverse, table, weights, quad, group)
    back, taps = lax.optimization_barrier((back, taps))
    returned = lax.all_to_all(
        back.reshape(devices, local * q_count, LANES), ("lat", "lon"), 0, 0, tiled=True
    )
    local_part = disco(taps, grad_pre, low, high, left, right, disco_weight)
    return combine(returned, local_part, flip, group)


def solution(mesh):
    return jax.shard_map(
        shards,
        mesh=mesh,
        in_specs=(P("lat", "lon", None), P("lat", "lon", None), P(), P(), P(), P()),
        out_specs=P("lat", "lon", None),
        check_vma=False,
    )
```

profile of v0, /device:TPU:0, one launch (start us, length us, event | category | flops | bytes accessed | tf_op | source)
XLA Modules:
  0.0 118.6 jit_solution(193503077712518333)
XLA Ops:
  0.0 0.0 copy-start
  0.0 0.0 copy-start.8
  0.0 0.0 copy-start.7
  0.0 0.0 copy-start.4
  0.0 5.1 %gradient.1 = (bf16[64,32,256]{2,1,0:T(8,128)(2,1)}, bf16[32,128,128]{2,1,0:T(8,128)(2,1)}) custom-call(s32[1]{0:T(128)} %bitcast.flip_ref, bf16[64,32,256]{2,1,0:T(8,128)(2,1)} %pre_ref.1, bf16[64,32,256]{2,1,0:T(8,128)(2,1)} %cot_ref.1), custom_call_target="tpu_custom_call" | custom-call | tf_op jit(solution)/shard_map/gradient/pallas_call | solution.py:65
  5.1 7.4 %all-to-all-start = ((bf16[32,128,128]{2,1,0:T(8,128)(2,1)}), bf16[32,128,128]{2,1,0:T(8,128)(2,1)S(1)}, u32[]{:S(2)}, u32[]{:S(2)}) async-start(bf16[32,128,128]{2,1,0:T(8,128)(2,1)} %get-tuple-element.9), calls=%async_computation | async-start | bytes 2097152 | tf_op jit(solution)/shard_map/all_to_all | solution.py:465
  12.5 0.0 copy-done
  12.5 0.2 constant_dynamic-slice_fusion
  12.7 0.7 copy.25
  13.4 0.0 copy-done.7
  13.4 0.1 compare_convert_fusion
  13.4 0.0 copy-done.4
  13.5 0.1 fusion.8
  13.6 0.1 fusion.21
  13.7 0.0 copy-done.8
  13.7 0.7 multiply_add_fusion.start_ref
  14.4 14.9 %legendre.1.table_ref = bf16[128,128,128]{2,1,0:T(8,128)(2,1)} custom-call(f32[1,128]{1,0:T(1,128)} %constant.115.cos_ref, f32[128,128]{1,0:T(8,128)} %multiply_add_fusion.start_ref), custom_call_target="tpu_custom_call" | custom-call | flops 83886080 | bytes 4194304 | tf_op jit(solution)/shard_map/legendre/pallas_call | solution.py:129
  29.3 0.5 sine_negate_fusion
  29.9 0.7 fusion.inverse_ref
  30.6 0.8 multiply_convert_fusion.forward_ref
  31.3 8.7 %all-to-all-done = bf16[32,128,128]{2,1,0:T(8,128)(2,1)S(1)} async-done(((bf16[32,128,128]{2,1,0:T(8,128)(2,1)}), bf16[32,128,128]{2,1,0:T(8,128)(2,1)S(1)}, u32[]{:S(2)}, u32[]{:S(2)}) %all-to-all-start) | async-done | bytes 1048608 | tf_op jit(solution)/shard_map/all_to_all | solution.py:465
  40.0 0.0 copy-start.3
  40.1 1.0 copy-done.3
  41.0 0.0 copy-start.1
  41.0 26.8 %spectral.1 = bf16[4,8,128,128]{3,2,1,0:T(8,128)(2,1)} custom-call(bf16[4,8,128,128]{3,2,1,0:T(8,128)(2,1)} %bitcast.14, bf16[256,256]{1,0:T(8,128)(2,1)} %multiply_convert_fusion.forward_ref, bf16[256,256]{1,0:T(8,128)(2,1)} %fusion.inverse_ref, bf16[128,128,128]{2,1,0:T(8,128)(2,1)} %legendre.1.table_ref, f32[2,8,128]{2,1,0:T(8,128)} %bitcast.15, ...), custom_call_target="tpu_custom_call" | custom-call | tf_op jit(solution)/shard_map/spectral/pallas_call | solution.py:298
  67.9 2.6 %all-to-all-start.1 = ((bf16[32,128,128]{2,1,0:T(8,128)(2,1)}), bf16[32,128,128]{2,1,0:T(8,128)(2,1)S(1)}, u32[]{:S(2)}, u32[]{:S(2)}) async-start(bf16[32,128,128]{2,1,0:T(8,128)(2,1)} %bitcast.13), calls=%async_computation.1 | async-start | bytes 2097152 | tf_op jit(solution)/shard_map/all_to_all | solution.py:501
  70.5 0.0 copy-done.1
  70.5 0.6 copy.18
  71.1 0.1 fusion.23
  71.2 0.2 collective-permute-start
  71.3 1.6 %collective-permute-start.1 = (bf16[2,32,256]{2,0,1:T(2,128)(2,1)S(1)}, bf16[2,32,256]{2,0,1:T(2,128)(2,1)S(1)}, u32[]{:S(2)}, u32[]{:S(2)}) collective-permute-start(bf16[2,32,256]{2,0,1:T(2,128)(2,1)S(1)} %get-tuple-element.15), channel_id=1, source_target_pairs={{8,0},{16,8},{24,16},{0,24},{9,1},{17,9},{25,17},{1,25},{10,2},{18... | collective-permute-start | bytes 98312 | tf_op jit(solution)/shard_map/ppermute | solution.py:436
  73.0 5.4 %collective-permute-done = bf16[2,32,256]{2,0,1:T(2,128)(2,1)S(1)} collective-permute-done((bf16[2,32,256]{2,0,1:T(2,128)(2,1)S(1)}, bf16[2,32,256]{2,0,1:T(2,128)(2,1)S(1)}, u32[]{:S(2)}, u32[]{:S(2)}) %collective-permute-start) | collective-permute-done | bytes 32800 | tf_op jit(solution)/shard_map/ppermute | solution.py:436
  78.4 0.0 collective-permute-done.1
  78.5 1.7 %collective-permute-start.2 = (bf16[2,68,256]{2,1,0:T(8,128)(2,1)S(1)}, bf16[2,68,256]{2,1,0:T(8,128)(2,1)S(1)}, u32[]{:S(2)}, u32[]{:S(2)}) collective-permute-start(bf16[2,68,256]{2,1,0:T(8,128)(2,1)S(1)} %maximum_bitcast_fusion), channel_id=1, source_target_pairs={{0,1},{1,2},{2,3},{3,4},{4,5},{5,6},{6,7},{7,0},{8,9},{9,10},{10,1... | collective-permute-start | bytes 208904 | tf_op jit(solution)/shard_map/ppermute | solution.py:436
  80.2 4.6 %collective-permute-start.3 = (bf16[2,68,256]{2,1,0:T(8,128)(2,1)S(1)}, bf16[2,68,256]{2,1,0:T(8,128)(2,1)S(1)}, u32[]{:S(2)}, u32[]{:S(2)}) collective-permute-start(bf16[2,68,256]{2,1,0:T(8,128)(2,1)S(1)} %maximum_bitcast_fusion.1), channel_id=1, source_target_pairs={{1,0},{2,1},{3,2},{4,3},{5,4},{6,5},{7,6},{0,7},{9,8},{10,9},{11,1... | collective-permute-start | bytes 208904 | tf_op jit(solution)/shard_map/ppermute | solution.py:436
  84.8 0.6 copy.23.low_ref
  85.4 0.6 copy.24.high_ref
  86.0 0.7 copy.22.tap_ref
  86.7 7.9 %collective-permute-done.2.left_ref = bf16[2,68,256]{2,1,0:T(8,128)(2,1)S(1)} collective-permute-done((bf16[2,68,256]{2,1,0:T(8,128)(2,1)S(1)}, bf16[2,68,256]{2,1,0:T(8,128)(2,1)S(1)}, u32[]{:S(2)}, u32[]{:S(2)}) %collective-permute-start.2) | collective-permute-done | bytes 69664 | tf_op jit(solution)/shard_map/ppermute | solution.py:436
  94.6 0.0 copy-start.5
  94.6 0.0 collective-permute-done.3.right_ref
  94.6 0.6 copy-done.5
  95.2 0.0 copy-start.6
  95.2 0.6 copy-done.6
  95.8 17.1 %disco.1.disco_ref = f32[64,32,256]{2,1,0:T(8,128)} custom-call(f32[68,75]{1,0:T(8,128)} %copy.22.tap_ref, bf16[64,32,256]{2,1,0:T(8,128)(2,1)} %get-tuple-element.12.grad_ref, bf16[2,32,256]{2,1,0:T(8,128)(2,1)} %copy.23.low_ref, bf16[2,32,256]{2,1,0:T(8,128)(2,1)} %copy.24.high_ref, bf16[2,68,256]{2,1,0:T(8,128)(2,1)} %copy-done.5, ...), custom_call_target="tpu_custom_call" | custom-call | flops 524288000 | bytes 4194304 | tf_op jit(solution)/shard_map/disco/pallas_call | solution.py:370
  112.9 0.0 all-to-all-done.1.back_ref
  112.9 0.0 copy-start.2
  112.9 1.0 copy-done.2
  113.9 4.7 %combine.1 = bf16[64,32,256]{2,1,0:T(8,128)(2,1)} custom-call(s32[1]{0:T(128)} %bitcast.flip_ref, bf16[32,128,128]{2,1,0:T(8,128)(2,1)} %copy-done.2, f32[64,32,256]{2,1,0:T(8,128)} %disco.1.disco_ref), custom_call_target="tpu_custom_call" | custom-call | tf_op jit(solution)/shard_map/combine/pallas_call | solution.py:420
  (11 shorter events, 0.1 us)
Async XLA Ops:
  0.0 12.5 %copy-start = (f32[128,2,256]{2,1,0:T(2,128)S(1)}, f32[128,2,256]{2,1,0:T(2,128)}, u32[]{:S(2)}) copy-start(f32[128,2,256]{2,1,0:T(2,128)} %param.9) | copy-start | bytes 786436
  0.0 13.7 %copy-start.8 = (f32[128]{0:T(128)S(1)}, f32[128]{0:T(128)}, u32[]{:S(2)}) copy-start(f32[128]{0:T(128)} %constant.117) | copy-start | bytes 1540
  0.0 13.4 %copy-start.7 = (s32[256,5]{0,1:T(8,128)S(1)}, s32[256,5]{0,1:T(8,128)}, u32[]{:S(2)}) copy-start(s32[256,5]{0,1:T(8,128)} %param.12) | copy-start | bytes 15364
  0.0 13.4 %copy-start.4 = (f32[3,256,5,5]{1,0,3,2:T(4,128)S(1)}, f32[3,256,5,5]{1,0,3,2:T(4,128)}, u32[]{:S(2)}) copy-start(f32[3,256,5,5]{1,0,3,2:T(4,128)} %param.11) | copy-start | bytes 230404
  5.1 35.0 %all-to-all-start = ((bf16[32,128,128]{2,1,0:T(8,128)(2,1)}), bf16[32,128,128]{2,1,0:T(8,128)(2,1)S(1)}, u32[]{:S(2)}, u32[]{:S(2)}) async-start(bf16[32,128,128]{2,1,0:T(8,128)(2,1)} %get-tuple-element.9), calls=%async_computation | async-start | bytes 2097152 | tf_op jit(solution)/shard_map/all_to_all | solution.py:465
  40.0 1.0 copy-start.3
  41.0 29.5 %copy-start.1 = (bf16[64,32,256]{2,1,0:T(8,128)(2,1)S(1)}, bf16[64,32,256]{2,1,0:T(8,128)(2,1)}, u32[]{:S(2)}) copy-start(bf16[64,32,256]{2,1,0:T(8,128)(2,1)} %get-tuple-element.12.grad_ref) | copy-start | bytes 3145732
  67.9 45.1 %all-to-all-start.1 = ((bf16[32,128,128]{2,1,0:T(8,128)(2,1)}), bf16[32,128,128]{2,1,0:T(8,128)(2,1)S(1)}, u32[]{:S(2)}, u32[]{:S(2)}) async-start(bf16[32,128,128]{2,1,0:T(8,128)(2,1)} %bitcast.13), calls=%async_computation.1 | async-start | bytes 2097152 | tf_op jit(solution)/shard_map/all_to_all | solution.py:501
  71.2 7.2 %collective-permute-start = (bf16[2,32,256]{2,0,1:T(2,128)(2,1)S(1)}, bf16[2,32,256]{2,0,1:T(2,128)(2,1)S(1)}, u32[]{:S(2)}, u32[]{:S(2)}) collective-permute-start(bf16[2,32,256]{2,0,1:T(2,128)(2,1)S(1)} %get-tuple-element.16), channel_id=1, source_target_pairs={{0,8},{8,16},{16,24},{24,0},{1,9},{9,17},{17,25},{25,1},{2,10},{10... | collective-permute-start | bytes 98312 | tf_op jit(solution)/shard_map/ppermute | solution.py:436
  71.3 7.1 %collective-permute-start.1 = (bf16[2,32,256]{2,0,1:T(2,128)(2,1)S(1)}, bf16[2,32,256]{2,0,1:T(2,128)(2,1)S(1)}, u32[]{:S(2)}, u32[]{:S(2)}) collective-permute-start(bf16[2,32,256]{2,0,1:T(2,128)(2,1)S(1)} %get-tuple-element.15), channel_id=1, source_target_pairs={{8,0},{16,8},{24,16},{0,24},{9,1},{17,9},{25,17},{1,25},{10,2},{18... | collective-permute-start | bytes 98312 | tf_op jit(solution)/shard_map/ppermute | solution.py:436
  78.5 16.1 %collective-permute-start.2 = (bf16[2,68,256]{2,1,0:T(8,128)(2,1)S(1)}, bf16[2,68,256]{2,1,0:T(8,128)(2,1)S(1)}, u32[]{:S(2)}, u32[]{:S(2)}) collective-permute-start(bf16[2,68,256]{2,1,0:T(8,128)(2,1)S(1)} %maximum_bitcast_fusion), channel_id=1, source_target_pairs={{0,1},{1,2},{2,3},{3,4},{4,5},{5,6},{6,7},{7,0},{8,9},{9,10},{10,1... | collective-permute-start | bytes 208904 | tf_op jit(solution)/shard_map/ppermute | solution.py:436
  80.2 14.4 %collective-permute-start.3 = (bf16[2,68,256]{2,1,0:T(8,128)(2,1)S(1)}, bf16[2,68,256]{2,1,0:T(8,128)(2,1)S(1)}, u32[]{:S(2)}, u32[]{:S(2)}) collective-permute-start(bf16[2,68,256]{2,1,0:T(8,128)(2,1)S(1)} %maximum_bitcast_fusion.1), channel_id=1, source_target_pairs={{1,0},{2,1},{3,2},{4,3},{5,4},{6,5},{7,6},{0,7},{9,8},{10,9},{11,1... | collective-permute-start | bytes 208904 | tf_op jit(solution)/shard_map/ppermute | solution.py:436
  94.6 0.6 copy-start.5
  95.2 0.6 copy-start.6
  112.9 1.0 copy-start.2
where the time goes:
time: 120 us; the launch traced here: 119 us
  Pallas kernels  68.6 us (57%)
  waiting for transfers between devices  22 us (18%)
  starting transfers between devices  18.1 us (15%)
  local copies, waits for them, and re-layouts  6.82 us (6%)
  other arithmetic  2.93 us (2%)
    pallas_call x1, Pallas kernels, spectral(): pl.pallas_call(functools.partial(spectral_kernel, group=group, q_count=q_...  26.8 us
    pallas_call x1, Pallas kernels, disco(): pl.pallas_call(disco_kernel, grid=(steps,), in_specs=[pl.BlockSpec(memory...  17.1 us
    pallas_call x1, Pallas kernels, legendre(): pl.pallas_call(functools.partial(legendre_kernel, degrees=degrees, span=8...  14.9 us
    ppermute x2, waiting for transfers between devices, neighbours(): lax.ppermute(block_low, axis, forward)  13.3 us
    all_to_all x1, waiting for transfers between devices, shards(): received = lax.all_to_all(to_send, ('lat', 'lon'), 0, 0, tiled=True)  8.74 us
    all_to_all x1, starting transfers between devices, shards(): received = lax.all_to_all(to_send, ('lat', 'lon'), 0, 0, tiled=True)  7.37 us
    ppermute x2, starting transfers between devices, neighbours(): lax.ppermute(block_high, axis, backward)  6.28 us
    pallas_call x1, Pallas kernels, gradient(): pl.pallas_call(functools.partial(grad_kernel, group=group, q_count=q_coun...  5.06 us
  transfers between devices with their start and end apart: 6, of which 3 were waited for; matrix products, arithmetic and copies ran while one was open for 5% of the time, Pallas kernels for 27%

commit v1 on v0

--- a/solution.py
+++ b/solution.py
@@ -14,11 +14,11 @@
 LANES = 128
 F32 = jnp.float32
 BF16 = jnp.bfloat16
-VMEM_LIMIT = 56 * 1024 * 1024
-
-
-def params():
-    return pltpu.CompilerParams(vmem_limit_bytes=VMEM_LIMIT)
+MIB = 1024 * 1024
+
+
+def params(limit):
+    return pltpu.CompilerParams(vmem_limit_bytes=limit)
 
 
 def gelu_slope(pre_values):
@@ -27,7 +27,9 @@
     return normal_cdf + pre_values * density
 
 
-def grad_kernel(flip_ref, pre_ref, cot_ref, grad_ref, send_ref, rows_scr, chan_scr, *, group, q_count):
+def grad_kernel(
+    flip_ref, pre_ref, cot_ref, grad_ref, send_ref, first_ref, last_ref, rows_scr, chan_scr, *, group, q_count
+):
     step = pl.program_id(0)
     rows, cols, channels = pre_ref.shape
     flip = flip_ref[0]
@@ -48,8 +50,13 @@
             turned = stacked[:, tile * LANES : (tile + 1) * LANES].T
             chan_scr[pl.ds(tile * LANES * q_count + q_out, LANES, stride=q_count), :] = turned
 
+    @pl.when(step == 0)
+    def _():
+        first_ref[...] = grad_ref[:REACH]
+
     @pl.when(step == pl.num_programs(0) - 1)
     def _():
+        last_ref[...] = grad_ref[rows - REACH :]
         for dest in range(send_ref.shape[0]):
             count = send_ref.shape[1]
             send_ref[dest] = chan_scr[dest * count : (dest + 1) * count, :].astype(BF16)
@@ -62,25 +69,25 @@
     block = (rows // steps, cols, channels)
     spec = pl.BlockSpec(block, lambda i: (i, 0, 0))
     send = (devices, channels // devices * q_count, LANES)
+    edge = (REACH, cols, channels)
     return pl.pallas_call(
         functools.partial(grad_kernel, group=group, q_count=q_count),
         grid=(steps,),
         in_specs=[pl.BlockSpec(memory_space=pltpu.SMEM), spec, spec],
-        out_specs=[spec, pl.BlockSpec(send, lambda i: (0, 0, 0))],
-        out_shape=[
-            jax.ShapeDtypeStruct(pre_act.shape, BF16),
-            jax.ShapeDtypeStruct(send, BF16),
-        ],
+        out_specs=[spec, pl.BlockSpec(send, lambda i: (0, 0, 0))] + [pl.BlockSpec(edge, lambda i: (0, 0, 0))] * 2,
+        out_shape=[jax.ShapeDtypeStruct(shape, BF16) for shape in (pre_act.shape, send, edge, edge)],
         scratch_shapes=[
             pltpu.VMEM(block, F32),
             pltpu.VMEM((channels * q_count, LANES), F32),
         ],
-        compiler_params=params(),
+        compiler_params=params(60 * MIB),
         name="gradient",
     )(flip, pre_act, cotangent)
 
 
-def legendre_kernel(cos_ref, start_ref, table_ref, scr, *, degrees, span):
+def legendre_kernel(norm_ref, cos_ref, start_ref, *refs, degrees, span):
+    scr = refs[-1]
+    table_ref = refs[0]
     orders = table_ref.shape[0]
     groups = orders // 8
     first = pl.program_id(0) * orders
@@ -91,20 +98,19 @@
     zero = jnp.zeros((8, LANES), F32)
 
     def chunk(index, state):
-        latest, earlier, scale = (list(part) for part in state)
+        latest, earlier, coef_b, scale = (list(part) for part in state)
         factor = [jnp.exp(value) for value in scale]
         for step in range(span):
             degree = index * span + step
             deg_val = degree.astype(F32)
-            square = deg_val * deg_val
-            prev = (deg_val - 1.0) * (deg_val - 1.0)
-            upper = jnp.full((8, LANES), jnp.maximum(4.0 * square - 1.0, 0.0))
-            lower = jnp.full((8, LANES), jnp.maximum(4.0 * prev - 1.0, 1.0))
+            norm = norm_ref[0, degree]
+            inverse_norm = norm_ref[1, degree]
             for g in range(groups):
-                coef_a = jnp.sqrt(upper / jnp.maximum(square - squares[g], 1.0))
-                coef_b = jnp.sqrt(jnp.maximum(prev - squares[g], 0.0) / lower)
-                value = coef_a * (cosine * latest[g] - coef_b * earlier[g])
+                gap = jnp.maximum(deg_val * deg_val - squares[g], 1.0)
+                root = lax.rsqrt(gap)
+                value = (root * norm) * (cosine * latest[g] - coef_b[g] * earlier[g])
                 value = jnp.where(order_vals[g] == deg_val, 1.0, value)
+                coef_b[g] = gap * root * inverse_norm
                 earlier[g] = latest[g]
                 latest[g] = value
                 scr[pl.ds(g * 8 * degrees + degree, 8, stride=degrees), :] = value * factor[g]
@@ -114,42 +120,54 @@
             latest[g] = latest[g] * shrink
             earlier[g] = earlier[g] * shrink
             scale[g] = scale[g] + jnp.where(large, 40.0 * math.log(2.0), 0.0)
-        return (tuple(latest), tuple(earlier), tuple(scale))
+        return (tuple(latest), tuple(earlier), tuple(coef_b), tuple(scale))
 
     starts = tuple(start_ref[8 * g : 8 * g + 8, :] for g in range(groups))
     zeros = (zero,) * groups
-    lax.fori_loop(0, degrees // span, chunk, (zeros, zeros, starts))
+    lax.fori_loop(0, degrees // span, chunk, (zeros, zeros, zeros, starts))
     for order in range(orders):
-        table_ref[order] = scr[order * degrees : (order + 1) * degrees, :].astype(BF16)
-
-
-def legendre(cosine, start, degrees):
+        values = scr[order * degrees : (order + 1) * degrees, :]
+        table_ref[order] = values.astype(BF16)
+        for turned_ref in refs[1:-1]:
+            turned_ref[order] = values.T.astype(BF16)
+
+
+def legendre(norms, cosine, start, both):
     orders, points = start.shape
+    degrees = norms.shape[1]
     block = math.gcd(orders, 32)
     return pl.pallas_call(
         functools.partial(legendre_kernel, degrees=degrees, span=8),
         grid=(orders // block, points // LANES),
         in_specs=[
+            pl.BlockSpec(memory_space=pltpu.SMEM),
             pl.BlockSpec((1, LANES), lambda i, j: (0, j)),
             pl.BlockSpec((block, LANES), lambda i, j: (i, j)),
         ],
-        out_specs=pl.BlockSpec((block, degrees, LANES), lambda i, j: (i, 0, j)),
-        out_shape=jax.ShapeDtypeStruct((orders, degrees, points), BF16),
+        out_specs=[
+            pl.BlockSpec((block, degrees, LANES), lambda i, j: (i, 0, j)),
+            pl.BlockSpec((block, LANES, degrees), lambda i, j: (i, j, 0)),
+        ][: 1 + both],
+        out_shape=[
+            jax.ShapeDtypeStruct((orders, degrees, points), BF16),
+            jax.ShapeDtypeStruct((orders, points, degrees), BF16),
+        ][: 1 + both],
         scratch_shapes=[pltpu.VMEM((block * degrees, LANES), F32)],
-        compiler_params=params(),
+        compiler_params=params(56 * MIB),
         cost_estimate=pl.CostEstimate(
             flops=40 * orders * degrees * points,
-            bytes_accessed=2 * orders * degrees * points,
+            bytes_accessed=4 * orders * degrees * points,
             transcendentals=0,
         ),
         name="legendre",
-    )(cosine, start)
+    )(norms, cosine, start)
 
 
 def spectral_kernel(
-    recv_ref, forward_ref, inverse_ref, table_ref, weight_ref, quad_ref, back_ref,
-    grid_scr, even_scr, odd_scr, north_scr, south_scr, *, group, q_count, unroll,
+    from_ref, forward_ref, inverse_ref, weight_ref, quad_ref, *refs, group, q_count, unroll
 ):
+    *tables, back_ref, recv_ref, grid_scr, even_scr, odd_scr, north_scr, south_scr, copied = refs
+    table_ref = tables[0]
     step = pl.program_id(0)
     bands, sectors = recv_ref.shape[:2]
     local, lats, lons = grid_scr.shape
@@ -172,6 +190,9 @@
 
     @pl.when(step == 0)
     def _():
+        copy = pltpu.make_async_copy(from_ref, recv_ref, copied)
+        copy.start()
+        copy.wait()
         for chan in range(local):
             at = chan * q_count
             for band in range(bands):
@@ -224,9 +245,12 @@
             ],
             axis=0,
         ).astype(BF16)
-        analysed = lax.dot_general(
-            stacked, table, (((1,), (1,)), ((), ())), preferred_element_type=F32
-        )
+        if len(tables) == 2:
+            analysed = jnp.dot(stacked, tables[1][index], preferred_element_type=F32)
+        else:
+            analysed = lax.dot_general(
+                stacked, table, (((1,), (1,)), ((), ())), preferred_element_type=F32
+            )
         real_a = jnp.where(even, analysed[0:local], analysed[2 * local : 3 * local])
         imag_a = jnp.where(even, analysed[local : 2 * local], analysed[3 * local : 4 * local])
         real_m = real_w * real_a + imag_w * imag_a
@@ -282,11 +306,11 @@
                         back_ref[band, unit * group + k, at : at + q_count, :] = value.astype(BF16)
 
 
-def spectral(received, forward, inverse, table, weights, quad, group):
+def spectral(received, forward, inverse, tables, weights, quad, group):
     bands, sectors, rows, _ = received.shape
     local = weights.shape[1]
     q_count = rows // local
-    orders, degrees, half = table.shape
+    orders, degrees, half = tables[0].shape
     lons = forward.shape[1]
     block = max(1, min(orders, 2**19 // (degrees * half)))
     tiles = half // LANES
@@ -299,19 +323,27 @@
         functools.partial(spectral_kernel, group=group, q_count=q_count, unroll=math.gcd(block, 8)),
         grid=(orders // block,),
         in_specs=[
-            whole(received.shape),
+            pl.BlockSpec(memory_space=pl.ANY),
             whole(forward.shape),
             whole(inverse.shape),
-            pl.BlockSpec((block, degrees, half), lambda i: (i, 0, 0)),
             whole(weights.shape),
             whole(quad.shape),
-        ],
+        ]
+        + [pl.BlockSpec((block,) + table.shape[1:], lambda i: (i, 0, 0)) for table in tables],
         out_specs=whole(received.shape),
         out_shape=jax.ShapeDtypeStruct(received.shape, BF16),
-        scratch_shapes=[pltpu.VMEM((local, 2 * half, lons), BF16), lines, lines, lines, lines],
-        compiler_params=params(),
+        scratch_shapes=[
+            pltpu.VMEM(received.shape, BF16),
+            pltpu.VMEM((local, 2 * half, lons), BF16),
+            lines,
+            lines,
+            lines,
+            lines,
+            pltpu.SemaphoreType.DMA,
+        ],
+        compiler_params=params(50 * MIB),
         name="spectral",
-    )(received, forward, inverse, table, weights, quad)
+    )(received, forward, inverse, weights, quad, *tables)
 
 
 def disco_kernel(tap_ref, grad_ref, low_ref, high_ref, left_ref, right_ref, mix_ref, out_ref, padded, taps_scr):
@@ -378,7 +410,7 @@
             pltpu.VMEM((channels // LANES, rows + 2 * REACH, cols + 16, LANES), F32),
             pltpu.VMEM((kernels, rows // steps, cols, channels), BF16),
         ],
-        compiler_params=params(),
+        compiler_params=params(14 * MIB),
         cost_estimate=pl.CostEstimate(
             flops=1000 * rows * cols * channels, bytes_accessed=8 * rows * cols * channels, transcendentals=0
         ),
@@ -386,13 +418,16 @@
     )(taps, grad, low, high, left, right, mix)
 
 
-def combine_kernel(flip_ref, back_ref, disco_ref, out_ref, chan_scr, *, group, q_count):
+def combine_kernel(flip_ref, from_ref, disco_ref, out_ref, back_ref, chan_scr, copied, *, group, q_count):
     step = pl.program_id(0)
     rows, cols, channels = out_ref.shape
     flip = flip_ref[0]
 
     @pl.when(step == 0)
     def _():
+        copy = pltpu.make_async_copy(from_ref, back_ref, copied)
+        copy.start()
+        copy.wait()
         count = back_ref.shape[1]
         for source in range(back_ref.shape[0]):
             chan_scr[source * count : (source + 1) * count, :] = back_ref[source].astype(F32)
@@ -420,11 +455,15 @@
     return pl.pallas_call(
         functools.partial(combine_kernel, group=group, q_count=q_count),
         grid=(steps,),
-        in_specs=[pl.BlockSpec(memory_space=pltpu.SMEM), pl.BlockSpec(back.shape, lambda i: (0, 0, 0)), spec],
+        in_specs=[pl.BlockSpec(memory_space=pltpu.SMEM), pl.BlockSpec(memory_space=pl.ANY), spec],
         out_specs=spec,
         out_shape=jax.ShapeDtypeStruct(local_part.shape, BF16),
-        scratch_shapes=[pltpu.VMEM((channels * q_count, LANES), F32)],
-        compiler_params=params(),
+        scratch_shapes=[
+            pltpu.VMEM(back.shape, BF16),
+            pltpu.VMEM((channels * q_count, LANES), F32),
+            pltpu.SemaphoreType.DMA,
+        ],
+        compiler_params=params(10 * MIB),
         name="combine",
     )(flip, back, local_part)
 
@@ -461,13 +500,8 @@
     q_count = lat_rows // group
     flip = (2 * band_index >= lat_count).astype(jnp.int32).reshape(1)
 
-    grad_pre, to_send = gradient(pre_act, cotangent, flip, devices, group)
+    grad_pre, to_send, first_rows, last_rows = gradient(pre_act, cotangent, flip, devices, group)
     received = lax.all_to_all(to_send, ("lat", "lon"), 0, 0, tiled=True)
-
-    low, high = neighbours("lat", grad_pre[-REACH:], grad_pre[:REACH])
-    west = jnp.concatenate([part[:, :REACH] for part in (low, grad_pre, high)], axis=0)
-    east = jnp.concatenate([part[:, -REACH:] for part in (low, grad_pre, high)], axis=0)
-    left, right = neighbours("lon", jnp.transpose(east, (1, 0, 2)), jnp.transpose(west, (1, 0, 2)))
 
     lane = np.arange(total_lat // 2)
     lats = lane // lat_rows * lat_rows + lane % q_count * group + lane % lat_rows // q_count
@@ -483,7 +517,14 @@
         )
         + order_vals * jnp.log(jnp.sin(colatitude))
     )
-    table = legendre(jnp.cos(colatitude), start, mode_count)
+    degree_norm = jnp.sqrt(jnp.maximum(4.0 * jnp.square(jnp.arange(mode_count, dtype=F32)) - 1.0, 1.0))
+    norms = jnp.stack([degree_norm, 1.0 / degree_norm])
+    both = mode_count * mode_count * total_lat < 2**25
+    tables = legendre(norms, jnp.cos(colatitude), start, both)
+    low, high = neighbours("lat", last_rows, first_rows)
+    west = jnp.concatenate([part[:, :REACH] for part in (low, grad_pre, high)], axis=0)
+    east = jnp.concatenate([part[:, -REACH:] for part in (low, grad_pre, high)], axis=0)
+    left, right = neighbours("lon", jnp.transpose(east, (1, 0, 2)), jnp.transpose(west, (1, 0, 2)))
     forward, inverse = fourier_tables(mode_count, total_lon)
     quad = 2.0 * math.pi / total_lon * (math.pi / total_lat) * jnp.sin(colatitude)
     weights = jnp.transpose(
@@ -495,8 +536,9 @@
     tap_coef = lax.dynamic_slice_in_dim(tap_coef, band_index * lat_rows, lat_rows + 2 * REACH, 1)
     taps = jnp.transpose(tap_coef, (1, 0, 2, 3)).reshape(lat_rows + 2 * REACH, -1)
 
+    received, low, high, left, right = lax.optimization_barrier((received, low, high, left, right))
     blocks = received.reshape(lat_count, lon_count, local * q_count, LANES)
-    back = spectral(blocks, forward, inverse, table, weights, quad, group)
+    back = spectral(blocks, forward, inverse, tables, weights, quad, group)
     back, taps = lax.optimization_barrier((back, taps))
     returned = lax.all_to_all(
         back.reshape(devices, local * q_count, LANES), ("lat", "lon"), 0, 0, tiled=True

time: 120 us -> 93.4 us (0.78)
  Pallas kernels: 68.6 us -> 49.8 us
  waiting for transfers between devices: 22 us -> 16.7 us
    pallas_call x1, Pallas kernels: 26.8 us -> 11.6 us  [spectral(): pl.pallas_call(functools.partial(spectral_kernel, group=group, q_count=q_...]
    all_to_all x1, waiting for transfers between devices: 0.01 us -> 9.69 us  [shards(): lax.all_to_all(back.reshape(devices, local * q_count, LANES), ('lat', 'lo...]
    all_to_all x1, waiting for transfers between devices: 8.74 us -> 0.01 us  [shards(): received = lax.all_to_all(to_send, ('lat', 'lon'), 0, 0, tiled=True)]
    ppermute x2, waiting for transfers between devices: 13.3 us -> 5.15 us  [neighbours(): lax.ppermute(block_low, axis, forward)]
    pallas_call x1 -> x3, local copies, waits for them, and re-layouts: 0.59 us -> 3.41 us  [gradient(): pl.pallas_call(functools.partial(grad_kernel, group=group, q_count=q_coun...]
    ppermute x2, waiting for transfers between devices: 0.01 us -> 1.87 us  [neighbours(): lax.ppermute(block_high, axis, backward)]
    pallas_call x1, Pallas kernels: 14.9 us -> 13.2 us  [legendre(): pl.pallas_call(functools.partial(legendre_kernel, degrees=degrees, span=8...]
    unnamed x19 -> x23, local copies, waits for them, and re-layouts: 3.91 us -> 2.55 us
  transfers between devices with their start and end apart: 6 -> 6, of which waited for: 3 -> 3; matrix products, arithmetic and copies ran while one was open for 5% -> 6% of each run, Pallas kernels for 27% -> 31%
where the time goes in v1:
time: 93.4 us; the launch traced here: 92.7 us
  Pallas kernels  49.8 us (53%)
  starting transfers between devices  17.3 us (19%)
  waiting for transfers between devices  16.7 us (18%)
  local copies, waits for them, and re-layouts  6.42 us (7%)
  other arithmetic  2.2 us (2%)
    pallas_call x1, Pallas kernels, disco(): pl.pallas_call(disco_kernel, grid=(steps,), in_specs=[pl.BlockSpec(memory...  15.8 us
    pallas_call x1, Pallas kernels, legendre(): pl.pallas_call(functools.partial(legendre_kernel, degrees=degrees, span=8...  13.2 us
    pallas_call x1, Pallas kernels, spectral(): pl.pallas_call(functools.partial(spectral_kernel, group=group, q_count=q_...  11.6 us
    all_to_all x1, waiting for transfers between devices, shards(): lax.all_to_all(back.reshape(devices, local * q_count, LANES), ('lat', 'lo...  9.69 us
    all_to_all x1, starting transfers between devices, shards(): received = lax.all_to_all(to_send, ('lat', 'lon'), 0, 0, tiled=True)  6.65 us
    ppermute x2, starting transfers between devices, neighbours(): lax.ppermute(block_high, axis, backward)  6.63 us
    pallas_call x1, Pallas kernels, gradient(): pl.pallas_call(functools.partial(grad_kernel, group=group, q_count=q_coun...  5.17 us
    ppermute x2, waiting for transfers between devices, neighbours(): lax.ppermute(block_low, axis, forward)  5.15 us
  transfers between devices with their start and end apart: 6, of which 3 were waited for; matrix products, arithmetic and copies ran while one was open for 6% of the time, Pallas kernels for 31%

profile of v1, /device:TPU:0, one launch (start us, length us, event | category | flops | bytes accessed | tf_op | source)
XLA Modules:
  0.0 92.7 jit_solution(6796558299450768790)
XLA Ops:
  0.0 0.0 copy-start
  0.0 0.0 copy-start.10
  0.0 0.0 copy-start.9
  0.0 0.0 copy-start.6
  0.0 5.2 %gradient.1 = (bf16[64,32,256]{2,1,0:T(8,128)(2,1)}, bf16[32,128,128]{2,1,0:T(8,128)(2,1)}, bf16[2,32,256]{2,1,0:T(8,128)(2,1)}, bf16[2,32,256]{2,1,0:T(8,128)(2,1)}) custom-call(s32[1]{0:T(128)} %bitcast.flip_ref, bf16[64,32,256]{2,1,0:T(8,128)(2,1)} %pre_ref.1, bf16[64,32,256]{2,1,0:T(8,128)(2,1)} %cot_ref.1), custom_call_target="tpu_custom_call" | custom-call | tf_op jit(solution)/shard_map/gradient/pallas_call | solution.py:73
  5.2 0.0 copy-start.5
  5.2 0.8 copy.16
  6.0 0.5 collective-permute-start
  6.5 0.8 copy.17
  7.3 2.0 %collective-permute-start.1 = (bf16[2,32,256]{2,0,1:T(2,128)(2,1)S(1)}, bf16[2,32,256]{2,0,1:T(2,128)(2,1)S(1)}, u32[]{:S(2)}, u32[]{:S(2)}) collective-permute-start(bf16[2,32,256]{2,0,1:T(2,128)(2,1)S(1)} %copy.17), channel_id=1, source_target_pairs={{8,0},{16,8},{24,16},{0,24},{9,1},{17,9},{25,17},{1,25},{10,2},{18... | collective-permute-start | bytes 98312 | tf_op jit(solution)/shard_map/ppermute | solution.py:475
  9.4 6.7 %all-to-all-start = ((bf16[32,128,128]{2,1,0:T(8,128)(2,1)}), bf16[32,128,128]{2,1,0:T(8,128)(2,1)S(1)}, u32[]{:S(2)}, u32[]{:S(2)}) async-start(bf16[32,128,128]{2,1,0:T(8,128)(2,1)} %get-tuple-element.18), calls=%async_computation | async-start | bytes 2097152 | tf_op jit(solution)/shard_map/all_to_all | solution.py:504
  16.1 1.8 %copy.18 = bf16[64,32,256]{2,0,1:T(8,128)(2,1)S(1)} copy(bf16[64,32,256]{2,1,0:T(8,128)(2,1)} %get-tuple-element.21.grad_ref) | data formatting | bytes 2097152 | tf_op jit(solution)/shard_map/gradient/pallas_call | solution.py:73
  17.9 0.0 copy-done.9
  17.9 0.1 compare_convert_fusion
  18.0 0.0 copy-done.6
  18.0 0.1 fusion.21
  18.1 0.1 fusion.8
  18.2 0.0 copy-done
  18.2 0.2 constant_dynamic-slice_fusion
  18.4 0.5 sine_negate_fusion
  19.0 0.0 copy-done.10
  19.0 0.7 multiply_add_fusion.start_ref
  19.7 0.1 multiply_convert_fusion.forward_ref
  19.8 0.6 pad_maximum_fusion.2.norm_ref
  20.4 0.1 copy.25
  20.5 13.2 %legendre.1 = (bf16[128,128,128]{2,1,0:T(8,128)(2,1)}, bf16[128,128,128]{2,1,0:T(8,128)(2,1)}) custom-call(f32[2,128]{1,0:T(2,128)} %pad_maximum_fusion.2.norm_ref, f32[1,128]{1,0:T(1,128)} %constant.122.cos_ref, f32[128,128]{1,0:T(8,128)} %multiply_add_fusion.start_ref), custom_call_target="tpu_custom_call" | custom-call | flops 83886080 | bytes 8388608 | tf_op jit(solution)/shard_map/legendre/pallas_call | solution.py:139
  33.7 0.0 collective-permute-done
  33.7 0.0 collective-permute-done.1
  33.7 0.0 copy-start.7
  33.8 0.6 copy-done.7
  34.4 4.6 %collective-permute-start.3 = (bf16[2,68,256]{2,1,0:T(8,128)(2,1)S(1)}, bf16[2,68,256]{2,1,0:T(8,128)(2,1)S(1)}, u32[]{:S(2)}, u32[]{:S(2)}) collective-permute-start(bf16[2,68,256]{2,1,0:T(8,128)(2,1)S(1)} %maximum_bitcast_fusion.1), channel_id=1, source_target_pairs={{1,0},{2,1},{3,2},{4,3},{5,4},{6,5},{7,6},{0,7},{9,8},{10,9},{11,1... | collective-permute-start | bytes 208904 | tf_op jit(solution)/shard_map/ppermute | solution.py:475
  39.0 0.1 collective-permute-start.2
  39.1 1.9 %collective-permute-done.3.right_ref = bf16[2,68,256]{2,1,0:T(8,128)(2,1)S(1)} collective-permute-done((bf16[2,68,256]{2,1,0:T(8,128)(2,1)S(1)}, bf16[2,68,256]{2,1,0:T(8,128)(2,1)S(1)}, u32[]{:S(2)}, u32[]{:S(2)}) %collective-permute-start.3) | collective-permute-done | bytes 69664 | tf_op jit(solution)/shard_map/ppermute | solution.py:475
  41.0 5.1 %collective-permute-done.2.left_ref = bf16[2,68,256]{2,1,0:T(8,128)(2,1)S(1)} collective-permute-done((bf16[2,68,256]{2,1,0:T(8,128)(2,1)S(1)}, bf16[2,68,256]{2,1,0:T(8,128)(2,1)S(1)}, u32[]{:S(2)}, u32[]{:S(2)}) %collective-permute-start.2) | collective-permute-done | bytes 69664 | tf_op jit(solution)/shard_map/ppermute | solution.py:475
  46.1 0.0 copy-start.3
  46.1 0.0 all-to-all-done
  46.1 0.0 copy-done.5
  46.1 0.0 copy-start.8
  46.1 0.0 copy-start.1
  46.1 11.6 %spectral.1 = bf16[4,8,128,128]{3,2,1,0:T(8,128)(2,1)} custom-call(bf16[4,8,128,128]{3,2,1,0:T(8,128)(2,1)S(1)} %bitcast.13, bf16[256,256]{1,0:T(8,128)(2,1)S(1)} %multiply_convert_fusion.forward_ref, bf16[256,256]{1,0:T(8,128)(2,1)S(1)} %fusion.inverse_ref, f32[2,8,128]{2,1,0:T(8,128)S(1)} %bitcast.14, f32[1,128]{1,0:T(1,128)S(1)} %copy-done.5, ...), custom_call_target="tpu_custom_call" | custom-call | tf_op jit(solution)/shard_map/spectral/pallas_call | solution.py:322
  57.8 0.0 copy-done.3
  57.8 3.4 %all-to-all-start.1 = ((bf16[32,128,128]{2,1,0:T(8,128)(2,1)}), bf16[32,128,128]{2,1,0:T(8,128)(2,1)}, u32[]{:S(2)}, u32[]{:S(2)}) async-start(bf16[32,128,128]{2,1,0:T(8,128)(2,1)} %bitcast.7), calls=%async_computation.1 | async-start | bytes 2097152 | tf_op jit(solution)/shard_map/all_to_all | solution.py:543
  61.2 0.1 copy.22.tap_ref
  61.3 0.0 copy-done.8
  61.3 0.0 copy-done.1
  61.3 0.0 copy-start.2
  61.4 1.0 %copy-done.2 = bf16[3,256,256]{2,1,0:T(8,128)(2,1)S(1)} copy-done((bf16[3,256,256]{2,1,0:T(8,128)(2,1)S(1)}, bf16[3,256,256]{2,1,0:T(8,128)(2,1)}, u32[]{:S(2)}) %copy-start.2) | copy-done | bytes 393240
  62.3 0.0 copy-start.4
  62.3 0.9 copy-done.4
  63.2 15.8 %disco.1.disco_ref = f32[64,32,256]{2,1,0:T(8,128)S(1)} custom-call(f32[68,75]{1,0:T(8,128)S(1)} %copy.22.tap_ref, bf16[64,32,256]{2,1,0:T(8,128)(2,1)S(1)} %copy-done.1, bf16[2,32,256]{2,1,0:T(8,128)(2,1)S(1)} %copy.23.low_ref, bf16[2,32,256]{2,1,0:T(8,128)(2,1)S(1)} %copy.24.high_ref, bf16[2,68,256]{2,1,0:T(8,128)(2,1)S(1)} %copy-done.4, ...), custom_call_target="tpu_custom_call" | custom-call | flops 524288000 | bytes 4194304 | tf_op jit(solution)/shard_map/disco/pallas_call | solution.py:402
  79.1 9.7 %all-to-all-done.1.from_ref = bf16[32,128,128]{2,1,0:T(8,128)(2,1)} async-done(((bf16[32,128,128]{2,1,0:T(8,128)(2,1)}), bf16[32,128,128]{2,1,0:T(8,128)(2,1)}, u32[]{:S(2)}, u32[]{:S(2)}) %all-to-all-start.1) | async-done | bytes 1048608 | tf_op jit(solution)/shard_map/all_to_all | solution.py:543
  88.8 3.9 %combine.1 = bf16[64,32,256]{2,1,0:T(8,128)(2,1)} custom-call(s32[1]{0:T(128)} %bitcast.flip_ref, bf16[32,128,128]{2,1,0:T(8,128)(2,1)} %all-to-all-done.1.from_ref, f32[64,32,256]{2,1,0:T(8,128)S(1)} %disco.1.disco_ref), custom_call_target="tpu_custom_call" | custom-call | tf_op jit(solution)/shard_map/combine/pallas_call | solution.py:455
  (15 shorter events, 0.2 us)
Async XLA Ops:
  0.0 18.2 %copy-start = (f32[128,2,256]{2,1,0:T(2,128)S(1)}, f32[128,2,256]{2,1,0:T(2,128)}, u32[]{:S(2)}) copy-start(f32[128,2,256]{2,1,0:T(2,128)} %param.9) | copy-start | bytes 786436
  0.0 19.0 %copy-start.10 = (f32[128]{0:T(128)S(1)}, f32[128]{0:T(128)}, u32[]{:S(2)}) copy-start(f32[128]{0:T(128)} %constant.123) | copy-start | bytes 1540
  0.0 17.9 %copy-start.9 = (s32[256,5]{0,1:T(8,128)S(1)}, s32[256,5]{0,1:T(8,128)}, u32[]{:S(2)}) copy-start(s32[256,5]{0,1:T(8,128)} %param.12) | copy-start | bytes 15364
  0.0 18.0 %copy-start.6 = (f32[3,256,5,5]{1,0,3,2:T(4,128)S(1)}, f32[3,256,5,5]{1,0,3,2:T(4,128)}, u32[]{:S(2)}) copy-start(f32[3,256,5,5]{1,0,3,2:T(4,128)} %param.11) | copy-start | bytes 230404
  5.2 40.9 %copy-start.5 = (f32[1,128]{1,0:T(1,128)S(1)}, f32[1,128]{1,0:T(1,128)}, u32[]{:S(2)}) copy-start(f32[1,128]{1,0:T(1,128)} %constant.120.quad_ref) | copy-start | bytes 1540
  6.0 27.7 %collective-permute-start = (bf16[2,32,256]{2,0,1:T(2,128)(2,1)S(1)}, bf16[2,32,256]{2,0,1:T(2,128)(2,1)S(1)}, u32[]{:S(2)}, u32[]{:S(2)}) collective-permute-start(bf16[2,32,256]{2,0,1:T(2,128)(2,1)S(1)} %copy.16), channel_id=1, source_target_pairs={{0,8},{8,16},{16,24},{24,0},{1,9},{9,17},{17,25},{25,1},{2,10},{10... | collective-permute-start | bytes 98312 | tf_op jit(solution)/shard_map/ppermute | solution.py:475
  7.3 26.4 %collective-permute-start.1 = (bf16[2,32,256]{2,0,1:T(2,128)(2,1)S(1)}, bf16[2,32,256]{2,0,1:T(2,128)(2,1)S(1)}, u32[]{:S(2)}, u32[]{:S(2)}) collective-permute-start(bf16[2,32,256]{2,0,1:T(2,128)(2,1)S(1)} %copy.17), channel_id=1, source_target_pairs={{8,0},{16,8},{24,16},{0,24},{9,1},{17,9},{25,17},{1,25},{10,2},{18... | collective-permute-start | bytes 98312 | tf_op jit(solution)/shard_map/ppermute | solution.py:475
  9.4 36.7 %all-to-all-start = ((bf16[32,128,128]{2,1,0:T(8,128)(2,1)}), bf16[32,128,128]{2,1,0:T(8,128)(2,1)S(1)}, u32[]{:S(2)}, u32[]{:S(2)}) async-start(bf16[32,128,128]{2,1,0:T(8,128)(2,1)} %get-tuple-element.18), calls=%async_computation | async-start | bytes 2097152 | tf_op jit(solution)/shard_map/all_to_all | solution.py:504
  33.7 0.6 copy-start.7
  34.4 6.6 %collective-permute-start.3 = (bf16[2,68,256]{2,1,0:T(8,128)(2,1)S(1)}, bf16[2,68,256]{2,1,0:T(8,128)(2,1)S(1)}, u32[]{:S(2)}, u32[]{:S(2)}) collective-permute-start(bf16[2,68,256]{2,1,0:T(8,128)(2,1)S(1)} %maximum_bitcast_fusion.1), channel_id=1, source_target_pairs={{1,0},{2,1},{3,2},{4,3},{5,4},{6,5},{7,6},{0,7},{9,8},{10,9},{11,1... | collective-permute-start | bytes 208904 | tf_op jit(solution)/shard_map/ppermute | solution.py:475
  39.0 7.1 %collective-permute-start.2 = (bf16[2,68,256]{2,1,0:T(8,128)(2,1)S(1)}, bf16[2,68,256]{2,1,0:T(8,128)(2,1)S(1)}, u32[]{:S(2)}, u32[]{:S(2)}) collective-permute-start(bf16[2,68,256]{2,1,0:T(8,128)(2,1)S(1)} %maximum_bitcast_fusion), channel_id=1, source_target_pairs={{0,1},{1,2},{2,3},{3,4},{4,5},{5,6},{6,7},{7,0},{8,9},{9,10},{10,1... | collective-permute-start | bytes 208904 | tf_op jit(solution)/shard_map/ppermute | solution.py:475
  46.1 11.7 %copy-start.3 = (bf16[2,68,256]{2,1,0:T(8,128)(2,1)}, bf16[2,68,256]{2,1,0:T(8,128)(2,1)S(1)}, u32[]{:S(2)}) copy-start(bf16[2,68,256]{2,1,0:T(8,128)(2,1)S(1)} %collective-permute-done.2.left_ref) | copy-start | bytes 208900
  46.1 15.2 %copy-start.8 = (bf16[2,32,256]{2,0,1:T(2,128)(2,1)S(1)}, bf16[2,32,256]{2,0,1:T(2,128)(2,1)}, u32[]{:S(2)}) copy-start(bf16[2,32,256]{2,0,1:T(2,128)(2,1)} %copy-done.7) | copy-start | bytes 98308
  46.1 15.2 %copy-start.1 = (bf16[64,32,256]{2,1,0:T(8,128)(2,1)S(1)}, bf16[64,32,256]{2,1,0:T(8,128)(2,1)}, u32[]{:S(2)}) copy-start(bf16[64,32,256]{2,1,0:T(8,128)(2,1)} %get-tuple-element.21.grad_ref) | copy-start | bytes 3145732
  57.8 31.0 %all-to-all-start.1 = ((bf16[32,128,128]{2,1,0:T(8,128)(2,1)}), bf16[32,128,128]{2,1,0:T(8,128)(2,1)}, u32[]{:S(2)}, u32[]{:S(2)}) async-start(bf16[32,128,128]{2,1,0:T(8,128)(2,1)} %bitcast.7), calls=%async_computation.1 | async-start | bytes 2097152 | tf_op jit(solution)/shard_map/all_to_all | solution.py:543
  61.3 1.0 %copy-start.2 = (bf16[3,256,256]{2,1,0:T(8,128)(2,1)S(1)}, bf16[3,256,256]{2,1,0:T(8,128)(2,1)}, u32[]{:S(2)}) copy-start(bf16[3,256,256]{2,1,0:T(8,128)(2,1)} %mix_ref.1) | copy-start | bytes 1179652
  62.3 0.9 copy-start.4

commit v2 on v1

v2 whole, which is shorter than its diff:
```python
import functools
import math

import jax
import jax.numpy as jnp
import numpy as np
from jax import lax
from jax.experimental import pallas as pl
from jax.experimental.pallas import tpu as pltpu
from jax.sharding import PartitionSpec as P

REACH = 2
TAPS = 2 * REACH + 1
LANES = 128
PAD = 8
CHUNKS = 4
F32 = jnp.float32
BF16 = jnp.bfloat16
MIB = 1024 * 1024


def params(limit):
    return pltpu.CompilerParams(vmem_limit_bytes=limit)


def gelu_slope(pre_values):
    normal_cdf = 0.5 * (1.0 + lax.erf(pre_values * (1.0 / math.sqrt(2.0))))
    density = jnp.exp(-0.5 * pre_values * pre_values) * (1.0 / math.sqrt(2.0 * math.pi))
    return normal_cdf + pre_values * density


def grad_kernel(
    flip_ref, pre_hbm, cot_hbm, grad_hbm, send_hbm, first_ref, last_ref, west_ref, east_ref,
    pre_ref, cot_ref, grad_ref, send_ref, rows_scr, chan_scr, in_sems, out_sems, *, group, q_count,
):
    rows, cols, channels = pre_ref.shape
    part = rows // CHUNKS
    flip = flip_ref[0]

    def fetch(chunk):
        at = pl.ds(chunk * part, part)
        return [
            pltpu.make_async_copy(pre_hbm.at[at], pre_ref.at[at], in_sems.at[0, chunk]),
            pltpu.make_async_copy(cot_hbm.at[at], cot_ref.at[at], in_sems.at[1, chunk]),
        ]

    def keep(chunk):
        at = pl.ds(chunk * part, part)
        return pltpu.make_async_copy(grad_ref.at[at], grad_hbm.at[at], out_sems.at[0, chunk])

    def send(chunk):
        count = send_ref.shape[0] // CHUNKS
        at = pl.ds(chunk * count, count)
        return pltpu.make_async_copy(send_ref.at[at], send_hbm.at[at], out_sems.at[1, chunk])

    for chunk in range(CHUNKS):
        for copy in fetch(chunk):
            copy.start()
    for chunk in range(CHUNKS):
        for copy in fetch(chunk):
            copy.wait()
        for row in range(chunk * part, (chunk + 1) * part):
            grad = (cot_ref[row].astype(F32) * gelu_slope(pre_ref[row].astype(F32))).astype(BF16)
            grad_ref[row] = grad
            rows_scr[row] = grad.astype(F32)
        keep(chunk).start()
        for q_index in range(chunk * part // group, (chunk + 1) * part // group):
            q_out = jnp.where(flip == 1, q_count - 1 - q_index, q_index)
            slabs = []
            for r in range(group):
                slabs.append(rows_scr[q_index * group + jnp.where(flip == 1, group - 1 - r, r)])
            stacked = jnp.concatenate(slabs, axis=0)
            for tile in range(channels // LANES):
                turned = stacked[:, tile * LANES : (tile + 1) * LANES].T
                chan_scr[pl.ds(tile * LANES * q_count + q_out, LANES, stride=q_count), :] = turned
    dests, count = send_ref.shape[:2]
    for chunk in range(CHUNKS):
        for dest in range(chunk * dests // CHUNKS, (chunk + 1) * dests // CHUNKS):
            send_ref[dest] = chan_scr[dest * count : (dest + 1) * count, :].astype(BF16)
        send(chunk).start()
    for row in range(REACH):
        first_ref[row * cols : (row + 1) * cols, :] = grad_ref[row]
        last_ref[row * cols : (row + 1) * cols, :] = grad_ref[rows - REACH + row]
    for side in range(REACH):
        west_ref[side * rows : (side + 1) * rows, :] = rows_scr[:, side, :].astype(BF16)
        east_ref[side * rows : (side + 1) * rows, :] = rows_scr[:, cols - REACH + side, :].astype(BF16)
    for chunk in range(CHUNKS):
        keep(chunk).wait()
        send(chunk).wait()


def gradient(pre_act, cotangent, flip, devices, group):
    rows, cols, channels = pre_act.shape
    q_count = rows // group
    send = (devices, channels // devices * q_count, LANES)
    edges = [(REACH * cols, channels)] * 2 + [(REACH * rows, channels)] * 2
    anywhere = pl.BlockSpec(memory_space=pl.ANY)
    vmem = pl.BlockSpec(memory_space=pltpu.VMEM)
    return pl.pallas_call(
        functools.partial(grad_kernel, group=group, q_count=q_count),
        in_specs=[pl.BlockSpec(memory_space=pltpu.SMEM), anywhere, anywhere],
        out_specs=[anywhere, anywhere] + [vmem] * 4,
        out_shape=[jax.ShapeDtypeStruct(shape, BF16) for shape in (pre_act.shape, send, *edges)],
        scratch_shapes=[
            pltpu.VMEM(pre_act.shape, BF16),
            pltpu.VMEM(pre_act.shape, BF16),
            pltpu.VMEM(pre_act.shape, BF16),
            pltpu.VMEM(send, BF16),
            pltpu.VMEM(pre_act.shape, F32),
            pltpu.VMEM((channels * q_count, LANES), F32),
            pltpu.SemaphoreType.DMA((2, CHUNKS)),
            pltpu.SemaphoreType.DMA((2, CHUNKS)),
        ],
        compiler_params=params(60 * MIB),
        name="gradient",
    )(flip, pre_act, cotangent)


def legendre_kernel(norm_ref, cos_ref, start_ref, *refs, degrees, span):
    scr = refs[-1]
    pitch = degrees + PAD
    table_ref = refs[0]
    orders = table_ref.shape[0]
    groups = orders // 8
    first = pl.program_id(0) * orders
    cosine = jnp.broadcast_to(cos_ref[...], (8, LANES))
    sub = lax.broadcasted_iota(jnp.int32, (8, LANES), 0)
    order_vals = [(first + 8 * g + sub).astype(F32) for g in range(groups)]
    squares = [order * order for order in order_vals]
    zero = jnp.zeros((8, LANES), F32)

    def chunk(index, state):
        latest, earlier, coef_b, scale = (list(part) for part in state)
        factor = [jnp.exp(value) for value in scale]
        for step in range(span):
            degree = index * span + step
            deg_val = degree.astype(F32)
            norm = norm_ref[0, degree]
            inverse_norm = norm_ref[1, degree]
            for g in range(groups):
                gap = jnp.maximum(deg_val * deg_val - squares[g], 1.0)
                root = lax.rsqrt(gap)
                value = (root * norm) * (cosine * latest[g] - coef_b[g] * earlier[g])
                value = jnp.where(order_vals[g] == deg_val, 1.0, value)
                coef_b[g] = gap * root * inverse_norm
                earlier[g] = latest[g]
                latest[g] = value
                scr[pl.ds(g * 8 * pitch + degree, 8, stride=pitch), :] = value * factor[g]
        for g in range(groups):
            large = jnp.maximum(jnp.abs(latest[g]), jnp.abs(earlier[g])) > 2.0**20
            shrink = jnp.where(large, 2.0**-40, 1.0)
            latest[g] = latest[g] * shrink
            earlier[g] = earlier[g] * shrink
            scale[g] = scale[g] + jnp.where(large, 40.0 * math.log(2.0), 0.0)
        return (tuple(latest), tuple(earlier), tuple(coef_b), tuple(scale))

    starts = tuple(start_ref[8 * g : 8 * g + 8, :] for g in range(groups))
    zeros = (zero,) * groups
    lax.fori_loop(0, degrees // span, chunk, (zeros, zeros, zeros, starts))
    for order in range(orders):
        values = scr[order * pitch : order * pitch + degrees, :]
        table_ref[order] = values.astype(BF16)
        for turned_ref in refs[1:-1]:
            turned_ref[order] = values.T.astype(BF16)


def legendre(norms, cosine, start, both):
    orders, points = start.shape
    degrees = norms.shape[1]
    block = math.gcd(orders, 32)
    return pl.pallas_call(
        functools.partial(legendre_kernel, degrees=degrees, span=8),
        grid=(orders // block, points // LANES),
        in_specs=[
            pl.BlockSpec(memory_space=pltpu.SMEM),
            pl.BlockSpec((1, LANES), lambda i, j: (0, j)),
            pl.BlockSpec((block, LANES), lambda i, j: (i, j)),
        ],
        out_specs=[
            pl.BlockSpec((block, degrees, LANES), lambda i, j: (i, 0, j)),
            pl.BlockSpec((block, LANES, degrees), lambda i, j: (i, j, 0)),
        ][: 1 + both],
        out_shape=[
            jax.ShapeDtypeStruct((orders, degrees, points), BF16),
            jax.ShapeDtypeStruct((orders, points, degrees), BF16),
        ][: 1 + both],
        scratch_shapes=[pltpu.VMEM((block * (degrees + PAD), LANES), F32)],
        compiler_params=params(56 * MIB),
        cost_estimate=pl.CostEstimate(
            flops=40 * orders * degrees * points,
            bytes_accessed=4 * orders * degrees * points,
            transcendentals=0,
        ),
        name="legendre",
    )(norms, cosine, start)


def spectral_kernel(
    recv_hbm, forward_ref, inverse_ref, weight_ref, quad_ref, *refs, group, q_count, unroll, count
):
    tables = refs[:count]
    back_hbm, recv_ref, back_ref, grid_scr, even_scr, odd_scr, north_scr, south_scr = refs[count : count + 8]
    slots = refs[count + 8 : 2 * count + 8]
    recv_sem, table_sems, back_sems = refs[2 * count + 8 :]
    bands, sectors = recv_ref.shape[:2]
    local, lats, lons = grid_scr.shape
    slot_count, orders_here, degrees, half = slots[0].shape
    tiles = half // LANES
    modes = forward_ref.shape[0]
    orders = modes // 2
    blocks = orders // orders_here
    pitch = modes + PAD
    band_rows = group * q_count
    width = LANES // group
    lane_group = lax.broadcasted_iota(jnp.int32, (q_count, LANES), 1) // width

    def fetch(block, slot):
        at = pl.ds(block * orders_here, orders_here)
        return [
            pltpu.make_async_copy(table.at[at], ring.at[slot], table_sems.at[kind, slot])
            for kind, (table, ring) in enumerate(zip(tables, slots))
        ]

    def give(chan):
        at = pl.ds(chan * q_count, q_count)
        return pltpu.make_async_copy(back_ref.at[:, :, at], back_hbm.at[:, :, at], back_sems.at[chan])

    def place(band, r):
        if band < bands // 2:
            return band * band_rows + r * q_count
        return lats // 2 + (bands - 1 - band) * band_rows + r * q_count

    def rolled(value, places):
        shift = places * width % LANES
        return value if shift == 0 else pltpu.roll(value, shift, 1)

    receive = pltpu.make_async_copy(recv_hbm, recv_ref, recv_sem)
    receive.start()
    for block in range(slot_count):
        for copy in fetch(block, block):
            copy.start()
    receive.wait()

    for chan in range(local):
        at = chan * q_count
        for band in range(bands):
            for unit in range(sectors // group):
                pieces = [
                    recv_ref[band, unit * group + k, at : at + q_count, :].astype(F32) for k in range(group)
                ]
                for r in range(group):
                    value = rolled(pieces[0], -r)
                    for k in range(1, group):
                        value = jnp.where(lane_group == k, rolled(pieces[k], k - r), value)
                    row = place(band, r)
                    grid_scr[chan, row : row + q_count, unit * LANES : (unit + 1) * LANES] = value.astype(BF16)
        spectrum = lax.dot_general(
            forward_ref[...], grid_scr[chan], (((1,), (1,)), ((), ())), preferred_element_type=F32
        )
        for tile in range(tiles):
            north = spectrum[:, tile * LANES : (tile + 1) * LANES]
            south = spectrum[:, half + tile * LANES : half + (tile + 1) * LANES]
            even_scr[tile, chan * pitch : chan * pitch + modes, :] = north + south
            odd_scr[tile, chan * pitch : chan * pitch + modes, :] = north - south

    def lines(tile, mode):
        if local == 1:
            return (tile, pl.ds(mode, 1), slice(None))
        return (tile, pl.ds(mode, local, stride=pitch), slice(None))

    def load(scr, mode):
        parts = [scr[lines(tile, mode)] for tile in range(tiles)]
        return parts[0] if tiles == 1 else jnp.concatenate(parts, axis=1)

    degree_lane = lax.broadcasted_iota(jnp.int32, (local, degrees), 1)
    real_w = weight_ref[0]
    imag_w = weight_ref[1]
    quad = quad_ref[...]

    def one_order(slot, order, index):
        table = slots[0][slot, index]
        even = (degree_lane + order) % 2 == 0
        stacked = jnp.concatenate(
            [
                load(even_scr, order),
                load(even_scr, orders + order),
                load(odd_scr, order),
                load(odd_scr, orders + order),
            ],
            axis=0,
        ).astype(BF16)
        if count == 2:
            analysed = jnp.dot(stacked, slots[1][slot, index], preferred_element_type=F32)
        else:
            analysed = lax.dot_general(
                stacked, table, (((1,), (1,)), ((), ())), preferred_element_type=F32
            )
        real_a = jnp.where(even, analysed[0:local], analysed[2 * local : 3 * local])
        imag_a = jnp.where(even, analysed[local : 2 * local], analysed[3 * local : 4 * local])
        real_m = real_w * real_a + imag_w * imag_a
        imag_m = real_w * imag_a - imag_w * real_a
        mixed = jnp.concatenate(
            [
                jnp.where(even, real_m, 0.0),
                jnp.where(even, imag_m, 0.0),
                jnp.where(even, 0.0, real_m),
                jnp.where(even, 0.0, imag_m),
            ],
            axis=0,
        ).astype(BF16)
        synth = jnp.dot(mixed, table, preferred_element_type=F32) * quad
        for part in range(2):
            even_part = synth[part * local : (part + 1) * local]
            odd_part = synth[(2 + part) * local : (3 + part) * local]
            for tile in range(tiles):
                lanes = slice(tile * LANES, (tile + 1) * LANES)
                where = lines(tile, part * orders + order)
                north_scr[where] = even_part[:, lanes] + odd_part[:, lanes]
                south_scr[where] = even_part[:, lanes] - odd_part[:, lanes]

    def one_block(block, carry):
        slot = block % slot_count
        for copy in fetch(block, slot):
            copy.wait()

        def several(index, inner_carry):
            for inner in range(unroll):
                at = index * unroll + inner
                one_order(slot, block * orders_here + at, at)
            return inner_carry

        lax.fori_loop(0, orders_here // unroll, several, 0)

        @pl.when(block + slot_count < blocks)
        def _():
            for copy in fetch(block + slot_count, slot):
                copy.start()

        return carry

    lax.fori_loop(0, blocks, one_block, 0)

    for chan in range(local):
        rows = slice(chan * pitch, chan * pitch + modes)
        profile = jnp.concatenate(
            [scr[tile, rows, :].astype(BF16) for scr in (north_scr, south_scr) for tile in range(tiles)],
            axis=1,
        )
        field = lax.dot_general(
            profile, inverse_ref[...], (((0,), (0,)), ((), ())), preferred_element_type=F32
        )
        at = chan * q_count
        for band in range(bands):
            for unit in range(sectors // group):
                pieces = []
                for r in range(group):
                    row = place(band, r)
                    pieces.append(field[row : row + q_count, unit * LANES : (unit + 1) * LANES])
                for k in range(group):
                    value = rolled(pieces[0], -k)
                    for r in range(1, group):
                        value = jnp.where(lane_group == r, rolled(pieces[r], r - k), value)
                    back_ref[band, unit * group + k, at : at + q_count, :] = value.astype(BF16)
        give(chan).start()
    for chan in range(local):
        give(chan).wait()


def spectral(received, forward, inverse, tables, weights, quad, group):
    bands, sectors, rows, _ = received.shape
    local = weights.shape[1]
    q_count = rows // local
    orders, degrees, half = tables[0].shape
    lons = forward.shape[1]
    count = len(tables)
    block = max(1, min(orders, 2**19 // (degrees * half)))
    ring = min(orders // block, 4)
    tiles = half // LANES
    anywhere = pl.BlockSpec(memory_space=pl.ANY)
    vmem = pl.BlockSpec(memory_space=pltpu.VMEM)
    lines = pltpu.VMEM((tiles, local * (forward.shape[0] + PAD), LANES), F32)
    return pl.pallas_call(
        functools.partial(
            spectral_kernel, group=group, q_count=q_count, unroll=math.gcd(block, 16), count=count
        ),
        in_specs=[anywhere] + [vmem] * 4 + [anywhere] * count,
        out_specs=anywhere,
        out_shape=jax.ShapeDtypeStruct(received.shape, BF16),
        scratch_shapes=[
            pltpu.VMEM(received.shape, BF16),
            pltpu.VMEM(received.shape, BF16),
            pltpu.VMEM((local, 2 * half, lons), BF16),
            lines,
            lines,
            lines,
            lines,
        ]
        + [pltpu.VMEM((ring, block) + table.shape[1:], BF16) for table in tables]
        + [
            pltpu.SemaphoreType.DMA,
            pltpu.SemaphoreType.DMA((count, ring)),
            pltpu.SemaphoreType.DMA((local,)),
        ],
        compiler_params=params(50 * MIB),
        name="spectral",
    )(received, forward, inverse, weights, quad, *tables)


def disco_kernel(
    tap_ref, grad_ref, low_ref, high_ref, left_ref, right_ref, corner_ref, mix_ref, out_ref, padded, taps_scr
):
    step = pl.program_id(0)
    rows, cols, channels = grad_ref.shape
    rows_here = out_ref.shape[0]
    kernels = mix_ref.shape[0]
    halves = channels // LANES
    origin = 8

    @pl.when(step == 0)
    def _():
        for half in range(halves):
            lanes = slice(half * LANES, (half + 1) * LANES)
            padded[half, REACH : REACH + rows, origin : origin + cols, :] = grad_ref[:, :, lanes].astype(F32)
            corners = corner_ref[:, lanes].astype(F32)
            for edge, (source, base) in enumerate(((low_ref, 0), (high_ref, REACH + rows))):
                values = source[:, lanes].astype(F32)
                for row in range(REACH):
                    padded[half, base + row, origin : origin + cols, :] = values[row * cols : (row + 1) * cols]
                    for side in range(REACH):
                        for end, column in enumerate((origin - REACH, origin + cols)):
                            at = ((edge * 2 + end) * REACH + side) * REACH + row
                            column = column + side
                            padded[half, base + row, column : column + 1, :] = corners[at : at + 1]
            for source, column in ((left_ref, origin - REACH), (right_ref, origin + cols)):
                values = source[:, lanes].astype(F32)
                for side in range(REACH):
                    padded[half, REACH : REACH + rows, column + side, :] = values[side * rows : (side + 1) * rows]

    def one_row(row, carry):
        for half in range(halves):
            sums = [jnp.zeros((cols, LANES), F32) for _ in range(kernels)]
            for lat_tap in range(TAPS):
                source = step * rows_here + row + 2 * REACH - lat_tap
                for lon_tap in range(TAPS):
                    start = origin + REACH - lon_tap
                    slab = padded[half, source, start : start + cols, :]
                    for kernel in range(kernels):
                        tap = tap_ref[source, (kernel * TAPS + lat_tap) * TAPS + lon_tap]
                        sums[kernel] = sums[kernel] + tap * slab
            for kernel in range(kernels):
                taps_scr[kernel, row, :, half * LANES : (half + 1) * LANES] = sums[kernel].astype(BF16)
        return carry

    lax.fori_loop(0, rows_here, one_row, 0)
    total = None
    for kernel in range(kernels):
        flat = taps_scr[kernel].reshape(rows_here * cols, channels)
        term = lax.dot_general(
            flat, mix_ref[kernel], (((1,), (1,)), ((), ())), preferred_element_type=F32
        )
        total = term if total is None else total + term
    out_ref[...] = total.reshape(rows_here, cols, channels)


def disco(taps, grad, low, high, left, right, corners, mix):
    rows, cols, channels = grad.shape
    kernels = mix.shape[0]
    steps = 4

    def whole(shape):
        return pl.BlockSpec(shape, lambda i: (0,) * len(shape))

    return pl.pallas_call(
        disco_kernel,
        grid=(steps,),
        in_specs=[pl.BlockSpec(memory_space=pltpu.SMEM)]
        + [whole(value.shape) for value in (grad, low, high, left, right, corners, mix)],
        out_specs=pl.BlockSpec((rows // steps, cols, channels), lambda i: (i, 0, 0)),
        out_shape=jax.ShapeDtypeStruct(grad.shape, F32),
        scratch_shapes=[
            pltpu.VMEM((channels // LANES, rows + 2 * REACH, cols + 16, LANES), F32),
            pltpu.VMEM((kernels, rows // steps, cols, channels), BF16),
        ],
        compiler_params=params(14 * MIB),
        cost_estimate=pl.CostEstimate(
            flops=1000 * rows * cols * channels, bytes_accessed=8 * rows * cols * channels, transcendentals=0
        ),
        name="disco",
    )(taps, grad, low, high, left, right, corners, mix)


def combine_kernel(
    flip_ref, back_hbm, disco_ref, out_hbm, back_ref, chan_scr, out_ref, in_sems, out_sems, *, group, q_count
):
    rows, cols, channels = disco_ref.shape
    sources, count = back_ref.shape[:2]
    part = rows // CHUNKS
    flip = flip_ref[0]

    def fetch(chunk):
        at = pl.ds(chunk * (sources // CHUNKS), sources // CHUNKS)
        return pltpu.make_async_copy(back_hbm.at[at], back_ref.at[at], in_sems.at[chunk])

    def give(chunk):
        at = pl.ds(chunk * part, part)
        return pltpu.make_async_copy(out_ref.at[at], out_hbm.at[at], out_sems.at[chunk])

    for chunk in range(CHUNKS):
        fetch(chunk).start()
    for chunk in range(CHUNKS):
        fetch(chunk).wait()
        for source in range(chunk * sources // CHUNKS, (chunk + 1) * sources // CHUNKS):
            chan_scr[source * count : (source + 1) * count, :] = back_ref[source].astype(F32)
    for chunk in range(CHUNKS):
        for q_index in range(chunk * part // group, (chunk + 1) * part // group):
            q_from = jnp.where(flip == 1, q_count - 1 - q_index, q_index)
            turned = jnp.concatenate(
                [
                    chan_scr[pl.ds(tile * LANES * q_count + q_from, LANES, stride=q_count), :].T
                    for tile in range(channels // LANES)
                ],
                axis=1,
            )
            for r in range(group):
                row = q_index * group + jnp.where(flip == 1, group - 1 - r, r)
                out_ref[row] = (disco_ref[row] + turned[r * cols : (r + 1) * cols]).astype(BF16)
        give(chunk).start()
    for chunk in range(CHUNKS):
        give(chunk).wait()


def combine(back, local_part, flip, group):
    rows, cols, channels = local_part.shape
    q_count = rows // group
    anywhere = pl.BlockSpec(memory_space=pl.ANY)
    return pl.pallas_call(
        functools.partial(combine_kernel, group=group, q_count=q_count),
        in_specs=[
            pl.BlockSpec(memory_space=pltpu.SMEM),
            anywhere,
            pl.BlockSpec(memory_space=pltpu.VMEM),
        ],
        out_specs=anywhere,
        out_shape=jax.ShapeDtypeStruct(local_part.shape, BF16),
        scratch_shapes=[
            pltpu.VMEM(back.shape, BF16),
            pltpu.VMEM((channels * q_count, LANES), F32),
            pltpu.VMEM(local_part.shape, BF16),
            pltpu.SemaphoreType.DMA((CHUNKS,)),
            pltpu.SemaphoreType.DMA((CHUNKS,)),
        ],
        compiler_params=params(12 * MIB),
        name="combine",
    )(flip, back, local_part)


def shifted(block, lat_step, lon_step):
    lat_count = lax.axis_size("lat")
    lon_count = lax.axis_size("lon")
    pairs = [
        (
            lat * lon_count + lon,
            (lat + lat_step) % lat_count * lon_count + (lon + lon_step) % lon_count,
        )
        for lat in range(lat_count)
        for lon in range(lon_count)
    ]
    return lax.ppermute(block, ("lat", "lon"), pairs)


def halos(first_rows, last_rows, west, east):
    channels = west.shape[-1]

    def corner(side, start):
        block = side.reshape(REACH, -1, channels)[:, start:][:, :REACH]
        return block.reshape(REACH * REACH, channels)

    low = shifted(last_rows, 1, 0)
    high = shifted(first_rows, -1, 0)
    left = shifted(east, 0, 1)
    right = shifted(west, 0, -1)
    corners = [
        shifted(corner(east, -REACH), 1, 1),
        shifted(corner(west, -REACH), 1, -1),
        shifted(corner(east, 0), -1, 1),
        shifted(corner(west, 0), -1, -1),
    ]
    return (low, high, left, right, jnp.concatenate(corners, axis=0))


def fourier_tables(order_count, points):
    order_list = jnp.arange(order_count, dtype=jnp.int32)[:, None]
    grid_pos = jnp.arange(points, dtype=jnp.int32)[None, :]
    angles = 2.0 * math.pi / points * (grid_pos * order_list % points).astype(F32)
    factor = jnp.where(order_list == 0, 1.0, 2.0).astype(F32)
    inverse = jnp.concatenate([jnp.cos(angles), -jnp.sin(angles)], axis=0)
    forward = jnp.concatenate([factor, factor], axis=0) * inverse
    return (forward.astype(BF16), inverse.astype(BF16))


def shards(pre_act, cotangent, spec_weight, disco_weight, disco_filter, support):
    lat_rows, lon_cols, channels = pre_act.shape
    lat_count = lax.axis_size("lat")
    lon_count = lax.axis_size("lon")
    devices = lat_count * lon_count
    band_index = lax.axis_index("lat")
    device_id = band_index * lon_count + lax.axis_index("lon")
    total_lat = lat_rows * lat_count
    total_lon = lon_cols * lon_count
    mode_count = spec_weight.shape[0]
    local = channels // devices
    group = LANES // lon_cols
    q_count = lat_rows // group
    flip = (2 * band_index >= lat_count).astype(jnp.int32).reshape(1)

    grad_pre, to_send, *edges = gradient(pre_act, cotangent, flip, devices, group)
    received = lax.all_to_all(to_send, ("lat", "lon"), 0, 0, tiled=True)

    lane = np.arange(total_lat // 2)
    lats = lane // lat_rows * lat_rows + lane % q_count * group + lane % lat_rows // q_count
    colatitude = math.pi / total_lat * (jnp.asarray(lats, F32) + 0.5)[None, :]
    order_vals = jnp.arange(mode_count, dtype=F32)[:, None]
    start = (
        0.5 * jnp.log((2.0 * order_vals + 1.0) / (4.0 * math.pi))
        + 0.5
        * (
            lax.lgamma(2.0 * order_vals + 1.0)
            - order_vals * math.log(4.0)
            - 2.0 * lax.lgamma(order_vals + 1.0)
        )
        + order_vals * jnp.log(jnp.sin(colatitude))
    )
    degree_norm = jnp.sqrt(jnp.maximum(4.0 * jnp.square(jnp.arange(mode_count, dtype=F32)) - 1.0, 1.0))
    norms = jnp.stack([degree_norm, 1.0 / degree_norm])
    both = mode_count * mode_count * total_lat < 2**25
    tables = legendre(norms, jnp.cos(colatitude), start, both)
    forward, inverse = fourier_tables(mode_count, total_lon)
    quad = 2.0 * math.pi / total_lon * (math.pi / total_lat) * jnp.sin(colatitude)
    weights = jnp.transpose(
        lax.dynamic_slice_in_dim(spec_weight, device_id * local, local, 2), (1, 2, 0)
    )
    offsets = jnp.arange(TAPS, dtype=jnp.int32) - REACH
    allowed = (jnp.abs(offsets)[None, None, :] <= support[:, :, None]).astype(F32)
    tap_coef = jnp.pad(disco_filter * allowed[None], ((0, 0), (REACH, REACH), (0, 0), (0, 0)))
    tap_coef = lax.dynamic_slice_in_dim(tap_coef, band_index * lat_rows, lat_rows + 2 * REACH, 1)
    taps = jnp.transpose(tap_coef, (1, 0, 2, 3)).reshape(lat_rows + 2 * REACH, -1)

    received, rim = lax.optimization_barrier((received, halos(*edges)))
    blocks = received.reshape(lat_count, lon_count, local * q_count, LANES)
    back = spectral(blocks, forward, inverse, tables, weights, quad, group)
    back, taps = lax.optimization_barrier((back, taps))
    returned = lax.all_to_all(
        back.reshape(devices, local * q_count, LANES), ("lat", "lon"), 0, 0, tiled=True
    )
    local_part = disco(taps, grad_pre, *rim, disco_weight)
    return combine(returned, local_part, flip, group)


def solution(mesh):
    return jax.shard_map(
        shards,
        mesh=mesh,
        in_specs=(P("lat", "lon", None), P("lat", "lon", None), P(), P(), P(), P()),
        out_specs=P("lat", "lon", None),
        check_vma=False,
    )
```

time: 93.4 us -> 91.2 us (0.976)
  Pallas kernels: 49.8 us -> 39.4 us
  starting transfers between devices: 17.3 us -> 24.9 us
  waiting for transfers between devices: 16.7 us -> 18 us
    ppermute x4 -> x8, starting transfers between devices: 7.23 us -> 19.2 us  [shifted(): return lax.ppermute(block, ('lat', 'lon'), pairs)]
    all_to_all x1, waiting for transfers between devices: 0.01 us -> 8.38 us  [shards(): received = lax.all_to_all(to_send, ('lat', 'lon'), 0, 0, tiled=True)]
    ppermute x4 -> x8, waiting for transfers between devices: 7.02 us -> 1.82 us  [shifted(): return lax.ppermute(block, ('lat', 'lon'), pairs)]
    pallas_call x1, Pallas kernels: 13.2 us -> 8.32 us  [legendre(): pl.pallas_call(functools.partial(legendre_kernel, degrees=degrees, span=8...]
    all_to_all x1, starting transfers between devices: 6.65 us -> 2.64 us  [shards(): received = lax.all_to_all(to_send, ('lat', 'lon'), 0, 0, tiled=True)]
    pallas_call x1, Pallas kernels: 11.6 us -> 7.69 us  [spectral(): pl.pallas_call(functools.partial(spectral_kernel, group=group, q_count=q_...]
    pallas_call x3 -> x0, local copies, waits for them, and re-layouts: 3.41 us -> none  [gradient(): pl.pallas_call(functools.partial(grad_kernel, group=group, q_count=q_coun...]
    all_to_all x1, waiting for transfers between devices: 9.69 us -> 7.84 us  [shards(): lax.all_to_all(back.reshape(devices, local * q_count, LANES), ('lat', 'lo...]
  transfers between devices with their start and end apart: 6 -> 10, of which waited for: 3 -> 3; matrix products, arithmetic and copies ran while one was open for 6% -> 5% of each run, Pallas kernels for 31% -> 27%
where the time goes in v2:
time: 91.2 us; the launch traced here: 90.6 us
  Pallas kernels  39.4 us (43%)
  starting transfers between devices  24.9 us (27%)
  waiting for transfers between devices  18 us (20%)
  local copies, waits for them, and re-layouts  5.86 us (6%)
  other arithmetic  2.15 us (2%)
    ppermute x8, starting transfers between devices, shifted(): return lax.ppermute(block, ('lat', 'lon'), pairs)  19.2 us
    pallas_call x1, Pallas kernels, disco(): pl.pallas_call(disco_kernel, grid=(steps,), in_specs=[pl.BlockSpec(memory...  15.8 us
    all_to_all x1, waiting for transfers between devices, shards(): received = lax.all_to_all(to_send, ('lat', 'lon'), 0, 0, tiled=True)  8.38 us
    pallas_call x1, Pallas kernels, legendre(): pl.pallas_call(functools.partial(legendre_kernel, degrees=degrees, span=8...  8.32 us
    all_to_all x1, waiting for transfers between devices, shards(): lax.all_to_all(back.reshape(devices, local * q_count, LANES), ('lat', 'lo...  7.84 us
    pallas_call x1, Pallas kernels, spectral(): pl.pallas_call(functools.partial(spectral_kernel, group=group, q_count=q_...  7.69 us
    pallas_call x1, Pallas kernels, gradient(): pl.pallas_call(functools.partial(grad_kernel, group=group, q_count=q_coun...  5.25 us
    unnamed x29, local copies, waits for them, and re-layouts  3.92 us
  transfers between devices with their start and end apart: 10, of which 3 were waited for; matrix products, arithmetic and copies ran while one was open for 5% of the time, Pallas kernels for 27%

profile of v2, /device:TPU:0, one launch (start us, length us, event | category | flops | bytes accessed | tf_op | source)
XLA Modules:
  0.0 90.6 jit_solution(3236374809538169343)
XLA Ops:
  0.0 0.0 copy-start
  0.0 0.0 copy-start.10
  0.0 0.0 copy-start.7
  0.0 0.0 copy-start.9
  0.0 0.0 copy-start.8
  0.0 5.3 %gradient.1 = (bf16[64,32,256]{2,1,0:T(8,128)(2,1)}, bf16[32,128,128]{2,1,0:T(8,128)(2,1)}, bf16[64,256]{1,0:T(8,128)(2,1)}, bf16[64,256]{1,0:T(8,128)(2,1)}, bf...) custom-call(s32[1]{0:T(128)} %bitcast.flip_ref, bf16[64,32,256]{2,1,0:T(8,128)(2,1)} %pre_hbm.1, bf16[64,32,256]{2,1,0:T(8,128)(2,1)} %cot_hbm.1), custom_call_target="tpu_custom_call" | custom-call | tf_op jit(solution)/shard_map/gradient/pallas_call | solution.py:99
  5.3 0.0 copy-start.11
  5.3 0.0 copy-start.13
  5.3 0.0 copy-start.12
  5.3 3.0 %collective-permute-start.2 = (bf16[128,256]{1,0:T(8,128)(2,1)}, bf16[128,256]{1,0:T(8,128)(2,1)S(1)}, u32[]{:S(2)}, u32[]{:S(2)}) collective-permute-start(bf16[128,256]{1,0:T(8,128)(2,1)} %get-tuple-element.24), channel_id=1, source_target_pairs={{0,1},{1,2},{2,3},{3,4},{4,5},{5,6},{6,7},{7,0},{8,9},{9,10},{10,1... | collective-permute-start | bytes 196616 | tf_op jit(solution)/shard_map/ppermute | solution.py:568
  8.4 0.7 fusion.24
  9.1 0.7 collective-permute-start.4
  9.8 0.7 fusion.25
  10.6 4.8 %collective-permute-start.5 = (bf16[4,256]{1,0:T(4,128)(2,1)S(1)}, bf16[4,256]{1,0:T(4,128)(2,1)S(1)}, u32[]{:S(2)}, u32[]{:S(2)}) collective-permute-start(bf16[4,256]{1,0:T(4,128)(2,1)S(1)} %reshape.342), channel_id=1, source_target_pairs={{0,15},{1,8},{2,9},{3,10},{4,11},{5,12},{6,13},{7,14},{8,23},{9,16... | collective-permute-start | bytes 6152 | tf_op jit(solution)/shard_map/ppermute | solution.py:568
  15.4 0.0 collective-permute-start.6
  15.4 4.3 %collective-permute-start.7 = (bf16[4,256]{1,0:T(4,128)(2,1)S(1)}, bf16[4,256]{1,0:T(4,128)(2,1)S(1)}, u32[]{:S(2)}, u32[]{:S(2)}) collective-permute-start(bf16[4,256]{1,0:T(4,128)(2,1)S(1)} %reshape.344), channel_id=1, source_target_pairs={{0,31},{1,24},{2,25},{3,26},{4,27},{5,28},{6,29},{7,30},{8,7},{9,0... | collective-permute-start | bytes 6152 | tf_op jit(solution)/shard_map/ppermute | solution.py:568
  19.7 2.6 %all-to-all-start = ((bf16[32,128,128]{2,1,0:T(8,128)(2,1)}), bf16[32,128,128]{2,1,0:T(8,128)(2,1)S(1)}, u32[]{:S(2)}, u32[]{:S(2)}) async-start(bf16[32,128,128]{2,1,0:T(8,128)(2,1)} %get-tuple-element.21), calls=%async_computation | async-start | bytes 2097152 | tf_op jit(solution)/shard_map/all_to_all | solution.py:617
  22.4 0.1 fusion.21
  22.5 0.6 pad_maximum_fusion.3.norm_ref
  23.1 0.0 copy-done.9
  23.1 0.1 compare_convert_fusion
  23.2 0.0 copy-done.8
  23.2 0.1 fusion.8
  23.3 0.0 copy-done
  23.3 0.2 constant_dynamic-slice_fusion
  23.6 0.5 sine_negate_fusion
  24.1 0.0 copy-done.10
  24.1 0.7 multiply_add_fusion.start_ref
  24.8 0.1 multiply_convert_fusion.forward_ref
  24.9 8.3 %legendre.1 = (bf16[128,128,128]{2,1,0:T(8,128)(2,1)}, bf16[128,128,128]{2,1,0:T(8,128)(2,1)}) custom-call(f32[2,128]{1,0:T(2,128)} %pad_maximum_fusion.3.norm_ref, f32[1,128]{1,0:T(1,128)} %constant.122.cos_ref, f32[128,128]{1,0:T(8,128)} %multiply_add_fusion.start_ref), custom_call_target="tpu_custom_call" | custom-call | flops 83886080 | bytes 8388608 | tf_op jit(solution)/shard_map/legendre/pallas_call | solution.py:171
  33.3 0.1 copy.13
  33.4 0.0 collective-permute-done.4
  33.4 0.0 copy-done.11
  33.4 4.6 %collective-permute-start.3 = (bf16[128,256]{1,0:T(8,128)(2,1)S(1)}, bf16[128,256]{1,0:T(8,128)(2,1)S(1)}, u32[]{:S(2)}, u32[]{:S(2)}) collective-permute-start(bf16[128,256]{1,0:T(8,128)(2,1)S(1)} %copy-done.11), channel_id=1, source_target_pairs={{0,7},{1,0},{2,1},{3,2},{4,3},{5,4},{6,5},{7,6},{8,15},{9,8},{10,9... | collective-permute-start | bytes 196616 | tf_op jit(solution)/shard_map/ppermute | solution.py:568
  38.0 0.0 collective-permute-done.5
  38.0 0.0 copy-done.13
  38.0 0.0 collective-permute-start
  38.0 0.0 collective-permute-done.6
  38.0 0.0 copy-done.12
  38.0 1.7 %collective-permute-start.1 = (bf16[64,256]{1,0:T(8,128)(2,1)S(1)}, bf16[64,256]{1,0:T(8,128)(2,1)S(1)}, u32[]{:S(2)}, u32[]{:S(2)}) collective-permute-start(bf16[64,256]{1,0:T(8,128)(2,1)S(1)} %copy-done.12), channel_id=1, source_target_pairs={{0,24},{1,25},{2,26},{3,27},{4,28},{5,29},{6,30},{7,31},{8,0},{9,1... | collective-permute-start | bytes 98312 | tf_op jit(solution)/shard_map/ppermute | solution.py:568
  39.7 0.0 collective-permute-done.7
  39.8 1.8 %collective-permute-done.low_ref = bf16[64,256]{1,0:T(8,128)(2,1)S(1)} collective-permute-done((bf16[64,256]{1,0:T(8,128)(2,1)S(1)}, bf16[64,256]{1,0:T(8,128)(2,1)S(1)}, u32[]{:S(2)}, u32[]{:S(2)}) %collective-permute-start) | collective-permute-done | bytes 32800 | tf_op jit(solution)/shard_map/ppermute | solution.py:568
  41.6 0.0 collective-permute-done.1.high_ref
  41.6 0.0 copy-start.5
  41.6 0.0 collective-permute-done.2.left_ref
  41.6 0.0 collective-permute-done.3.right_ref
  41.6 0.0 copy-start.3
  41.6 8.4 %all-to-all-done = bf16[32,128,128]{2,1,0:T(8,128)(2,1)S(1)} async-done(((bf16[32,128,128]{2,1,0:T(8,128)(2,1)}), bf16[32,128,128]{2,1,0:T(8,128)(2,1)S(1)}, u32[]{:S(2)}, u32[]{:S(2)}) %all-to-all-start) | async-done | bytes 1048608 | tf_op jit(solution)/shard_map/all_to_all | solution.py:617
  50.0 0.0 copy-done.7
  50.0 7.7 %spectral.1 = bf16[4,8,128,128]{3,2,1,0:T(8,128)(2,1)} custom-call(bf16[4,8,128,128]{3,2,1,0:T(8,128)(2,1)S(1)} %bitcast.11, bf16[256,256]{1,0:T(8,128)(2,1)S(1)} %multiply_convert_fusion.forward_ref, bf16[256,256]{1,0:T(8,128)(2,1)S(1)} %fusion.inverse_ref, f32[2,8,128]{2,1,0:T(8,128)S(1)} %bitcast.12, f32[1,128]{1,0:T(1,128)S(1)} %copy-done.7, ...), custom_call_target="tpu_custom_call" | custom-call | tf_op jit(solution)/shard_map/spectral/pallas_call | solution.py:382
  57.7 0.0 copy-done.5
  57.7 0.0 copy-done.3
  57.7 3.0 %all-to-all-start.1 = ((bf16[32,128,128]{2,1,0:T(8,128)(2,1)}), bf16[32,128,128]{2,1,0:T(8,128)(2,1)S(1)}, u32[]{:S(2)}, u32[]{:S(2)}) async-start(bf16[32,128,128]{2,1,0:T(8,128)(2,1)} %bitcast.7), calls=%async_computation.1 | async-start | bytes 2097152 | tf_op jit(solution)/shard_map/all_to_all | solution.py:652
  60.7 0.1 copy.12.tap_ref
  60.8 1.2 %copy-done.1 = bf16[64,32,256]{2,1,0:T(8,128)(2,1)S(1)} copy-done((bf16[64,32,256]{2,1,0:T(8,128)(2,1)S(1)}, bf16[64,32,256]{2,1,0:T(8,128)(2,1)}, u32[]{:S(2)}) %copy-start.1) | copy-done | bytes 1048600
  62.1 0.0 copy-start.2
  62.1 1.0 %copy-done.2 = bf16[3,256,256]{2,1,0:T(8,128)(2,1)S(1)} copy-done((bf16[3,256,256]{2,1,0:T(8,128)(2,1)S(1)}, bf16[3,256,256]{2,1,0:T(8,128)(2,1)}, u32[]{:S(2)}) %copy-start.2) | copy-done | bytes 393240
  63.1 0.0 copy-start.4
  63.1 0.8 copy-done.4
  63.9 0.0 copy-start.6
  63.9 0.8 copy-done.6
  64.7 15.8 %disco.1.disco_ref = f32[64,32,256]{2,1,0:T(8,128)S(1)} custom-call(f32[68,75]{1,0:T(8,128)S(1)} %copy.12.tap_ref, bf16[64,32,256]{2,1,0:T(8,128)(2,1)S(1)} %copy-done.1, bf16[64,256]{1,0:T(8,128)(2,1)S(1)} %collective-permute-done.low_ref, bf16[64,256]{1,0:T(8,128)(2,1)S(1)} %copy-done.6, bf16[128,256]{1,0:T(8,128)(2,1)S(1)} %collective-permute-done.2.left_ref, ...), custom_call_target="tpu_custom_call" | custom-call | flops 524288000 | bytes 4194304 | tf_op jit(solution)/shard_map/disco/pallas_call | solution.py:473
  80.5 7.8 %all-to-all-done.1.back_hbm = bf16[32,128,128]{2,1,0:T(8,128)(2,1)S(1)} async-done(((bf16[32,128,128]{2,1,0:T(8,128)(2,1)}), bf16[32,128,128]{2,1,0:T(8,128)(2,1)S(1)}, u32[]{:S(2)}, u32[]{:S(2)}) %all-to-all-start.1) | async-done | bytes 1048608 | tf_op jit(solution)/shard_map/all_to_all | solution.py:652
  88.3 2.3 %combine.1 = bf16[64,32,256]{2,1,0:T(8,128)(2,1)} custom-call(s32[1]{0:T(128)} %bitcast.flip_ref, bf16[32,128,128]{2,1,0:T(8,128)(2,1)S(1)} %all-to-all-done.1.back_hbm, f32[64,32,256]{2,1,0:T(8,128)S(1)} %disco.1.disco_ref), custom_call_target="tpu_custom_call" | custom-call | tf_op jit(solution)/shard_map/combine/pallas_call | solution.py:536
  (14 shorter events, 0.2 us)
Async XLA Ops:
  0.0 23.3 %copy-start = (f32[128,2,256]{2,1,0:T(2,128)S(1)}, f32[128,2,256]{2,1,0:T(2,128)}, u32[]{:S(2)}) copy-start(f32[128,2,256]{2,1,0:T(2,128)} %param.9) | copy-start | bytes 786436
  0.0 24.1 %copy-start.10 = (f32[128]{0:T(128)S(1)}, f32[128]{0:T(128)}, u32[]{:S(2)}) copy-start(f32[128]{0:T(128)} %constant.123) | copy-start | bytes 1540
  0.0 50.0 %copy-start.7 = (f32[1,128]{1,0:T(1,128)S(1)}, f32[1,128]{1,0:T(1,128)}, u32[]{:S(2)}) copy-start(f32[1,128]{1,0:T(1,128)} %constant.120.quad_ref) | copy-start | bytes 1540
  0.0 23.1 %copy-start.9 = (s32[256,5]{0,1:T(8,128)S(1)}, s32[256,5]{0,1:T(8,128)}, u32[]{:S(2)}) copy-start(s32[256,5]{0,1:T(8,128)} %param.12) | copy-start | bytes 15364
  0.0 23.2 %copy-start.8 = (f32[3,256,5,5]{1,0,3,2:T(4,128)S(1)}, f32[3,256,5,5]{1,0,3,2:T(4,128)}, u32[]{:S(2)}) copy-start(f32[3,256,5,5]{1,0,3,2:T(4,128)} %param.11) | copy-start | bytes 230404
  5.3 28.1 %copy-start.11 = (bf16[128,256]{1,0:T(8,128)(2,1)S(1)}, bf16[128,256]{1,0:T(8,128)(2,1)}, u32[]{:S(2)}) copy-start(bf16[128,256]{1,0:T(8,128)(2,1)} %get-tuple-element.25) | copy-start | bytes 196612
  5.3 32.7 %copy-start.13 = (bf16[64,256]{1,0:T(8,128)(2,1)S(1)}, bf16[64,256]{1,0:T(8,128)(2,1)}, u32[]{:S(2)}) copy-start(bf16[64,256]{1,0:T(8,128)(2,1)} %get-tuple-element.22) | copy-start | bytes 98308
  5.3 32.7 %copy-start.12 = (bf16[64,256]{1,0:T(8,128)(2,1)S(1)}, bf16[64,256]{1,0:T(8,128)(2,1)}, u32[]{:S(2)}) copy-start(bf16[64,256]{1,0:T(8,128)(2,1)} %get-tuple-element.23) | copy-start | bytes 98308
  5.3 36.3 %collective-permute-start.2 = (bf16[128,256]{1,0:T(8,128)(2,1)}, bf16[128,256]{1,0:T(8,128)(2,1)S(1)}, u32[]{:S(2)}, u32[]{:S(2)}) collective-permute-start(bf16[128,256]{1,0:T(8,128)(2,1)} %get-tuple-element.24), channel_id=1, source_target_pairs={{0,1},{1,2},{2,3},{3,4},{4,5},{5,6},{6,7},{7,0},{8,9},{9,10},{10,1... | collective-permute-start | bytes 196616 | tf_op jit(solution)/shard_map/ppermute | solution.py:568
  9.1 24.3 %collective-permute-start.4 = (bf16[4,256]{1,0:T(4,128)(2,1)S(1)}, bf16[4,256]{1,0:T(4,128)(2,1)S(1)}, u32[]{:S(2)}, u32[]{:S(2)}) collective-permute-start(bf16[4,256]{1,0:T(4,128)(2,1)S(1)} %reshape.340), channel_id=1, source_target_pairs={{0,9},{1,10},{2,11},{3,12},{4,13},{5,14},{6,15},{7,8},{8,17},{9,18... | collective-permute-start | bytes 6152 | tf_op jit(solution)/shard_map/ppermute | solution.py:568
  10.6 27.4 %collective-permute-start.5 = (bf16[4,256]{1,0:T(4,128)(2,1)S(1)}, bf16[4,256]{1,0:T(4,128)(2,1)S(1)}, u32[]{:S(2)}, u32[]{:S(2)}) collective-permute-start(bf16[4,256]{1,0:T(4,128)(2,1)S(1)} %reshape.342), channel_id=1, source_target_pairs={{0,15},{1,8},{2,9},{3,10},{4,11},{5,12},{6,13},{7,14},{8,23},{9,16... | collective-permute-start | bytes 6152 | tf_op jit(solution)/shard_map/ppermute | solution.py:568
  15.4 22.6 %collective-permute-start.6 = (bf16[4,256]{1,0:T(4,128)(2,1)S(1)}, bf16[4,256]{1,0:T(4,128)(2,1)S(1)}, u32[]{:S(2)}, u32[]{:S(2)}) collective-permute-start(bf16[4,256]{1,0:T(4,128)(2,1)S(1)} %reshape.343), channel_id=1, source_target_pairs={{0,25},{1,26},{2,27},{3,28},{4,29},{5,30},{6,31},{7,24},{8,1},{9,2... | collective-permute-start | bytes 6152 | tf_op jit(solution)/shard_map/ppermute | solution.py:568
  15.4 24.3 %collective-permute-start.7 = (bf16[4,256]{1,0:T(4,128)(2,1)S(1)}, bf16[4,256]{1,0:T(4,128)(2,1)S(1)}, u32[]{:S(2)}, u32[]{:S(2)}) collective-permute-start(bf16[4,256]{1,0:T(4,128)(2,1)S(1)} %reshape.344), channel_id=1, source_target_pairs={{0,31},{1,24},{2,25},{3,26},{4,27},{5,28},{6,29},{7,30},{8,7},{9,0... | collective-permute-start | bytes 6152 | tf_op jit(solution)/shard_map/ppermute | solution.py:568
  19.7 30.2 %all-to-all-start = ((bf16[32,128,128]{2,1,0:T(8,128)(2,1)}), bf16[32,128,128]{2,1,0:T(8,128)(2,1)S(1)}, u32[]{:S(2)}, u32[]{:S(2)}) async-start(bf16[32,128,128]{2,1,0:T(8,128)(2,1)} %get-tuple-element.21), calls=%async_computation | async-start | bytes 2097152 | tf_op jit(solution)/shard_map/all_to_all | solution.py:617
  33.4 8.2 %collective-permute-start.3 = (bf16[128,256]{1,0:T(8,128)(2,1)S(1)}, bf16[128,256]{1,0:T(8,128)(2,1)S(1)}, u32[]{:S(2)}, u32[]{:S(2)}) collective-permute-start(bf16[128,256]{1,0:T(8,128)(2,1)S(1)} %copy-done.11), channel_id=1, source_target_pairs={{0,7},{1,0},{2,1},{3,2},{4,3},{5,4},{6,5},{7,6},{8,15},{9,8},{10,9... | collective-permute-start | bytes 196616 | tf_op jit(solution)/shard_map/ppermute | solution.py:568
  38.0 3.6 %collective-permute-start = (bf16[64,256]{1,0:T(8,128)(2,1)S(1)}, bf16[64,256]{1,0:T(8,128)(2,1)S(1)}, u32[]{:S(2)}, u32[]{:S(2)}) collective-permute-start(bf16[64,256]{1,0:T(8,128)(2,1)S(1)} %copy-done.13), channel_id=1, source_target_pairs={{0,8},{1,9},{2,10},{3,11},{4,12},{5,13},{6,14},{7,15},{8,16},{9,17... | collective-permute-start | bytes 98312 | tf_op jit(solution)/shard_map/ppermute | solution.py:568
  38.0 3.6 %collective-permute-start.1 = (bf16[64,256]{1,0:T(8,128)(2,1)S(1)}, bf16[64,256]{1,0:T(8,128)(2,1)S(1)}, u32[]{:S(2)}, u32[]{:S(2)}) collective-permute-start(bf16[64,256]{1,0:T(8,128)(2,1)S(1)} %copy-done.12), channel_id=1, source_target_pairs={{0,24},{1,25},{2,26},{3,27},{4,28},{5,29},{6,30},{7,31},{8,0},{9,1... | collective-permute-start | bytes 98312 | tf_op jit(solution)/shard_map/ppermute | solution.py:568
  41.6 16.1 %copy-start.5 = (bf16[64,256]{1,0:T(8,128)(2,1)}, bf16[64,256]{1,0:T(8,128)(2,1)S(1)}, u32[]{:S(2)}) copy-start(bf16[64,256]{1,0:T(8,128)(2,1)S(1)} %collective-permute-done.1.high_ref) | copy-start | bytes 98308
  41.6 16.1 %copy-start.3 = (bf16[128,256]{1,0:T(8,128)(2,1)}, bf16[128,256]{1,0:T(8,128)(2,1)S(1)}, u32[]{:S(2)}) copy-start(bf16[128,256]{1,0:T(8,128)(2,1)S(1)} %collective-permute-done.3.right_ref) | copy-start | bytes 196612
  57.7 30.6 %all-to-all-start.1 = ((bf16[32,128,128]{2,1,0:T(8,128)(2,1)}), bf16[32,128,128]{2,1,0:T(8,128)(2,1)S(1)}, u32[]{:S(2)}, u32[]{:S(2)}) async-start(bf16[32,128,128]{2,1,0:T(8,128)(2,1)} %bitcast.7), calls=%async_computation.1 | async-start | bytes 2097152 | tf_op jit(solution)/shard_map/all_to_all | solution.py:652
  60.8 1.2 %copy-start.1 = (bf16[64,32,256]{2,1,0:T(8,128)(2,1)S(1)}, bf16[64,32,256]{2,1,0:T(8,128)(2,1)}, u32[]{:S(2)}) copy-start(bf16[64,32,256]{2,1,0:T(8,128)(2,1)} %get-tuple-element.31.grad_ref) | copy-start | bytes 3145732
  62.1 1.0 %copy-start.2 = (bf16[3,256,256]{2,1,0:T(8,128)(2,1)S(1)}, bf16[3,256,256]{2,1,0:T(8,128)(2,1)}, u32[]{:S(2)}) copy-start(bf16[3,256,256]{2,1,0:T(8,128)(2,1)} %mix_ref.1) | copy-start | bytes 1179652
  63.1 0.8 copy-start.4
  63.9 0.8 copy-start.6

commit v3 on v2

--- a/solution.py
+++ b/solution.py
@@ -56,27 +56,37 @@
     for chunk in range(CHUNKS):
         for copy in fetch(chunk):
             copy.start()
+    def one_block(q_index, carry):
+        base = q_index * group
+        for row in range(group):
+            at = base + row
+            grad = (cot_ref[at].astype(F32) * gelu_slope(pre_ref[at].astype(F32))).astype(BF16)
+            grad_ref[at] = grad
+            rows_scr[at] = grad.astype(F32)
+        q_out = jnp.where(flip == 1, q_count - 1 - q_index, q_index)
+        slabs = []
+        for r in range(group):
+            slabs.append(rows_scr[base + jnp.where(flip == 1, group - 1 - r, r)])
+        stacked = jnp.concatenate(slabs, axis=0)
+        for tile in range(channels // LANES):
+            turned = stacked[:, tile * LANES : (tile + 1) * LANES].T
+            chan_scr[pl.ds(tile * LANES * q_count + q_out, LANES, stride=q_count), :] = turned
+        return carry
+
     for chunk in range(CHUNKS):
         for copy in fetch(chunk):
             copy.wait()
-        for row in range(chunk * part, (chunk + 1) * part):
-            grad = (cot_ref[row].astype(F32) * gelu_slope(pre_ref[row].astype(F32))).astype(BF16)
-            grad_ref[row] = grad
-            rows_scr[row] = grad.astype(F32)
+        lax.fori_loop(chunk * part // group, (chunk + 1) * part // group, one_block, 0)
         keep(chunk).start()
-        for q_index in range(chunk * part // group, (chunk + 1) * part // group):
-            q_out = jnp.where(flip == 1, q_count - 1 - q_index, q_index)
-            slabs = []
-            for r in range(group):
-                slabs.append(rows_scr[q_index * group + jnp.where(flip == 1, group - 1 - r, r)])
-            stacked = jnp.concatenate(slabs, axis=0)
-            for tile in range(channels // LANES):
-                turned = stacked[:, tile * LANES : (tile + 1) * LANES].T
-                chan_scr[pl.ds(tile * LANES * q_count + q_out, LANES, stride=q_count), :] = turned
     dests, count = send_ref.shape[:2]
-    for chunk in range(CHUNKS):
-        for dest in range(chunk * dests // CHUNKS, (chunk + 1) * dests // CHUNKS):
-            send_ref[dest] = chan_scr[dest * count : (dest + 1) * count, :].astype(BF16)
+
+    def one_dest(dest, carry):
+        at = pl.ds(pl.multiple_of(dest * count, 16), count)
+        send_ref[dest] = chan_scr[at, :].astype(BF16)
+        return carry
+
+    for chunk in range(CHUNKS):
+        lax.fori_loop(chunk * dests // CHUNKS, (chunk + 1) * dests // CHUNKS, one_dest, 0)
         send(chunk).start()
     for row in range(REACH):
         first_ref[row * cols : (row + 1) * cols, :] = grad_ref[row]
@@ -187,7 +197,7 @@
         scratch_shapes=[pltpu.VMEM((block * (degrees + PAD), LANES), F32)],
         compiler_params=params(56 * MIB),
         cost_estimate=pl.CostEstimate(
-            flops=40 * orders * degrees * points,
+            flops=4000 * orders * degrees * points,
             bytes_accessed=4 * orders * degrees * points,
             transcendentals=0,
         ),
@@ -222,7 +232,7 @@
         ]
 
     def give(chan):
-        at = pl.ds(chan * q_count, q_count)
+        at = pl.ds(pl.multiple_of(chan * q_count, 16), q_count)
         return pltpu.make_async_copy(back_ref.at[:, :, at], back_hbm.at[:, :, at], back_sems.at[chan])
 
     def place(band, r):
@@ -241,13 +251,11 @@
             copy.start()
     receive.wait()
 
-    for chan in range(local):
-        at = chan * q_count
+    def analyse(chan, carry):
+        at = pl.ds(pl.multiple_of(chan * q_count, 16), q_count)
         for band in range(bands):
             for unit in range(sectors // group):
-                pieces = [
-                    recv_ref[band, unit * group + k, at : at + q_count, :].astype(F32) for k in range(group)
-                ]
+                pieces = [recv_ref[band, unit * group + k, at, :].astype(F32) for k in range(group)]
                 for r in range(group):
                     value = rolled(pieces[0], -r)
                     for k in range(1, group):
@@ -257,11 +265,15 @@
         spectrum = lax.dot_general(
             forward_ref[...], grid_scr[chan], (((1,), (1,)), ((), ())), preferred_element_type=F32
         )
+        rows = pl.ds(pl.multiple_of(chan * pitch, 8), modes)
         for tile in range(tiles):
             north = spectrum[:, tile * LANES : (tile + 1) * LANES]
             south = spectrum[:, half + tile * LANES : half + (tile + 1) * LANES]
-            even_scr[tile, chan * pitch : chan * pitch + modes, :] = north + south
-            odd_scr[tile, chan * pitch : chan * pitch + modes, :] = north - south
+            even_scr[tile, rows, :] = north + south
+            odd_scr[tile, rows, :] = north - south
+        return carry
+
+    lax.fori_loop(0, local, analyse, 0)
 
     def lines(tile, mode):
         if local == 1:
@@ -340,8 +352,8 @@
 
     lax.fori_loop(0, blocks, one_block, 0)
 
-    for chan in range(local):
-        rows = slice(chan * pitch, chan * pitch + modes)
+    def restore(chan, carry):
+        rows = pl.ds(pl.multiple_of(chan * pitch, 8), modes)
         profile = jnp.concatenate(
             [scr[tile, rows, :].astype(BF16) for scr in (north_scr, south_scr) for tile in range(tiles)],
             axis=1,
@@ -349,7 +361,7 @@
         field = lax.dot_general(
             profile, inverse_ref[...], (((0,), (0,)), ((), ())), preferred_element_type=F32
         )
-        at = chan * q_count
+        at = pl.ds(pl.multiple_of(chan * q_count, 16), q_count)
         for band in range(bands):
             for unit in range(sectors // group):
                 pieces = []
@@ -360,8 +372,11 @@
                     value = rolled(pieces[0], -k)
                     for r in range(1, group):
                         value = jnp.where(lane_group == r, rolled(pieces[r], r - k), value)
-                    back_ref[band, unit * group + k, at : at + q_count, :] = value.astype(BF16)
+                    back_ref[band, unit * group + k, at, :] = value.astype(BF16)
         give(chan).start()
+        return carry
+
+    lax.fori_loop(0, local, restore, 0)
     for chan in range(local):
         give(chan).wait()
 
@@ -428,7 +443,7 @@
                     padded[half, base + row, origin : origin + cols, :] = values[row * cols : (row + 1) * cols]
                     for side in range(REACH):
                         for end, column in enumerate((origin - REACH, origin + cols)):
-                            at = ((edge * 2 + end) * REACH + side) * REACH + row
+                            at = ((end * 2 + edge) * REACH + row) * REACH + side
                             column = column + side
                             padded[half, base + row, column : column + 1, :] = corners[at : at + 1]
             for source, column in ((left_ref, origin - REACH), (right_ref, origin + cols)):
@@ -505,25 +520,31 @@
         at = pl.ds(chunk * part, part)
         return pltpu.make_async_copy(out_ref.at[at], out_hbm.at[at], out_sems.at[chunk])
 
+    def one_source(source, carry):
+        chan_scr[pl.ds(pl.multiple_of(source * count, 16), count), :] = back_ref[source].astype(F32)
+        return carry
+
+    def one_block(q_index, carry):
+        q_from = jnp.where(flip == 1, q_count - 1 - q_index, q_index)
+        turned = jnp.concatenate(
+            [
+                chan_scr[pl.ds(tile * LANES * q_count + q_from, LANES, stride=q_count), :].T
+                for tile in range(channels // LANES)
+            ],
+            axis=1,
+        )
+        for r in range(group):
+            row = q_index * group + jnp.where(flip == 1, group - 1 - r, r)
+            out_ref[row] = (disco_ref[row] + turned[r * cols : (r + 1) * cols]).astype(BF16)
+        return carry
+
     for chunk in range(CHUNKS):
         fetch(chunk).start()
     for chunk in range(CHUNKS):
         fetch(chunk).wait()
-        for source in range(chunk * sources // CHUNKS, (chunk + 1) * sources // CHUNKS):
-            chan_scr[source * count : (source + 1) * count, :] = back_ref[source].astype(F32)
-    for chunk in range(CHUNKS):
-        for q_index in range(chunk * part // group, (chunk + 1) * part // group):
-            q_from = jnp.where(flip == 1, q_count - 1 - q_index, q_index)
-            turned = jnp.concatenate(
-                [
-                    chan_scr[pl.ds(tile * LANES * q_count + q_from, LANES, stride=q_count), :].T
-                    for tile in range(channels // LANES)
-                ],
-                axis=1,
-            )
-            for r in range(group):
-                row = q_index * group + jnp.where(flip == 1, group - 1 - r, r)
-                out_ref[row] = (disco_ref[row] + turned[r * cols : (r + 1) * cols]).astype(BF16)
+        lax.fori_loop(chunk * sources // CHUNKS, (chunk + 1) * sources // CHUNKS, one_source, 0)
+    for chunk in range(CHUNKS):
+        lax.fori_loop(chunk * part // group, (chunk + 1) * part // group, one_block, 0)
         give(chunk).start()
     for chunk in range(CHUNKS):
         give(chunk).wait()
@@ -554,38 +575,17 @@
     )(flip, back, local_part)
 
 
-def shifted(block, lat_step, lon_step):
-    lat_count = lax.axis_size("lat")
-    lon_count = lax.axis_size("lon")
-    pairs = [
-        (
-            lat * lon_count + lon,
-            (lat + lat_step) % lat_count * lon_count + (lon + lon_step) % lon_count,
-        )
-        for lat in range(lat_count)
-        for lon in range(lon_count)
-    ]
-    return lax.ppermute(block, ("lat", "lon"), pairs)
-
-
-def halos(first_rows, last_rows, west, east):
-    channels = west.shape[-1]
-
-    def corner(side, start):
-        block = side.reshape(REACH, -1, channels)[:, start:][:, :REACH]
-        return block.reshape(REACH * REACH, channels)
-
-    low = shifted(last_rows, 1, 0)
-    high = shifted(first_rows, -1, 0)
-    left = shifted(east, 0, 1)
-    right = shifted(west, 0, -1)
-    corners = [
-        shifted(corner(east, -REACH), 1, 1),
-        shifted(corner(west, -REACH), 1, -1),
-        shifted(corner(east, 0), -1, 1),
-        shifted(corner(west, 0), -1, -1),
-    ]
-    return (low, high, left, right, jnp.concatenate(corners, axis=0))
+def shifted(block, axis, step):
+    count = lax.axis_size(axis)
+    return lax.ppermute(block, axis, [(i, (i + step) % count) for i in range(count)])
+
+
+def corners_of(low, high, channels):
+    def ends(start):
+        blocks = [side.reshape(REACH, -1, channels)[:, start:][:, :REACH] for side in (low, high)]
+        return jnp.concatenate(blocks, axis=0).reshape(2 * REACH * REACH, channels)
+
+    return jnp.concatenate([shifted(ends(-REACH), "lon", 1), shifted(ends(0), "lon", -1)], axis=0)
 
 
 def fourier_tables(order_count, points):
@@ -645,14 +645,24 @@
     tap_coef = lax.dynamic_slice_in_dim(tap_coef, band_index * lat_rows, lat_rows + 2 * REACH, 1)
     taps = jnp.transpose(tap_coef, (1, 0, 2, 3)).reshape(lat_rows + 2 * REACH, -1)
 
-    received, rim = lax.optimization_barrier((received, halos(*edges)))
+    first_rows, last_rows, west, east = edges
+    edges, tables = lax.optimization_barrier((edges, tables))
+    first_rows, last_rows, west, east = edges
+    sides = (
+        shifted(last_rows, "lat", 1),
+        shifted(first_rows, "lat", -1),
+        shifted(east, "lon", 1),
+        shifted(west, "lon", -1),
+    )
+    received, sides = lax.optimization_barrier((received, sides))
     blocks = received.reshape(lat_count, lon_count, local * q_count, LANES)
     back = spectral(blocks, forward, inverse, tables, weights, quad, group)
-    back, taps = lax.optimization_barrier((back, taps))
+    back, taps, sides = lax.optimization_barrier((back, taps, sides))
+    corners = corners_of(sides[0], sides[1], channels)
     returned = lax.all_to_all(
         back.reshape(devices, local * q_count, LANES), ("lat", "lon"), 0, 0, tiled=True
     )
-    local_part = disco(taps, grad_pre, *rim, disco_weight)
+    local_part = disco(taps, grad_pre, *sides, corners, disco_weight)
     return combine(returned, local_part, flip, group)
 
 

time: 91.2 us -> 104 us (1.14); the launches traced: 90.6 us -> 102 us
  waiting for transfers between devices: 18 us -> 28.9 us
  Pallas kernels: 39.4 us -> 44.8 us
  starting transfers between devices: 24.9 us -> 21.3 us
  local copies, waits for them, and re-layouts: 5.86 us -> 4.4 us
    ppermute x8 -> x6, waiting for transfers between devices: 1.82 us -> 23.8 us  [shifted(): lax.ppermute(block, axis, [(i, (i + step) % count) for i in range(count)])]
    ppermute x8 -> x6, starting transfers between devices: 19.2 us -> 11.3 us  [shifted(): lax.ppermute(block, axis, [(i, (i + step) % count) for i in range(count)])]
    all_to_all x1, waiting for transfers between devices: 7.84 us -> 0.01 us  [shards(): lax.all_to_all(back.reshape(devices, local * q_count, LANES), ('lat', 'lo...]
    all_to_all x1, starting transfers between devices: 2.64 us -> 7.36 us  [shards(): received = lax.all_to_all(to_send, ('lat', 'lon'), 0, 0, tiled=True)]
    all_to_all x1, waiting for transfers between devices: 8.38 us -> 5.08 us  [shards(): received = lax.all_to_all(to_send, ('lat', 'lon'), 0, 0, tiled=True)]
    pallas_call x1, Pallas kernels: 7.69 us -> 10.9 us  [spectral(): pl.pallas_call(functools.partial(spectral_kernel, group=group, q_count=q_...]
    slice x2, local copies, waits for them, and re-layouts: 1.46 us -> 0.02 us  [ends(): side.reshape(REACH, -1, channels)[:, start:][:, :REACH]]
    pallas_call x1, Pallas kernels: 2.28 us -> 3.35 us  [combine(): pl.pallas_call(functools.partial(combine_kernel, group=group, q_count=q_c...]
  transfers between devices with their start and end apart: 10 -> 8, of which waited for: 3 -> 5; matrix products, arithmetic and copies ran while one was open for 5% -> 3% of each run, Pallas kernels for 27% -> 24%
where the time goes in v3:
time: 104 us; the launch traced here: 102 us
  Pallas kernels  44.8 us (43%)
  waiting for transfers between devices  28.9 us (28%)
  starting transfers between devices  21.3 us (20%)
  local copies, waits for them, and re-layouts  4.4 us (4%)
  other arithmetic  2.19 us (2%)
    ppermute x6, waiting for transfers between devices, shifted(): lax.ppermute(block, axis, [(i, (i + step) % count) for i in range(count)])  23.8 us
    pallas_call x1, Pallas kernels, disco(): pl.pallas_call(disco_kernel, grid=(steps,), in_specs=[pl.BlockSpec(memory...  15.8 us
    ppermute x6, starting transfers between devices, shifted(): lax.ppermute(block, axis, [(i, (i + step) % count) for i in range(count)])  11.3 us
    pallas_call x1, Pallas kernels, spectral(): pl.pallas_call(functools.partial(spectral_kernel, group=group, q_count=q_...  10.9 us
    pallas_call x1, Pallas kernels, legendre(): pl.pallas_call(functools.partial(legendre_kernel, degrees=degrees, span=8...  8.44 us
    all_to_all x1, starting transfers between devices, shards(): received = lax.all_to_all(to_send, ('lat', 'lon'), 0, 0, tiled=True)  7.36 us
    pallas_call x1, Pallas kernels, gradient(): pl.pallas_call(functools.partial(grad_kernel, group=group, q_count=q_coun...  6.23 us
    all_to_all x1, waiting for transfers between devices, shards(): received = lax.all_to_all(to_send, ('lat', 'lon'), 0, 0, tiled=True)  5.08 us
  transfers between devices with their start and end apart: 8, of which 5 were waited for; matrix products, arithmetic and copies ran while one was open for 3% of the time, Pallas kernels for 24%

profile of v3, /device:TPU:0, one launch (start us, length us, event | category | flops | bytes accessed | tf_op | source)
XLA Modules:
  0.0 101.8 jit_solution(9526377492773749952)
XLA Ops:
  0.0 0.0 copy-start
  0.0 0.0 copy-start.10
  0.0 6.2 %gradient.1 = (bf16[64,32,256]{2,1,0:T(8,128)(2,1)}, bf16[32,128,128]{2,1,0:T(8,128)(2,1)}, bf16[64,256]{1,0:T(8,128)(2,1)}, bf16[64,256]{1,0:T(8,128)(2,1)}, bf...) custom-call(s32[1]{0:T(128)} %bitcast.flip_ref, bf16[64,32,256]{2,1,0:T(8,128)(2,1)} %pre_hbm.1, bf16[64,32,256]{2,1,0:T(8,128)(2,1)} %cot_hbm.1), custom_call_target="tpu_custom_call" | custom-call | tf_op jit(solution)/shard_map/gradient/pallas_call | solution.py:109
  6.2 7.4 %all-to-all-start = ((bf16[32,128,128]{2,1,0:T(8,128)(2,1)}), bf16[32,128,128]{2,1,0:T(8,128)(2,1)S(1)}, u32[]{:S(2)}, u32[]{:S(2)}) async-start(bf16[32,128,128]{2,1,0:T(8,128)(2,1)} %get-tuple-element.30), calls=%async_computation | async-start | bytes 2097152 | tf_op jit(solution)/shard_map/all_to_all | solution.py:617
  13.6 0.1 fusion.21
  13.7 0.6 pad_maximum_fusion.4.norm_ref
  14.3 0.0 copy-done.10
  14.3 0.7 multiply_add_fusion.start_ref
  15.0 0.0 copy-start.12
  15.0 0.0 copy-start.11
  15.0 0.0 copy-start.14
  15.0 0.0 copy-start.13
  15.0 0.0 copy-start.9
  15.1 0.0 copy-start.8
  15.1 0.0 copy-start.7
  15.1 8.4 %legendre.1 = (bf16[128,128,128]{2,1,0:T(8,128)(2,1)}, bf16[128,128,128]{2,1,0:T(8,128)(2,1)}) custom-call(f32[2,128]{1,0:T(2,128)} %pad_maximum_fusion.4.norm_ref, f32[1,128]{1,0:T(1,128)} %constant.119.cos_ref, f32[128,128]{1,0:T(8,128)} %multiply_add_fusion.start_ref), custom_call_target="tpu_custom_call" | custom-call | flops 8388608000 | bytes 8388608 | tf_op jit(solution)/shard_map/legendre/pallas_call | solution.py:181
  23.5 0.0 copy-done.12
  23.5 1.8 %collective-permute-start.2 = (bf16[128,256]{1,0:T(8,128)(2,1)S(1)}, bf16[128,256]{1,0:T(8,128)(2,1)S(1)}, u32[]{:S(2)}, u32[]{:S(2)}) collective-permute-start(bf16[128,256]{1,0:T(8,128)(2,1)S(1)} %copy-done.12), channel_id=1, source_target_pairs={{0,1},{1,2},{2,3},{3,4},{4,5},{5,6},{6,7},{7,0},{8,9},{9,10},{10,1... | collective-permute-start | bytes 196616 | tf_op jit(solution)/shard_map/ppermute | solution.py:580
  25.3 0.0 copy-done.11
  25.3 3.0 %collective-permute-start.3 = (bf16[128,256]{1,0:T(8,128)(2,1)S(1)}, bf16[128,256]{1,0:T(8,128)(2,1)S(1)}, u32[]{:S(2)}, u32[]{:S(2)}) collective-permute-start(bf16[128,256]{1,0:T(8,128)(2,1)S(1)} %copy-done.11), channel_id=1, source_target_pairs={{0,7},{1,0},{2,1},{3,2},{4,3},{5,4},{6,5},{7,6},{8,15},{9,8},{10,9... | collective-permute-start | bytes 196616 | tf_op jit(solution)/shard_map/ppermute | solution.py:580
  28.3 0.0 copy-done.14
  28.3 0.0 collective-permute-start
  28.3 0.0 copy-done.13
  28.3 1.7 %collective-permute-start.1 = (bf16[64,256]{1,0:T(8,128)(2,1)S(1)}, bf16[64,256]{1,0:T(8,128)(2,1)S(1)}, u32[]{:S(2)}, u32[]{:S(2)}) collective-permute-start(bf16[64,256]{1,0:T(8,128)(2,1)S(1)} %copy-done.13), channel_id=1, source_target_pairs={{0,24},{8,0},{16,8},{24,16},{1,25},{9,1},{17,9},{25,17},{2,26},{10... | collective-permute-start | bytes 98312 | tf_op jit(solution)/shard_map/ppermute | solution.py:580
  30.0 0.0 copy-done
  30.0 0.2 constant_dynamic-slice_fusion
  30.2 0.5 sine_negate_fusion
  30.8 0.0 copy-done.9
  30.8 0.1 compare_convert_fusion
  30.9 0.1 multiply_convert_fusion.forward_ref
  31.0 0.0 copy-done.8
  31.0 0.1 fusion.8
  31.1 0.1 copy.13
  31.3 0.3 collective-permute-done.low_ref
  31.6 0.1 collective-permute-done.1.high_ref
  31.7 0.0 copy-start.5
  31.7 5.8 %collective-permute-done.2.left_ref = bf16[128,256]{1,0:T(8,128)(2,1)S(1)} collective-permute-done((bf16[128,256]{1,0:T(8,128)(2,1)S(1)}, bf16[128,256]{1,0:T(8,128)(2,1)S(1)}, u32[]{:S(2)}, u32[]{:S(2)}) %collective-permute-start.2) | collective-permute-done | bytes 65568 | tf_op jit(solution)/shard_map/ppermute | solution.py:580
  37.5 0.0 collective-permute-done.3.right_ref
  37.5 0.0 copy-start.3
  37.5 5.1 %all-to-all-done = bf16[32,128,128]{2,1,0:T(8,128)(2,1)S(1)} async-done(((bf16[32,128,128]{2,1,0:T(8,128)(2,1)}), bf16[32,128,128]{2,1,0:T(8,128)(2,1)S(1)}, u32[]{:S(2)}, u32[]{:S(2)}) %all-to-all-start) | async-done | bytes 1048608 | tf_op jit(solution)/shard_map/all_to_all | solution.py:617
  42.6 0.0 copy-done.7
  42.6 10.9 %spectral.1 = bf16[4,8,128,128]{3,2,1,0:T(8,128)(2,1)} custom-call(bf16[4,8,128,128]{3,2,1,0:T(8,128)(2,1)S(1)} %bitcast.11, bf16[256,256]{1,0:T(8,128)(2,1)S(1)} %multiply_convert_fusion.forward_ref, bf16[256,256]{1,0:T(8,128)(2,1)S(1)} %fusion.inverse_ref, f32[2,8,128]{2,1,0:T(8,128)S(1)} %bitcast.14, f32[1,128]{1,0:T(1,128)S(1)} %copy-done.7, ...), custom_call_target="tpu_custom_call" | custom-call | tf_op jit(solution)/shard_map/spectral/pallas_call | solution.py:397
  53.5 0.0 copy-done.3
  53.6 2.7 %all-to-all-start.1 = ((bf16[32,128,128]{2,1,0:T(8,128)(2,1)}), bf16[32,128,128]{2,1,0:T(8,128)(2,1)S(1)}, u32[]{:S(2)}, u32[]{:S(2)}) async-start(bf16[32,128,128]{2,1,0:T(8,128)(2,1)} %bitcast.5), calls=%async_computation.1 | async-start | bytes 2097152 | tf_op jit(solution)/shard_map/all_to_all | solution.py:662
  56.2 0.0 copy-done.5
  56.3 1.7 %collective-permute-start.4 = (bf16[8,256]{1,0:T(8,128)(2,1)S(1)}, bf16[8,256]{1,0:T(8,128)(2,1)S(1)}, u32[]{:S(2)}, u32[]{:S(2)}) collective-permute-start(bf16[8,256]{1,0:T(8,128)(2,1)S(1)} %reshape.338), channel_id=1, source_target_pairs={{0,1},{1,2},{2,3},{3,4},{4,5},{5,6},{6,7},{7,0},{8,9},{9,10},{10,1... | collective-permute-start | bytes 12296 | tf_op jit(solution)/shard_map/ppermute | solution.py:580
  58.0 3.1 %collective-permute-start.5 = (bf16[8,256]{1,0:T(8,128)(2,1)S(1)}, bf16[8,256]{1,0:T(8,128)(2,1)S(1)}, u32[]{:S(2)}, u32[]{:S(2)}) collective-permute-start(bf16[8,256]{1,0:T(8,128)(2,1)S(1)} %reshape.339), channel_id=1, source_target_pairs={{0,7},{1,0},{2,1},{3,2},{4,3},{5,4},{6,5},{7,6},{8,15},{9,8},{10,9... | collective-permute-start | bytes 12296 | tf_op jit(solution)/shard_map/ppermute | solution.py:580
  61.2 0.1 copy.12.tap_ref
  61.2 17.6 %collective-permute-done.4 = bf16[8,256]{1,0:T(8,128)(2,1)S(1)} collective-permute-done((bf16[8,256]{1,0:T(8,128)(2,1)S(1)}, bf16[8,256]{1,0:T(8,128)(2,1)S(1)}, u32[]{:S(2)}, u32[]{:S(2)}) %collective-permute-start.4) | collective-permute-done | bytes 4128 | tf_op jit(solution)/shard_map/ppermute | solution.py:580
  78.8 0.0 collective-permute-done.5
  78.8 0.0 copy-start.1
  78.8 1.2 %copy-done.1 = bf16[64,32,256]{2,1,0:T(8,128)(2,1)S(1)} copy-done((bf16[64,32,256]{2,1,0:T(8,128)(2,1)S(1)}, bf16[64,32,256]{2,1,0:T(8,128)(2,1)}, u32[]{:S(2)}) %copy-start.1) | copy-done | bytes 1048600
  80.0 0.0 copy-start.2
  80.0 1.0 copy-done.2
  81.0 0.0 copy-start.4
  81.0 0.8 copy-done.4
  81.9 0.0 copy-start.6
  81.9 0.8 copy-done.6
  82.6 15.8 %disco.1.disco_ref = f32[64,32,256]{2,1,0:T(8,128)S(1)} custom-call(f32[68,75]{1,0:T(8,128)S(1)} %copy.12.tap_ref, bf16[64,32,256]{2,1,0:T(8,128)(2,1)S(1)} %copy-done.1, bf16[64,256]{1,0:T(8,128)(2,1)S(1)} %collective-permute-done.low_ref, bf16[64,256]{1,0:T(8,128)(2,1)S(1)} %copy-done.6, bf16[128,256]{1,0:T(8,128)(2,1)S(1)} %collective-permute-done.2.left_ref, ...), custom_call_target="tpu_custom_call" | custom-call | flops 524288000 | bytes 4194304 | tf_op jit(solution)/shard_map/disco/pallas_call | solution.py:488
  98.5 0.0 all-to-all-done.1.back_hbm
  98.5 3.4 %combine.1 = bf16[64,32,256]{2,1,0:T(8,128)(2,1)} custom-call(s32[1]{0:T(128)} %bitcast.flip_ref, bf16[32,128,128]{2,1,0:T(8,128)(2,1)S(1)} %all-to-all-done.1.back_hbm, f32[64,32,256]{2,1,0:T(8,128)S(1)} %disco.1.disco_ref), custom_call_target="tpu_custom_call" | custom-call | tf_op jit(solution)/shard_map/combine/pallas_call | solution.py:557
  (15 shorter events, 0.2 us)
Async XLA Ops:
  0.0 30.0 %copy-start = (f32[128,2,256]{2,1,0:T(2,128)S(1)}, f32[128,2,256]{2,1,0:T(2,128)}, u32[]{:S(2)}) copy-start(f32[128,2,256]{2,1,0:T(2,128)} %param.9) | copy-start | bytes 786436
  0.0 14.3 %copy-start.10 = (f32[128]{0:T(128)S(1)}, f32[128]{0:T(128)}, u32[]{:S(2)}) copy-start(f32[128]{0:T(128)} %constant.121) | copy-start | bytes 1540
  6.2 36.4 %all-to-all-start = ((bf16[32,128,128]{2,1,0:T(8,128)(2,1)}), bf16[32,128,128]{2,1,0:T(8,128)(2,1)S(1)}, u32[]{:S(2)}, u32[]{:S(2)}) async-start(bf16[32,128,128]{2,1,0:T(8,128)(2,1)} %get-tuple-element.30), calls=%async_computation | async-start | bytes 2097152 | tf_op jit(solution)/shard_map/all_to_all | solution.py:617
  15.0 8.5 %copy-start.12 = (bf16[128,256]{1,0:T(8,128)(2,1)S(1)}, bf16[128,256]{1,0:T(8,128)(2,1)}, u32[]{:S(2)}) copy-start(bf16[128,256]{1,0:T(8,128)(2,1)} %get-tuple-element.39) | copy-start | bytes 196612
  15.0 10.3 %copy-start.11 = (bf16[128,256]{1,0:T(8,128)(2,1)S(1)}, bf16[128,256]{1,0:T(8,128)(2,1)}, u32[]{:S(2)}) copy-start(bf16[128,256]{1,0:T(8,128)(2,1)} %get-tuple-element.40) | copy-start | bytes 196612
  15.0 13.2 %copy-start.14 = (bf16[64,256]{1,0:T(8,128)(2,1)S(1)}, bf16[64,256]{1,0:T(8,128)(2,1)}, u32[]{:S(2)}) copy-start(bf16[64,256]{1,0:T(8,128)(2,1)} %get-tuple-element.37) | copy-start | bytes 98308
  15.0 13.2 %copy-start.13 = (bf16[64,256]{1,0:T(8,128)(2,1)S(1)}, bf16[64,256]{1,0:T(8,128)(2,1)}, u32[]{:S(2)}) copy-start(bf16[64,256]{1,0:T(8,128)(2,1)} %get-tuple-element.38) | copy-start | bytes 98308
  15.0 15.8 %copy-start.9 = (s32[256,5]{0,1:T(8,128)S(1)}, s32[256,5]{0,1:T(8,128)}, u32[]{:S(2)}) copy-start(s32[256,5]{0,1:T(8,128)} %param.12) | copy-start | bytes 15364
  15.1 15.9 %copy-start.8 = (f32[3,256,5,5]{1,0,3,2:T(4,128)S(1)}, f32[3,256,5,5]{1,0,3,2:T(4,128)}, u32[]{:S(2)}) copy-start(f32[3,256,5,5]{1,0,3,2:T(4,128)} %param.11) | copy-start | bytes 230404
  15.1 27.5 %copy-start.7 = (f32[1,128]{1,0:T(1,128)S(1)}, f32[1,128]{1,0:T(1,128)}, u32[]{:S(2)}) copy-start(f32[1,128]{1,0:T(1,128)} %constant.123.quad_ref) | copy-start | bytes 1540
  23.5 14.0 %collective-permute-start.2 = (bf16[128,256]{1,0:T(8,128)(2,1)S(1)}, bf16[128,256]{1,0:T(8,128)(2,1)S(1)}, u32[]{:S(2)}, u32[]{:S(2)}) collective-permute-start(bf16[128,256]{1,0:T(8,128)(2,1)S(1)} %copy-done.12), channel_id=1, source_target_pairs={{0,1},{1,2},{2,3},{3,4},{4,5},{5,6},{6,7},{7,0},{8,9},{9,10},{10,1... | collective-permute-start | bytes 196616 | tf_op jit(solution)/shard_map/ppermute | solution.py:580
  25.3 12.2 %collective-permute-start.3 = (bf16[128,256]{1,0:T(8,128)(2,1)S(1)}, bf16[128,256]{1,0:T(8,128)(2,1)S(1)}, u32[]{:S(2)}, u32[]{:S(2)}) collective-permute-start(bf16[128,256]{1,0:T(8,128)(2,1)S(1)} %copy-done.11), channel_id=1, source_target_pairs={{0,7},{1,0},{2,1},{3,2},{4,3},{5,4},{6,5},{7,6},{8,15},{9,8},{10,9... | collective-permute-start | bytes 196616 | tf_op jit(solution)/shard_map/ppermute | solution.py:580
  28.3 3.3 %collective-permute-start = (bf16[64,256]{1,0:T(8,128)(2,1)S(1)}, bf16[64,256]{1,0:T(8,128)(2,1)S(1)}, u32[]{:S(2)}, u32[]{:S(2)}) collective-permute-start(bf16[64,256]{1,0:T(8,128)(2,1)S(1)} %copy-done.14), channel_id=1, source_target_pairs={{0,8},{8,16},{16,24},{24,0},{1,9},{9,17},{17,25},{25,1},{2,10},{10... | collective-permute-start | bytes 98312 | tf_op jit(solution)/shard_map/ppermute | solution.py:580
  28.3 3.5 %collective-permute-start.1 = (bf16[64,256]{1,0:T(8,128)(2,1)S(1)}, bf16[64,256]{1,0:T(8,128)(2,1)S(1)}, u32[]{:S(2)}, u32[]{:S(2)}) collective-permute-start(bf16[64,256]{1,0:T(8,128)(2,1)S(1)} %copy-done.13), channel_id=1, source_target_pairs={{0,24},{8,0},{16,8},{24,16},{1,25},{9,1},{17,9},{25,17},{2,26},{10... | collective-permute-start | bytes 98312 | tf_op jit(solution)/shard_map/ppermute | solution.py:580
  31.7 24.5 %copy-start.5 = (bf16[64,256]{1,0:T(8,128)(2,1)}, bf16[64,256]{1,0:T(8,128)(2,1)S(1)}, u32[]{:S(2)}) copy-start(bf16[64,256]{1,0:T(8,128)(2,1)S(1)} %collective-permute-done.1.high_ref) | copy-start | bytes 98308
  37.5 16.0 %copy-start.3 = (bf16[128,256]{1,0:T(8,128)(2,1)}, bf16[128,256]{1,0:T(8,128)(2,1)S(1)}, u32[]{:S(2)}) copy-start(bf16[128,256]{1,0:T(8,128)(2,1)S(1)} %collective-permute-done.3.right_ref) | copy-start | bytes 196612
  53.6 44.9 %all-to-all-start.1 = ((bf16[32,128,128]{2,1,0:T(8,128)(2,1)}), bf16[32,128,128]{2,1,0:T(8,128)(2,1)S(1)}, u32[]{:S(2)}, u32[]{:S(2)}) async-start(bf16[32,128,128]{2,1,0:T(8,128)(2,1)} %bitcast.5), calls=%async_computation.1 | async-start | bytes 2097152 | tf_op jit(solution)/shard_map/all_to_all | solution.py:662
  56.3 22.5 %collective-permute-start.4 = (bf16[8,256]{1,0:T(8,128)(2,1)S(1)}, bf16[8,256]{1,0:T(8,128)(2,1)S(1)}, u32[]{:S(2)}, u32[]{:S(2)}) collective-permute-start(bf16[8,256]{1,0:T(8,128)(2,1)S(1)} %reshape.338), channel_id=1, source_target_pairs={{0,1},{1,2},{2,3},{3,4},{4,5},{5,6},{6,7},{7,0},{8,9},{9,10},{10,1... | collective-permute-start | bytes 12296 | tf_op jit(solution)/shard_map/ppermute | solution.py:580
  58.0 20.8 %collective-permute-start.5 = (bf16[8,256]{1,0:T(8,128)(2,1)S(1)}, bf16[8,256]{1,0:T(8,128)(2,1)S(1)}, u32[]{:S(2)}, u32[]{:S(2)}) collective-permute-start(bf16[8,256]{1,0:T(8,128)(2,1)S(1)} %reshape.339), channel_id=1, source_target_pairs={{0,7},{1,0},{2,1},{3,2},{4,3},{5,4},{6,5},{7,6},{8,15},{9,8},{10,9... | collective-permute-start | bytes 12296 | tf_op jit(solution)/shard_map/ppermute | solution.py:580
  78.8 1.2 %copy-start.1 = (bf16[64,32,256]{2,1,0:T(8,128)(2,1)S(1)}, bf16[64,32,256]{2,1,0:T(8,128)(2,1)}, u32[]{:S(2)}) copy-start(bf16[64,32,256]{2,1,0:T(8,128)(2,1)} %get-tuple-element.50.grad_ref) | copy-start | bytes 3145732
  80.0 1.0 copy-start.2
  81.0 0.8 copy-start.4
  81.9 0.8 copy-start.6

commit v4 on v2

--- a/solution.py
+++ b/solution.py
@@ -30,7 +30,7 @@
 
 
 def grad_kernel(
-    flip_ref, pre_hbm, cot_hbm, grad_hbm, send_hbm, first_ref, last_ref, west_ref, east_ref,
+    flip_ref, pre_hbm, cot_hbm, grad_hbm, send_hbm, first_ref, last_ref, west_ref, east_ref, corner_ref,
     pre_ref, cot_ref, grad_ref, send_ref, rows_scr, chan_scr, in_sems, out_sems, *, group, q_count,
 ):
     rows, cols, channels = pre_ref.shape
@@ -81,6 +81,13 @@
     for row in range(REACH):
         first_ref[row * cols : (row + 1) * cols, :] = grad_ref[row]
         last_ref[row * cols : (row + 1) * cols, :] = grad_ref[rows - REACH + row]
+    corners = [
+        rows_scr[start + row, column : column + REACH, :]
+        for start in (0, rows - REACH)
+        for column in (0, cols - REACH)
+        for row in range(REACH)
+    ]
+    corner_ref[...] = jnp.concatenate(corners, axis=0).astype(BF16)
     for side in range(REACH):
         west_ref[side * rows : (side + 1) * rows, :] = rows_scr[:, side, :].astype(BF16)
         east_ref[side * rows : (side + 1) * rows, :] = rows_scr[:, cols - REACH + side, :].astype(BF16)
@@ -94,12 +101,13 @@
     q_count = rows // group
     send = (devices, channels // devices * q_count, LANES)
     edges = [(REACH * cols, channels)] * 2 + [(REACH * rows, channels)] * 2
+    edges += [(4 * REACH * REACH, channels)]
     anywhere = pl.BlockSpec(memory_space=pl.ANY)
     vmem = pl.BlockSpec(memory_space=pltpu.VMEM)
     return pl.pallas_call(
         functools.partial(grad_kernel, group=group, q_count=q_count),
         in_specs=[pl.BlockSpec(memory_space=pltpu.SMEM), anywhere, anywhere],
-        out_specs=[anywhere, anywhere] + [vmem] * 4,
+        out_specs=[anywhere, anywhere] + [vmem] * len(edges),
         out_shape=[jax.ShapeDtypeStruct(shape, BF16) for shape in (pre_act.shape, send, *edges)],
         scratch_shapes=[
             pltpu.VMEM(pre_act.shape, BF16),
@@ -187,7 +195,7 @@
         scratch_shapes=[pltpu.VMEM((block * (degrees + PAD), LANES), F32)],
         compiler_params=params(56 * MIB),
         cost_estimate=pl.CostEstimate(
-            flops=40 * orders * degrees * points,
+            flops=4000 * orders * degrees * points,
             bytes_accessed=4 * orders * degrees * points,
             transcendentals=0,
         ),
@@ -407,7 +415,7 @@
 
 
 def disco_kernel(
-    tap_ref, grad_ref, low_ref, high_ref, left_ref, right_ref, corner_ref, mix_ref, out_ref, padded, taps_scr
+    tap_ref, diagonal_ref, grad_ref, low_ref, high_ref, left_ref, right_ref, corner_ref, mix_ref, out_ref, padded, taps_scr
 ):
     step = pl.program_id(0)
     rows, cols, channels = grad_ref.shape
@@ -421,16 +429,17 @@
         for half in range(halves):
             lanes = slice(half * LANES, (half + 1) * LANES)
             padded[half, REACH : REACH + rows, origin : origin + cols, :] = grad_ref[:, :, lanes].astype(F32)
-            corners = corner_ref[:, lanes].astype(F32)
             for edge, (source, base) in enumerate(((low_ref, 0), (high_ref, REACH + rows))):
                 values = source[:, lanes].astype(F32)
                 for row in range(REACH):
                     padded[half, base + row, origin : origin + cols, :] = values[row * cols : (row + 1) * cols]
-                    for side in range(REACH):
-                        for end, column in enumerate((origin - REACH, origin + cols)):
-                            at = ((edge * 2 + end) * REACH + side) * REACH + row
-                            column = column + side
-                            padded[half, base + row, column : column + 1, :] = corners[at : at + 1]
+            for which in range(4):
+                block = corner_ref[diagonal_ref[which]][:, lanes].astype(F32)
+                base = (0, REACH + rows)[which // 2]
+                column = (origin - REACH, origin + cols)[which % 2]
+                for row in range(REACH):
+                    at = ((3 - which) * REACH + row) * REACH
+                    padded[half, base + row, column : column + REACH, :] = block[at : at + REACH]
             for source, column in ((left_ref, origin - REACH), (right_ref, origin + cols)):
                 values = source[:, lanes].astype(F32)
                 for side in range(REACH):
@@ -462,7 +471,7 @@
     out_ref[...] = total.reshape(rows_here, cols, channels)
 
 
-def disco(taps, grad, low, high, left, right, corners, mix):
+def disco(taps, diagonal, grad, low, high, left, right, corners, mix):
     rows, cols, channels = grad.shape
     kernels = mix.shape[0]
     steps = 4
@@ -473,7 +482,7 @@
     return pl.pallas_call(
         disco_kernel,
         grid=(steps,),
-        in_specs=[pl.BlockSpec(memory_space=pltpu.SMEM)]
+        in_specs=[pl.BlockSpec(memory_space=pltpu.SMEM)] * 2
         + [whole(value.shape) for value in (grad, low, high, left, right, corners, mix)],
         out_specs=pl.BlockSpec((rows // steps, cols, channels), lambda i: (i, 0, 0)),
         out_shape=jax.ShapeDtypeStruct(grad.shape, F32),
@@ -486,7 +495,7 @@
             flops=1000 * rows * cols * channels, bytes_accessed=8 * rows * cols * channels, transcendentals=0
         ),
         name="disco",
-    )(taps, grad, low, high, left, right, corners, mix)
+    )(taps, diagonal, grad, low, high, left, right, corners, mix)
 
 
 def combine_kernel(
@@ -554,38 +563,9 @@
     )(flip, back, local_part)
 
 
-def shifted(block, lat_step, lon_step):
-    lat_count = lax.axis_size("lat")
-    lon_count = lax.axis_size("lon")
-    pairs = [
-        (
-            lat * lon_count + lon,
-            (lat + lat_step) % lat_count * lon_count + (lon + lon_step) % lon_count,
-        )
-        for lat in range(lat_count)
-        for lon in range(lon_count)
-    ]
-    return lax.ppermute(block, ("lat", "lon"), pairs)
-
-
-def halos(first_rows, last_rows, west, east):
-    channels = west.shape[-1]
-
-    def corner(side, start):
-        block = side.reshape(REACH, -1, channels)[:, start:][:, :REACH]
-        return block.reshape(REACH * REACH, channels)
-
-    low = shifted(last_rows, 1, 0)
-    high = shifted(first_rows, -1, 0)
-    left = shifted(east, 0, 1)
-    right = shifted(west, 0, -1)
-    corners = [
-        shifted(corner(east, -REACH), 1, 1),
-        shifted(corner(west, -REACH), 1, -1),
-        shifted(corner(east, 0), -1, 1),
-        shifted(corner(west, 0), -1, -1),
-    ]
-    return (low, high, left, right, jnp.concatenate(corners, axis=0))
+def shifted(block, axis, step):
+    count = lax.axis_size(axis)
+    return lax.ppermute(block, axis, [(i, (i + step) % count) for i in range(count)])
 
 
 def fourier_tables(order_count, points):
@@ -645,14 +625,27 @@
     tap_coef = lax.dynamic_slice_in_dim(tap_coef, band_index * lat_rows, lat_rows + 2 * REACH, 1)
     taps = jnp.transpose(tap_coef, (1, 0, 2, 3)).reshape(lat_rows + 2 * REACH, -1)
 
-    received, rim = lax.optimization_barrier((received, halos(*edges)))
+    everyone = lax.all_gather(edges.pop(), ("lat", "lon"))
+    edges, tables = lax.optimization_barrier((edges, tables))
+    first_rows, last_rows, west, east = edges
+    sides = (
+        shifted(last_rows, "lat", 1),
+        shifted(first_rows, "lat", -1),
+        shifted(east, "lon", 1),
+        shifted(west, "lon", -1),
+    )
+    received, sides, everyone = lax.optimization_barrier((received, sides, everyone))
+    lat_steps = np.array([-1, -1, 1, 1])
+    lon_steps = np.array([-1, 1, -1, 1])
+    diagonal = (band_index + lat_steps) % lat_count * lon_count
+    diagonal = diagonal + (lax.axis_index("lon") + lon_steps) % lon_count
     blocks = received.reshape(lat_count, lon_count, local * q_count, LANES)
     back = spectral(blocks, forward, inverse, tables, weights, quad, group)
     back, taps = lax.optimization_barrier((back, taps))
     returned = lax.all_to_all(
         back.reshape(devices, local * q_count, LANES), ("lat", "lon"), 0, 0, tiled=True
     )
-    local_part = disco(taps, grad_pre, *rim, disco_weight)
+    local_part = disco(taps, diagonal, grad_pre, *sides, everyone, disco_weight)
     return combine(returned, local_part, flip, group)
 
 

time: 91.2 us -> 143 us (1.57)
  blocking collectives: 0 us -> 71.9 us
  waiting for transfers between devices: 18 us -> 6.83 us
  starting transfers between devices: 24.9 us -> 16.5 us
    all_gather x0 -> x1, blocking collectives: none -> 71.9 us  [shards(): everyone = lax.all_gather(edges.pop(), ('lat', 'lon'))]
    ppermute x8 -> x4, starting transfers between devices: 19.2 us -> 6.47 us  [shifted(): lax.ppermute(block, axis, [(i, (i + step) % count) for i in range(count)])]
    all_to_all x1, waiting for transfers between devices: 8.38 us -> 0.01 us  [shards(): received = lax.all_to_all(to_send, ('lat', 'lon'), 0, 0, tiled=True)]
    all_to_all x1, starting transfers between devices: 2.64 us -> 7.38 us  [shards(): received = lax.all_to_all(to_send, ('lat', 'lon'), 0, 0, tiled=True)]
    ppermute x8 -> x4, waiting for transfers between devices: 1.82 us -> 0.01 us  [shifted(): lax.ppermute(block, axis, [(i, (i + step) % count) for i in range(count)])]
    slice x2 -> x0, local copies, waits for them, and re-layouts: 1.46 us -> none  [corner(): block = side.reshape(REACH, -1, channels)[:, start:][:, :REACH]]
    unnamed x29 -> x39, local copies, waits for them, and re-layouts: 3.92 us -> 4.9 us
  transfers between devices with their start and end apart: 10 -> 6, of which waited for: 3 -> 1; matrix products, arithmetic and copies ran while one was open for 5% -> 2% of each run, Pallas kernels for 27% -> 17%
where the time goes in v4:
time: 143 us
  blocking collectives  71.9 us (50%)
  Pallas kernels  39.6 us (28%)
  starting transfers between devices  16.5 us (12%)
  waiting for transfers between devices  6.83 us (5%)
  local copies, waits for them, and re-layouts  5.34 us (4%)
  other arithmetic  2.17 us (2%)
    all_gather x1, blocking collectives, shards(): everyone = lax.all_gather(edges.pop(), ('lat', 'lon'))  71.9 us
    pallas_call x1, Pallas kernels, disco(): pl.pallas_call(disco_kernel, grid=(steps,), in_specs=[pl.BlockSpec(memory...  15.8 us
    pallas_call x1, Pallas kernels, legendre(): pl.pallas_call(functools.partial(legendre_kernel, degrees=degrees, span=8...  8.44 us
    pallas_call x1, Pallas kernels, spectral(): pl.pallas_call(functools.partial(spectral_kernel, group=group, q_count=q_...  7.73 us
    all_to_all x1, starting transfers between devices, shards(): received = lax.all_to_all(to_send, ('lat', 'lon'), 0, 0, tiled=True)  7.38 us
    all_to_all x1, waiting for transfers between devices, shards(): lax.all_to_all(back.reshape(devices, local * q_count, LANES), ('lat', 'lo...  6.81 us
    ppermute x4, starting transfers between devices, shifted(): lax.ppermute(block, axis, [(i, (i + step) % count) for i in range(count)])  6.47 us
    pallas_call x1, Pallas kernels, gradient(): pl.pallas_call(functools.partial(grad_kernel, group=group, q_count=q_coun...  5.28 us
  transfers between devices with their start and end apart: 6, of which 1 were waited for; matrix products, arithmetic and copies ran while one was open for 2% of the time, Pallas kernels for 17%

profile of v4, /device:TPU:0, one launch (start us, length us, event | category | flops | bytes accessed | tf_op | source)
XLA Modules:
  0.0 142.6 jit_solution(18366303959690315020)
XLA Ops:
  0.0 0.0 copy-start
  0.0 0.0 copy-start.12
  0.0 5.3 %gradient.1 = (bf16[64,32,256]{2,1,0:T(8,128)(2,1)}, bf16[32,128,128]{2,1,0:T(8,128)(2,1)}, bf16[64,256]{1,0:T(8,128)(2,1)}, bf16[64,256]{1,0:T(8,128)(2,1)}, bf...) custom-call(s32[1]{0:T(128)} %bitcast.flip_ref, bf16[64,32,256]{2,1,0:T(8,128)(2,1)} %pre_hbm.1, ...), custom_call_target="tpu_custom_call" | custom-call | tf_op jit(solution)/shard_map/gradient/pallas_call | solution.py:107
  5.3 7.4 %all-to-all-start = ((bf16[32,128,128]{2,1,0:T(8,128)(2,1)}), bf16[32,128,128]{2,1,0:T(8,128)(2,1)S(1)}, u32[]{:S(2)}, u32[]{:S(2)}) async-start(bf16[32,128,128]{2,1,0:T(8,128)(2,1)} %get-tuple-element.28), calls=%async_computation | async-start | bytes 2097152 | tf_op jit(solution)/shard_map/all_to_all | solution.py:597
  12.7 0.1 fusion.25
  12.8 0.6 pad_maximum_fusion.1.norm_ref
  13.4 0.0 copy-done.12
  13.4 0.7 multiply_add_fusion.start_ref
  14.1 0.0 copy-start.16
  14.1 0.0 copy-start.15
  14.1 0.0 copy-start.18
  14.1 0.0 copy-start.17
  14.1 0.0 copy-start.11
  14.1 0.0 copy-start.10
  14.1 0.0 copy-start.9
  14.1 0.0 copy-start.8
  14.1 8.4 %legendre.1 = (bf16[128,128,128]{2,1,0:T(8,128)(2,1)}, bf16[128,128,128]{2,1,0:T(8,128)(2,1)}) custom-call(f32[2,128]{1,0:T(2,128)} %pad_maximum_fusion.1.norm_ref, f32[1,128]{1,0:T(1,128)} %constant.147.cos_ref, f32[128,128]{1,0:T(8,128)} %multiply_add_fusion.start_ref), custom_call_target="tpu_custom_call" | custom-call | flops 8388608000 | bytes 8388608 | tf_op jit(solution)/shard_map/legendre/pallas_call | solution.py:179
  22.6 0.0 copy-done.16
  22.6 1.8 %collective-permute-start.2 = (bf16[128,256]{1,0:T(8,128)(2,1)S(1)}, bf16[128,256]{1,0:T(8,128)(2,1)S(1)}, u32[]{:S(2)}, u32[]{:S(2)}) collective-permute-start(bf16[128,256]{1,0:T(8,128)(2,1)S(1)} %copy-done.16), channel_id=1, source_target_pairs={{0,1},{1,2},{2,3},{3,4},{4,5},{5,6},{6,7},{7,0},{8,9},{9,10},{10,1... | collective-permute-start | bytes 196616 | tf_op jit(solution)/shard_map/ppermute | solution.py:568
  24.4 0.0 copy-done.15
  24.4 3.0 %collective-permute-start.3 = (bf16[128,256]{1,0:T(8,128)(2,1)S(1)}, bf16[128,256]{1,0:T(8,128)(2,1)S(1)}, u32[]{:S(2)}, u32[]{:S(2)}) collective-permute-start(bf16[128,256]{1,0:T(8,128)(2,1)S(1)} %copy-done.15), channel_id=1, source_target_pairs={{0,7},{1,0},{2,1},{3,2},{4,3},{5,4},{6,5},{7,6},{8,15},{9,8},{10,9... | collective-permute-start | bytes 196616 | tf_op jit(solution)/shard_map/ppermute | solution.py:568
  27.3 0.0 copy-done.18
  27.3 0.0 collective-permute-start
  27.3 0.0 copy-done.17
  27.3 1.7 %collective-permute-start.1 = (bf16[64,256]{1,0:T(8,128)(2,1)S(1)}, bf16[64,256]{1,0:T(8,128)(2,1)S(1)}, u32[]{:S(2)}, u32[]{:S(2)}) collective-permute-start(bf16[64,256]{1,0:T(8,128)(2,1)S(1)} %copy-done.17), channel_id=1, source_target_pairs={{0,24},{8,0},{16,8},{24,16},{1,25},{9,1},{17,9},{25,17},{2,26},{10... | collective-permute-start | bytes 98312 | tf_op jit(solution)/shard_map/ppermute | solution.py:568
  29.1 0.0 copy-done
  29.1 0.2 constant_dynamic-slice_fusion
  29.3 0.5 sine_negate_fusion
  29.9 0.0 copy-done.11
  29.9 71.9 %all-gather = bf16[512,256]{1,0:T(8,128)(2,1)} all-gather(bf16[16,256]{1,0:T(8,128)(2,1)S(1)} %copy-done.11), channel_id=2, replica_groups=mesh['lat'=4,'lon'=8] {'lat','lon'}, dimensions={0}, use_global_device_ids=true | all-gather | bytes 270336 | tf_op jit(solution)/shard_map/all_gather | solution.py:628
  101.8 0.0 copy-done.10
  101.8 0.1 compare_convert_fusion
  101.9 0.1 multiply_convert_fusion.forward_ref
  102.0 0.0 copy-done.9
  102.0 0.1 fusion.8
  102.1 0.1 copy.15
  102.2 0.0 collective-permute-done.low_ref
  102.2 0.0 collective-permute-done.1.high_ref
  102.3 0.0 copy-start.6
  102.3 0.0 collective-permute-done.2.left_ref
  102.3 0.0 collective-permute-done.3.right_ref
  102.3 0.0 copy-start.4
  102.3 0.0 all-to-all-done
  102.3 0.0 copy-done.8
  102.3 0.0 copy-start.13
  102.3 0.0 copy-start.14
  102.3 7.7 %spectral.1 = bf16[4,8,128,128]{3,2,1,0:T(8,128)(2,1)} custom-call(bf16[4,8,128,128]{3,2,1,0:T(8,128)(2,1)S(1)} %bitcast.10, bf16[256,256]{1,0:T(8,128)(2,1)S(1)} %multiply_convert_fusion.forward_ref, bf16[256,256]{1,0:T(8,128)(2,1)S(1)} %fusion.inverse_ref, f32[2,8,128]{2,1,0:T(8,128)S(1)} %bitcast.12, f32[1,128]{1,0:T(1,128)S(1)} %copy-done.8, ...), custom_call_target="tpu_custom_call" | custom-call | tf_op jit(solution)/shard_map/spectral/pallas_call | solution.py:390
  110.1 0.0 copy-done.6
  110.1 0.0 copy-done.4
  110.1 2.7 %all-to-all-start.1 = ((bf16[32,128,128]{2,1,0:T(8,128)(2,1)}), bf16[32,128,128]{2,1,0:T(8,128)(2,1)S(1)}, u32[]{:S(2)}, u32[]{:S(2)}) async-start(bf16[32,128,128]{2,1,0:T(8,128)(2,1)} %bitcast.6), calls=%async_computation.1 | async-start | bytes 2097152 | tf_op jit(solution)/shard_map/all_to_all | solution.py:645
  112.8 0.0 copy-done.13
  112.8 0.0 copy-done.14
  112.8 0.1 copy.14.tap_ref
  112.9 0.0 copy-start.1
  112.9 1.2 copy-done.1
  114.1 0.0 copy-start.2
  114.1 0.9 copy-done.2
  115.1 0.0 copy-start.3
  115.1 1.0 copy-done.3
  116.1 0.8 copy-done.5
  116.9 0.8 copy-done.7
  117.7 15.8 %disco.1.disco_ref = f32[64,32,256]{2,1,0:T(8,128)S(1)} custom-call(f32[68,75]{1,0:T(8,128)S(1)} %copy.14.tap_ref, s32[4]{0:T(128)S(1)} %fusion.12.diagonal_ref, bf16[64,32,256]{2,1,0:T(8,128)(2,1)S(1)} %copy-done.1, bf16[64,256]{1,0:T(8,128)(2,1)S(1)} %collective-permute-done.low_ref, bf16[64,256]{1,0:T(8,128)(2,1)S(1)} %copy-done.7, ...), custom_call_target="tpu_custom_call" | custom-call | flops 524288000 | bytes 4194304 | tf_op jit(solution)/shard_map/disco/pallas_call | solution.py:482
  133.5 6.8 %all-to-all-done.1.back_hbm = bf16[32,128,128]{2,1,0:T(8,128)(2,1)S(1)} async-done(((bf16[32,128,128]{2,1,0:T(8,128)(2,1)}), bf16[32,128,128]{2,1,0:T(8,128)(2,1)S(1)}, u32[]{:S(2)}, u32[]{:S(2)}) %all-to-all-start.1) | async-done | bytes 1048608 | tf_op jit(solution)/shard_map/all_to_all | solution.py:645
  140.4 2.3 %combine.1 = bf16[64,32,256]{2,1,0:T(8,128)(2,1)} custom-call(s32[1]{0:T(128)} %bitcast.flip_ref, bf16[32,128,128]{2,1,0:T(8,128)(2,1)S(1)} %all-to-all-done.1.back_hbm, f32[64,32,256]{2,1,0:T(8,128)S(1)} %disco.1.disco_ref), custom_call_target="tpu_custom_call" | custom-call | tf_op jit(solution)/shard_map/combine/pallas_call | solution.py:545
  (11 shorter events, 0.1 us)
Async XLA Ops:
  0.0 29.1 %copy-start = (f32[128,2,256]{2,1,0:T(2,128)S(1)}, f32[128,2,256]{2,1,0:T(2,128)}, u32[]{:S(2)}) copy-start(f32[128,2,256]{2,1,0:T(2,128)} %param.11) | copy-start | bytes 786436
  0.0 13.4 %copy-start.12 = (f32[128]{0:T(128)S(1)}, f32[128]{0:T(128)}, u32[]{:S(2)}) copy-start(f32[128]{0:T(128)} %constant.149) | copy-start | bytes 1540
  5.3 97.0 %all-to-all-start = ((bf16[32,128,128]{2,1,0:T(8,128)(2,1)}), bf16[32,128,128]{2,1,0:T(8,128)(2,1)S(1)}, u32[]{:S(2)}, u32[]{:S(2)}) async-start(bf16[32,128,128]{2,1,0:T(8,128)(2,1)} %get-tuple-element.28), calls=%async_computation | async-start | bytes 2097152 | tf_op jit(solution)/shard_map/all_to_all | solution.py:597
  14.1 8.5 %copy-start.16 = (bf16[128,256]{1,0:T(8,128)(2,1)S(1)}, bf16[128,256]{1,0:T(8,128)(2,1)}, u32[]{:S(2)}) copy-start(bf16[128,256]{1,0:T(8,128)(2,1)} %get-tuple-element.37) | copy-start | bytes 196612
  14.1 10.3 %copy-start.15 = (bf16[128,256]{1,0:T(8,128)(2,1)S(1)}, bf16[128,256]{1,0:T(8,128)(2,1)}, u32[]{:S(2)}) copy-start(bf16[128,256]{1,0:T(8,128)(2,1)} %get-tuple-element.38) | copy-start | bytes 196612
  14.1 13.2 %copy-start.18 = (bf16[64,256]{1,0:T(8,128)(2,1)S(1)}, bf16[64,256]{1,0:T(8,128)(2,1)}, u32[]{:S(2)}) copy-start(bf16[64,256]{1,0:T(8,128)(2,1)} %get-tuple-element.35) | copy-start | bytes 98308
  14.1 13.2 %copy-start.17 = (bf16[64,256]{1,0:T(8,128)(2,1)S(1)}, bf16[64,256]{1,0:T(8,128)(2,1)}, u32[]{:S(2)}) copy-start(bf16[64,256]{1,0:T(8,128)(2,1)} %get-tuple-element.36) | copy-start | bytes 98308
  14.1 15.8 %copy-start.11 = (bf16[16,256]{1,0:T(8,128)(2,1)S(1)}, bf16[16,256]{1,0:T(8,128)(2,1)}, u32[]{:S(2)}) copy-start(bf16[16,256]{1,0:T(8,128)(2,1)} %get-tuple-element.39) | copy-start | bytes 24580
  14.1 87.7 %copy-start.10 = (s32[256,5]{0,1:T(8,128)S(1)}, s32[256,5]{0,1:T(8,128)}, u32[]{:S(2)}) copy-start(s32[256,5]{0,1:T(8,128)} %param.14) | copy-start | bytes 15364
  14.1 87.9 %copy-start.9 = (f32[3,256,5,5]{1,0,3,2:T(4,128)S(1)}, f32[3,256,5,5]{1,0,3,2:T(4,128)}, u32[]{:S(2)}) copy-start(f32[3,256,5,5]{1,0,3,2:T(4,128)} %param.13) | copy-start | bytes 230404
  14.1 88.2 %copy-start.8 = (f32[1,128]{1,0:T(1,128)S(1)}, f32[1,128]{1,0:T(1,128)}, u32[]{:S(2)}) copy-start(f32[1,128]{1,0:T(1,128)} %constant.151.quad_ref) | copy-start | bytes 1540
  22.6 79.7 %collective-permute-start.2 = (bf16[128,256]{1,0:T(8,128)(2,1)S(1)}, bf16[128,256]{1,0:T(8,128)(2,1)S(1)}, u32[]{:S(2)}, u32[]{:S(2)}) collective-permute-start(bf16[128,256]{1,0:T(8,128)(2,1)S(1)} %copy-done.16), channel_id=1, source_target_pairs={{0,1},{1,2},{2,3},{3,4},{4,5},{5,6},{6,7},{7,0},{8,9},{9,10},{10,1... | collective-permute-start | bytes 196616 | tf_op jit(solution)/shard_map/ppermute | solution.py:568
  24.4 77.9 %collective-permute-start.3 = (bf16[128,256]{1,0:T(8,128)(2,1)S(1)}, bf16[128,256]{1,0:T(8,128)(2,1)S(1)}, u32[]{:S(2)}, u32[]{:S(2)}) collective-permute-start(bf16[128,256]{1,0:T(8,128)(2,1)S(1)} %copy-done.15), channel_id=1, source_target_pairs={{0,7},{1,0},{2,1},{3,2},{4,3},{5,4},{6,5},{7,6},{8,15},{9,8},{10,9... | collective-permute-start | bytes 196616 | tf_op jit(solution)/shard_map/ppermute | solution.py:568
  27.3 74.9 %collective-permute-start = (bf16[64,256]{1,0:T(8,128)(2,1)S(1)}, bf16[64,256]{1,0:T(8,128)(2,1)S(1)}, u32[]{:S(2)}, u32[]{:S(2)}) collective-permute-start(bf16[64,256]{1,0:T(8,128)(2,1)S(1)} %copy-done.18), channel_id=1, source_target_pairs={{0,8},{8,16},{16,24},{24,0},{1,9},{9,17},{17,25},{25,1},{2,10},{10... | collective-permute-start | bytes 98312 | tf_op jit(solution)/shard_map/ppermute | solution.py:568
  27.3 74.9 %collective-permute-start.1 = (bf16[64,256]{1,0:T(8,128)(2,1)S(1)}, bf16[64,256]{1,0:T(8,128)(2,1)S(1)}, u32[]{:S(2)}, u32[]{:S(2)}) collective-permute-start(bf16[64,256]{1,0:T(8,128)(2,1)S(1)} %copy-done.17), channel_id=1, source_target_pairs={{0,24},{8,0},{16,8},{24,16},{1,25},{9,1},{17,9},{25,17},{2,26},{10... | collective-permute-start | bytes 98312 | tf_op jit(solution)/shard_map/ppermute | solution.py:568
  102.3 7.8 %copy-start.6 = (bf16[64,256]{1,0:T(8,128)(2,1)}, bf16[64,256]{1,0:T(8,128)(2,1)S(1)}, u32[]{:S(2)}) copy-start(bf16[64,256]{1,0:T(8,128)(2,1)S(1)} %collective-permute-done.1.high_ref) | copy-start | bytes 98308
  102.3 7.8 %copy-start.4 = (bf16[128,256]{1,0:T(8,128)(2,1)}, bf16[128,256]{1,0:T(8,128)(2,1)S(1)}, u32[]{:S(2)}) copy-start(bf16[128,256]{1,0:T(8,128)(2,1)S(1)} %collective-permute-done.3.right_ref) | copy-start | bytes 196612
  102.3 10.5 %copy-start.13 = (s32[4]{0:T(128)S(1)}, s32[4]{0:T(128)}, u32[]{:S(2)}) copy-start(s32[4]{0:T(128)} %constant.140.clone) | copy-start | bytes 52
  102.3 10.5 %copy-start.14 = (s32[4]{0:T(128)S(1)}, s32[4]{0:T(128)}, u32[]{:S(2)}) copy-start(s32[4]{0:T(128)} %constant.141.clone) | copy-start | bytes 52
  110.1 30.3 %all-to-all-start.1 = ((bf16[32,128,128]{2,1,0:T(8,128)(2,1)}), bf16[32,128,128]{2,1,0:T(8,128)(2,1)S(1)}, u32[]{:S(2)}, u32[]{:S(2)}) async-start(bf16[32,128,128]{2,1,0:T(8,128)(2,1)} %bitcast.6), calls=%async_computation.1 | async-start | bytes 2097152 | tf_op jit(solution)/shard_map/all_to_all | solution.py:645
  112.9 1.2 copy-start.1
  114.1 0.9 copy-start.2
  115.1 1.0 copy-start.3
  116.1 0.8 copy-start.5
  116.9 0.8 copy-start.7

commit v5 on v4

--- a/solution.py
+++ b/solution.py
@@ -30,7 +30,7 @@
 
 
 def grad_kernel(
-    flip_ref, pre_hbm, cot_hbm, grad_hbm, send_hbm, first_ref, last_ref, west_ref, east_ref, corner_ref,
+    flip_ref, pre_hbm, cot_hbm, grad_hbm, send_hbm, first_ref, last_ref, west_ref, east_ref,
     pre_ref, cot_ref, grad_ref, send_ref, rows_scr, chan_scr, in_sems, out_sems, *, group, q_count,
 ):
     rows, cols, channels = pre_ref.shape
@@ -81,13 +81,6 @@
     for row in range(REACH):
         first_ref[row * cols : (row + 1) * cols, :] = grad_ref[row]
         last_ref[row * cols : (row + 1) * cols, :] = grad_ref[rows - REACH + row]
-    corners = [
-        rows_scr[start + row, column : column + REACH, :]
-        for start in (0, rows - REACH)
-        for column in (0, cols - REACH)
-        for row in range(REACH)
-    ]
-    corner_ref[...] = jnp.concatenate(corners, axis=0).astype(BF16)
     for side in range(REACH):
         west_ref[side * rows : (side + 1) * rows, :] = rows_scr[:, side, :].astype(BF16)
         east_ref[side * rows : (side + 1) * rows, :] = rows_scr[:, cols - REACH + side, :].astype(BF16)
@@ -101,7 +94,6 @@
     q_count = rows // group
     send = (devices, channels // devices * q_count, LANES)
     edges = [(REACH * cols, channels)] * 2 + [(REACH * rows, channels)] * 2
-    edges += [(4 * REACH * REACH, channels)]
     anywhere = pl.BlockSpec(memory_space=pl.ANY)
     vmem = pl.BlockSpec(memory_space=pltpu.VMEM)
     return pl.pallas_call(
@@ -410,12 +402,15 @@
             pltpu.SemaphoreType.DMA((local,)),
         ],
         compiler_params=params(50 * MIB),
+        cost_estimate=pl.CostEstimate(
+            flops=2**33 * orders // 128, bytes_accessed=4 * orders * degrees * half, transcendentals=0
+        ),
         name="spectral",
     )(received, forward, inverse, weights, quad, *tables)
 
 
 def disco_kernel(
-    tap_ref, diagonal_ref, grad_ref, low_ref, high_ref, left_ref, right_ref, corner_ref, mix_ref, out_ref, padded, taps_scr
+    tap_ref, grad_ref, low_ref, high_ref, left_ref, right_ref, corner_ref, mix_ref, out_ref, padded, taps_scr
 ):
     step = pl.program_id(0)
     rows, cols, channels = grad_ref.shape
@@ -434,12 +429,12 @@
                 for row in range(REACH):
                     padded[half, base + row, origin : origin + cols, :] = values[row * cols : (row + 1) * cols]
             for which in range(4):
-                block = corner_ref[diagonal_ref[which]][:, lanes].astype(F32)
-                base = (0, REACH + rows)[which // 2]
-                column = (origin - REACH, origin + cols)[which % 2]
+                values = corner_ref[:, lanes].astype(F32)
+                base = (0, REACH + rows)[which % 2]
+                column = (origin - REACH, origin + cols)[which // 2]
                 for row in range(REACH):
-                    at = ((3 - which) * REACH + row) * REACH
-                    padded[half, base + row, column : column + REACH, :] = block[at : at + REACH]
+                    at = (which * REACH + row) * REACH
+                    padded[half, base + row, column : column + REACH, :] = values[at : at + REACH]
             for source, column in ((left_ref, origin - REACH), (right_ref, origin + cols)):
                 values = source[:, lanes].astype(F32)
                 for side in range(REACH):
@@ -471,7 +466,7 @@
     out_ref[...] = total.reshape(rows_here, cols, channels)
 
 
-def disco(taps, diagonal, grad, low, high, left, right, corners, mix):
+def disco(taps, grad, low, high, left, right, corners, mix):
     rows, cols, channels = grad.shape
     kernels = mix.shape[0]
     steps = 4
@@ -482,7 +477,7 @@
     return pl.pallas_call(
         disco_kernel,
         grid=(steps,),
-        in_specs=[pl.BlockSpec(memory_space=pltpu.SMEM)] * 2
+        in_specs=[pl.BlockSpec(memory_space=pltpu.SMEM)]
         + [whole(value.shape) for value in (grad, low, high, left, right, corners, mix)],
         out_specs=pl.BlockSpec((rows // steps, cols, channels), lambda i: (i, 0, 0)),
         out_shape=jax.ShapeDtypeStruct(grad.shape, F32),
@@ -495,7 +490,7 @@
             flops=1000 * rows * cols * channels, bytes_accessed=8 * rows * cols * channels, transcendentals=0
         ),
         name="disco",
-    )(taps, diagonal, grad, low, high, left, right, corners, mix)
+    )(taps, grad, low, high, left, right, corners, mix)
 
 
 def combine_kernel(
@@ -566,6 +561,14 @@
 def shifted(block, axis, step):
     count = lax.axis_size(axis)
     return lax.ppermute(block, axis, [(i, (i + step) % count) for i in range(count)])
+
+
+def corners_of(low, high, channels):
+    def ends(start):
+        blocks = [side.reshape(REACH, -1, channels)[:, start:][:, :REACH] for side in (low, high)]
+        return jnp.concatenate(blocks, axis=0).reshape(2 * REACH * REACH, channels)
+
+    return jnp.concatenate([shifted(ends(-REACH), "lon", 1), shifted(ends(0), "lon", -1)], axis=0)
 
 
 def fourier_tables(order_count, points):
@@ -625,7 +628,6 @@
     tap_coef = lax.dynamic_slice_in_dim(tap_coef, band_index * lat_rows, lat_rows + 2 * REACH, 1)
     taps = jnp.transpose(tap_coef, (1, 0, 2, 3)).reshape(lat_rows + 2 * REACH, -1)
 
-    everyone = lax.all_gather(edges.pop(), ("lat", "lon"))
     edges, tables = lax.optimization_barrier((edges, tables))
     first_rows, last_rows, west, east = edges
     sides = (
@@ -634,18 +636,15 @@
         shifted(east, "lon", 1),
         shifted(west, "lon", -1),
     )
-    received, sides, everyone = lax.optimization_barrier((received, sides, everyone))
-    lat_steps = np.array([-1, -1, 1, 1])
-    lon_steps = np.array([-1, 1, -1, 1])
-    diagonal = (band_index + lat_steps) % lat_count * lon_count
-    diagonal = diagonal + (lax.axis_index("lon") + lon_steps) % lon_count
+    corners = corners_of(sides[0], sides[1], channels)
+    received, sides = lax.optimization_barrier((received, sides))
     blocks = received.reshape(lat_count, lon_count, local * q_count, LANES)
     back = spectral(blocks, forward, inverse, tables, weights, quad, group)
-    back, taps = lax.optimization_barrier((back, taps))
+    back, taps, corners = lax.optimization_barrier((back, taps, corners))
     returned = lax.all_to_all(
         back.reshape(devices, local * q_count, LANES), ("lat", "lon"), 0, 0, tiled=True
     )
-    local_part = disco(taps, diagonal, grad_pre, *sides, everyone, disco_weight)
+    local_part = disco(taps, grad_pre, *sides, corners, disco_weight)
     return combine(returned, local_part, flip, group)
 
 

time: 143 us -> 82.5 us (0.58)
  blocking collectives: 71.9 us -> 0 us
  waiting for transfers between devices: 6.83 us -> 17 us
  starting transfers between devices: 16.5 us -> 18.6 us
    all_gather x1 -> x0, blocking collectives: 71.9 us -> none  [shards(): everyone = lax.all_gather(edges.pop(), ('lat', 'lon'))]
    ppermute x4 -> x6, waiting for transfers between devices: 0.01 us -> 6.04 us  [shifted(): lax.ppermute(block, axis, [(i, (i + step) % count) for i in range(count)])]
    all_to_all x1, waiting for transfers between devices: 0.01 us -> 3.15 us  [shards(): received = lax.all_to_all(to_send, ('lat', 'lon'), 0, 0, tiled=True)]
    ppermute x4 -> x6, starting transfers between devices: 6.47 us -> 8.6 us  [shifted(): lax.ppermute(block, axis, [(i, (i + step) % count) for i in range(count)])]
    unnamed x39 -> x31, local copies, waits for them, and re-layouts: 4.9 us -> 3.93 us
  transfers between devices with their start and end apart: 6 -> 8, of which waited for: 1 -> 4; matrix products, arithmetic and copies ran while one was open for 2% -> 3% of each run, Pallas kernels for 17% -> 30%
where the time goes in v5:
time: 82.5 us; the launch traced here: 82 us
  Pallas kernels  39.5 us (48%)
  starting transfers between devices  18.6 us (23%)
  waiting for transfers between devices  17 us (21%)
  local copies, waits for them, and re-layouts  4.4 us (5%)
  other arithmetic  2.2 us (3%)
    pallas_call x1, Pallas kernels, disco(): pl.pallas_call(disco_kernel, grid=(steps,), in_specs=[pl.BlockSpec(memory...  15.8 us
    ppermute x6, starting transfers between devices, shifted(): lax.ppermute(block, axis, [(i, (i + step) % count) for i in range(count)])  8.6 us
    pallas_call x1, Pallas kernels, legendre(): pl.pallas_call(functools.partial(legendre_kernel, degrees=degrees, span=8...  8.44 us
    all_to_all x1, waiting for transfers between devices, shards(): lax.all_to_all(back.reshape(devices, local * q_count, LANES), ('lat', 'lo...  7.84 us
    pallas_call x1, Pallas kernels, spectral(): pl.pallas_call(functools.partial(spectral_kernel, group=group, q_count=q_...  7.71 us
    all_to_all x1, starting transfers between devices, shards(): received = lax.all_to_all(to_send, ('lat', 'lon'), 0, 0, tiled=True)  7.38 us
    ppermute x6, waiting for transfers between devices, shifted(): lax.ppermute(block, axis, [(i, (i + step) % count) for i in range(count)])  6.04 us
    pallas_call x1, Pallas kernels, gradient(): pl.pallas_call(functools.partial(grad_kernel, group=group, q_count=q_coun...  5.25 us
  transfers between devices with their start and end apart: 8, of which 4 were waited for; matrix products, arithmetic and copies ran while one was open for 3% of the time, Pallas kernels for 30%

profile of v5, /device:TPU:0, one launch (start us, length us, event | category | flops | bytes accessed | tf_op | source)
XLA Modules:
  0.0 82.0 jit_solution(17180418944220991535)
XLA Ops:
  0.0 0.0 copy-start
  0.0 0.0 copy-start.10
  0.0 5.2 %gradient.1 = (bf16[64,32,256]{2,1,0:T(8,128)(2,1)}, bf16[32,128,128]{2,1,0:T(8,128)(2,1)}, bf16[64,256]{1,0:T(8,128)(2,1)}, bf16[64,256]{1,0:T(8,128)(2,1)}, bf...) custom-call(s32[1]{0:T(128)} %bitcast.flip_ref, bf16[64,32,256]{2,1,0:T(8,128)(2,1)} %pre_hbm.1, bf16[64,32,256]{2,1,0:T(8,128)(2,1)} %cot_hbm.1), custom_call_target="tpu_custom_call" | custom-call | tf_op jit(solution)/shard_map/gradient/pallas_call | solution.py:99
  5.3 7.4 %all-to-all-start = ((bf16[32,128,128]{2,1,0:T(8,128)(2,1)}), bf16[32,128,128]{2,1,0:T(8,128)(2,1)S(1)}, u32[]{:S(2)}, u32[]{:S(2)}) async-start(bf16[32,128,128]{2,1,0:T(8,128)(2,1)} %get-tuple-element.27), calls=%async_computation | async-start | bytes 2097152 | tf_op jit(solution)/shard_map/all_to_all | solution.py:600
  12.7 0.1 fusion.21
  12.7 0.6 pad_maximum_fusion.4.norm_ref
  13.4 0.0 copy-done.10
  13.4 0.7 multiply_add_fusion.start_ref
  14.1 0.0 copy-start.13
  14.1 0.0 copy-start.14
  14.1 0.0 copy-start.12
  14.1 0.0 copy-start.11
  14.1 0.0 copy-start.9
  14.1 0.0 copy-start.8
  14.1 0.0 copy-start.7
  14.1 8.4 %legendre.1 = (bf16[128,128,128]{2,1,0:T(8,128)(2,1)}, bf16[128,128,128]{2,1,0:T(8,128)(2,1)}) custom-call(f32[2,128]{1,0:T(2,128)} %pad_maximum_fusion.4.norm_ref, f32[1,128]{1,0:T(1,128)} %constant.119.cos_ref, f32[128,128]{1,0:T(8,128)} %multiply_add_fusion.start_ref), custom_call_target="tpu_custom_call" | custom-call | flops 8388608000 | bytes 8388608 | tf_op jit(solution)/shard_map/legendre/pallas_call | solution.py:171
  22.6 0.0 copy-done.13
  22.6 0.3 collective-permute-start
  22.8 0.0 copy-done.14
  22.8 1.5 %collective-permute-start.1 = (bf16[64,256]{1,0:T(8,128)(2,1)S(1)}, bf16[64,256]{1,0:T(8,128)(2,1)S(1)}, u32[]{:S(2)}, u32[]{:S(2)}) collective-permute-start(bf16[64,256]{1,0:T(8,128)(2,1)S(1)} %copy-done.14), channel_id=1, source_target_pairs={{0,24},{8,0},{16,8},{24,16},{1,25},{9,1},{17,9},{25,17},{2,26},{10... | collective-permute-start | bytes 98312 | tf_op jit(solution)/shard_map/ppermute | solution.py:563
  24.3 0.0 copy-done.12
  24.3 1.8 %collective-permute-start.2 = (bf16[128,256]{1,0:T(8,128)(2,1)S(1)}, bf16[128,256]{1,0:T(8,128)(2,1)S(1)}, u32[]{:S(2)}, u32[]{:S(2)}) collective-permute-start(bf16[128,256]{1,0:T(8,128)(2,1)S(1)} %copy-done.12), channel_id=1, source_target_pairs={{0,1},{1,2},{2,3},{3,4},{4,5},{5,6},{6,7},{7,0},{8,9},{9,10},{10,1... | collective-permute-start | bytes 196616 | tf_op jit(solution)/shard_map/ppermute | solution.py:563
  26.1 0.0 copy-done.11
  26.1 3.0 %collective-permute-start.3 = (bf16[128,256]{1,0:T(8,128)(2,1)S(1)}, bf16[128,256]{1,0:T(8,128)(2,1)S(1)}, u32[]{:S(2)}, u32[]{:S(2)}) collective-permute-start(bf16[128,256]{1,0:T(8,128)(2,1)S(1)} %copy-done.11), channel_id=1, source_target_pairs={{0,7},{1,0},{2,1},{3,2},{4,3},{5,4},{6,5},{7,6},{8,15},{9,8},{10,9... | collective-permute-start | bytes 196616 | tf_op jit(solution)/shard_map/ppermute | solution.py:563
  29.1 0.5 sine_negate_fusion
  29.6 0.0 copy-done.9
  29.6 0.1 compare_convert_fusion
  29.7 0.1 multiply_convert_fusion.forward_ref
  29.8 0.0 copy-done.8
  29.9 0.0 copy-done
  29.9 0.2 constant_dynamic-slice_fusion
  30.1 0.0 collective-permute-done.1.high_ref
  30.1 0.0 copy-start.5
  30.1 0.0 collective-permute-done.low_ref
  30.2 1.9 %collective-permute-start.5 = (bf16[8,256]{1,0:T(8,128)(2,1)S(1)}, bf16[8,256]{1,0:T(8,128)(2,1)S(1)}, u32[]{:S(2)}, u32[]{:S(2)}) collective-permute-start(bf16[8,256]{1,0:T(8,128)(2,1)S(1)} %reshape.338), channel_id=1, source_target_pairs={{0,7},{1,0},{2,1},{3,2},{4,3},{5,4},{6,5},{7,6},{8,15},{9,8},{10,9... | collective-permute-start | bytes 12296 | tf_op jit(solution)/shard_map/ppermute | solution.py:563
  32.1 0.2 collective-permute-start.4
  32.3 0.1 fusion.8
  32.4 0.1 copy.13
  32.5 1.3 %collective-permute-done.5 = bf16[8,256]{1,0:T(8,128)(2,1)S(1)} collective-permute-done((bf16[8,256]{1,0:T(8,128)(2,1)S(1)}, bf16[8,256]{1,0:T(8,128)(2,1)S(1)}, u32[]{:S(2)}, u32[]{:S(2)}) %collective-permute-start.5) | collective-permute-done | bytes 4128 | tf_op jit(solution)/shard_map/ppermute | solution.py:563
  33.8 4.7 %collective-permute-done.4 = bf16[8,256]{1,0:T(8,128)(2,1)S(1)} collective-permute-done((bf16[8,256]{1,0:T(8,128)(2,1)S(1)}, bf16[8,256]{1,0:T(8,128)(2,1)S(1)}, u32[]{:S(2)}, u32[]{:S(2)}) %collective-permute-start.4) | collective-permute-done | bytes 4128 | tf_op jit(solution)/shard_map/ppermute | solution.py:563
  38.6 0.0 collective-permute-done.2.left_ref
  38.6 0.0 collective-permute-done.3.right_ref
  38.6 0.0 copy-start.3
  38.6 3.1 %all-to-all-done = bf16[32,128,128]{2,1,0:T(8,128)(2,1)S(1)} async-done(((bf16[32,128,128]{2,1,0:T(8,128)(2,1)}), bf16[32,128,128]{2,1,0:T(8,128)(2,1)S(1)}, u32[]{:S(2)}, u32[]{:S(2)}) %all-to-all-start) | async-done | bytes 1048608 | tf_op jit(solution)/shard_map/all_to_all | solution.py:600
  41.7 0.0 copy-done.7
  41.7 7.7 %spectral.1 = bf16[4,8,128,128]{3,2,1,0:T(8,128)(2,1)} custom-call(bf16[4,8,128,128]{3,2,1,0:T(8,128)(2,1)S(1)} %bitcast.11, bf16[256,256]{1,0:T(8,128)(2,1)S(1)} %multiply_convert_fusion.forward_ref, bf16[256,256]{1,0:T(8,128)(2,1)S(1)} %fusion.inverse_ref, f32[2,8,128]{2,1,0:T(8,128)S(1)} %bitcast.14, f32[1,128]{1,0:T(1,128)S(1)} %copy-done.7, ...), custom_call_target="tpu_custom_call" | custom-call | flops 8589934592 | bytes 8388608 | tf_op jit(solution)/shard_map/spectral/pallas_call | solution.py:382
  49.5 0.0 copy-done.5
  49.5 0.0 copy-done.3
  49.5 2.7 %all-to-all-start.1 = ((bf16[32,128,128]{2,1,0:T(8,128)(2,1)}), bf16[32,128,128]{2,1,0:T(8,128)(2,1)S(1)}, u32[]{:S(2)}, u32[]{:S(2)}) async-start(bf16[32,128,128]{2,1,0:T(8,128)(2,1)} %bitcast.7), calls=%async_computation.1 | async-start | bytes 2097152 | tf_op jit(solution)/shard_map/all_to_all | solution.py:644
  52.1 0.1 copy.12.tap_ref
  52.2 0.0 copy-start.1
  52.2 1.2 %copy-done.1 = bf16[64,32,256]{2,1,0:T(8,128)(2,1)S(1)} copy-done((bf16[64,32,256]{2,1,0:T(8,128)(2,1)S(1)}, bf16[64,32,256]{2,1,0:T(8,128)(2,1)}, u32[]{:S(2)}) %copy-start.1) | copy-done | bytes 1048600
  53.5 0.0 copy-start.2
  53.5 1.0 %copy-done.2 = bf16[3,256,256]{2,1,0:T(8,128)(2,1)S(1)} copy-done((bf16[3,256,256]{2,1,0:T(8,128)(2,1)S(1)}, bf16[3,256,256]{2,1,0:T(8,128)(2,1)}, u32[]{:S(2)}) %copy-start.2) | copy-done | bytes 393240
  54.5 0.0 copy-start.4
  54.5 0.8 %copy-done.4 = bf16[128,256]{1,0:T(8,128)(2,1)S(1)} copy-done((bf16[128,256]{1,0:T(8,128)(2,1)S(1)}, bf16[128,256]{1,0:T(8,128)(2,1)}, u32[]{:S(2)}) %copy-start.4) | copy-done | bytes 65560
  55.3 0.0 copy-start.6
  55.3 0.8 copy-done.6
  56.1 15.8 %disco.1.disco_ref = f32[64,32,256]{2,1,0:T(8,128)S(1)} custom-call(f32[68,75]{1,0:T(8,128)S(1)} %copy.12.tap_ref, bf16[64,32,256]{2,1,0:T(8,128)(2,1)S(1)} %copy-done.1, bf16[64,256]{1,0:T(8,128)(2,1)S(1)} %collective-permute-done.low_ref, bf16[64,256]{1,0:T(8,128)(2,1)S(1)} %copy-done.6, bf16[128,256]{1,0:T(8,128)(2,1)S(1)} %collective-permute-done.2.left_ref, ...), custom_call_target="tpu_custom_call" | custom-call | flops 524288000 | bytes 4194304 | tf_op jit(solution)/shard_map/disco/pallas_call | solution.py:477
  71.9 7.8 %all-to-all-done.1.back_hbm = bf16[32,128,128]{2,1,0:T(8,128)(2,1)S(1)} async-done(((bf16[32,128,128]{2,1,0:T(8,128)(2,1)}), bf16[32,128,128]{2,1,0:T(8,128)(2,1)S(1)}, u32[]{:S(2)}, u32[]{:S(2)}) %all-to-all-start.1) | async-done | bytes 1048608 | tf_op jit(solution)/shard_map/all_to_all | solution.py:644
  79.7 2.3 %combine.1 = bf16[64,32,256]{2,1,0:T(8,128)(2,1)} custom-call(s32[1]{0:T(128)} %bitcast.flip_ref, bf16[32,128,128]{2,1,0:T(8,128)(2,1)S(1)} %all-to-all-done.1.back_hbm, f32[64,32,256]{2,1,0:T(8,128)S(1)} %disco.1.disco_ref), custom_call_target="tpu_custom_call" | custom-call | tf_op jit(solution)/shard_map/combine/pallas_call | solution.py:540
  (15 shorter events, 0.2 us)
Async XLA Ops:
  0.0 29.9 %copy-start = (f32[128,2,256]{2,1,0:T(2,128)S(1)}, f32[128,2,256]{2,1,0:T(2,128)}, u32[]{:S(2)}) copy-start(f32[128,2,256]{2,1,0:T(2,128)} %param.9) | copy-start | bytes 786436
  0.0 13.4 %copy-start.10 = (f32[128]{0:T(128)S(1)}, f32[128]{0:T(128)}, u32[]{:S(2)}) copy-start(f32[128]{0:T(128)} %constant.121) | copy-start | bytes 1540
  5.3 36.5 %all-to-all-start = ((bf16[32,128,128]{2,1,0:T(8,128)(2,1)}), bf16[32,128,128]{2,1,0:T(8,128)(2,1)S(1)}, u32[]{:S(2)}, u32[]{:S(2)}) async-start(bf16[32,128,128]{2,1,0:T(8,128)(2,1)} %get-tuple-element.27), calls=%async_computation | async-start | bytes 2097152 | tf_op jit(solution)/shard_map/all_to_all | solution.py:600
  14.1 8.5 %copy-start.13 = (bf16[64,256]{1,0:T(8,128)(2,1)S(1)}, bf16[64,256]{1,0:T(8,128)(2,1)}, u32[]{:S(2)}) copy-start(bf16[64,256]{1,0:T(8,128)(2,1)} %get-tuple-element.34) | copy-start | bytes 98308
  14.1 8.7 %copy-start.14 = (bf16[64,256]{1,0:T(8,128)(2,1)S(1)}, bf16[64,256]{1,0:T(8,128)(2,1)}, u32[]{:S(2)}) copy-start(bf16[64,256]{1,0:T(8,128)(2,1)} %get-tuple-element.35) | copy-start | bytes 98308
  14.1 10.2 %copy-start.12 = (bf16[128,256]{1,0:T(8,128)(2,1)S(1)}, bf16[128,256]{1,0:T(8,128)(2,1)}, u32[]{:S(2)}) copy-start(bf16[128,256]{1,0:T(8,128)(2,1)} %get-tuple-element.36) | copy-start | bytes 196612
  14.1 12.0 %copy-start.11 = (bf16[128,256]{1,0:T(8,128)(2,1)S(1)}, bf16[128,256]{1,0:T(8,128)(2,1)}, u32[]{:S(2)}) copy-start(bf16[128,256]{1,0:T(8,128)(2,1)} %get-tuple-element.37) | copy-start | bytes 196612
  14.1 15.5 %copy-start.9 = (s32[256,5]{0,1:T(8,128)S(1)}, s32[256,5]{0,1:T(8,128)}, u32[]{:S(2)}) copy-start(s32[256,5]{0,1:T(8,128)} %param.12) | copy-start | bytes 15364
  14.1 15.7 %copy-start.8 = (f32[3,256,5,5]{1,0,3,2:T(4,128)S(1)}, f32[3,256,5,5]{1,0,3,2:T(4,128)}, u32[]{:S(2)}) copy-start(f32[3,256,5,5]{1,0,3,2:T(4,128)} %param.11) | copy-start | bytes 230404
  14.1 27.6 %copy-start.7 = (f32[1,128]{1,0:T(1,128)S(1)}, f32[1,128]{1,0:T(1,128)}, u32[]{:S(2)}) copy-start(f32[1,128]{1,0:T(1,128)} %constant.123.quad_ref) | copy-start | bytes 1540
  22.6 7.5 %collective-permute-start = (bf16[64,256]{1,0:T(8,128)(2,1)S(1)}, bf16[64,256]{1,0:T(8,128)(2,1)S(1)}, u32[]{:S(2)}, u32[]{:S(2)}) collective-permute-start(bf16[64,256]{1,0:T(8,128)(2,1)S(1)} %copy-done.13), channel_id=1, source_target_pairs={{0,8},{8,16},{16,24},{24,0},{1,9},{9,17},{17,25},{25,1},{2,10},{10... | collective-permute-start | bytes 98312 | tf_op jit(solution)/shard_map/ppermute | solution.py:563
  22.8 7.3 %collective-permute-start.1 = (bf16[64,256]{1,0:T(8,128)(2,1)S(1)}, bf16[64,256]{1,0:T(8,128)(2,1)S(1)}, u32[]{:S(2)}, u32[]{:S(2)}) collective-permute-start(bf16[64,256]{1,0:T(8,128)(2,1)S(1)} %copy-done.14), channel_id=1, source_target_pairs={{0,24},{8,0},{16,8},{24,16},{1,25},{9,1},{17,9},{25,17},{2,26},{10... | collective-permute-start | bytes 98312 | tf_op jit(solution)/shard_map/ppermute | solution.py:563
  24.3 14.3 %collective-permute-start.2 = (bf16[128,256]{1,0:T(8,128)(2,1)S(1)}, bf16[128,256]{1,0:T(8,128)(2,1)S(1)}, u32[]{:S(2)}, u32[]{:S(2)}) collective-permute-start(bf16[128,256]{1,0:T(8,128)(2,1)S(1)} %copy-done.12), channel_id=1, source_target_pairs={{0,1},{1,2},{2,3},{3,4},{4,5},{5,6},{6,7},{7,0},{8,9},{9,10},{10,1... | collective-permute-start | bytes 196616 | tf_op jit(solution)/shard_map/ppermute | solution.py:563
  26.1 12.5 %collective-permute-start.3 = (bf16[128,256]{1,0:T(8,128)(2,1)S(1)}, bf16[128,256]{1,0:T(8,128)(2,1)S(1)}, u32[]{:S(2)}, u32[]{:S(2)}) collective-permute-start(bf16[128,256]{1,0:T(8,128)(2,1)S(1)} %copy-done.11), channel_id=1, source_target_pairs={{0,7},{1,0},{2,1},{3,2},{4,3},{5,4},{6,5},{7,6},{8,15},{9,8},{10,9... | collective-permute-start | bytes 196616 | tf_op jit(solution)/shard_map/ppermute | solution.py:563
  30.1 19.4 %copy-start.5 = (bf16[64,256]{1,0:T(8,128)(2,1)}, bf16[64,256]{1,0:T(8,128)(2,1)S(1)}, u32[]{:S(2)}) copy-start(bf16[64,256]{1,0:T(8,128)(2,1)S(1)} %collective-permute-done.1.high_ref) | copy-start | bytes 98308
  30.2 3.7 %collective-permute-start.5 = (bf16[8,256]{1,0:T(8,128)(2,1)S(1)}, bf16[8,256]{1,0:T(8,128)(2,1)S(1)}, u32[]{:S(2)}, u32[]{:S(2)}) collective-permute-start(bf16[8,256]{1,0:T(8,128)(2,1)S(1)} %reshape.338), channel_id=1, source_target_pairs={{0,7},{1,0},{2,1},{3,2},{4,3},{5,4},{6,5},{7,6},{8,15},{9,8},{10,9... | collective-permute-start | bytes 12296 | tf_op jit(solution)/shard_map/ppermute | solution.py:563
  32.1 6.5 %collective-permute-start.4 = (bf16[8,256]{1,0:T(8,128)(2,1)S(1)}, bf16[8,256]{1,0:T(8,128)(2,1)S(1)}, u32[]{:S(2)}, u32[]{:S(2)}) collective-permute-start(bf16[8,256]{1,0:T(8,128)(2,1)S(1)} %reshape.337), channel_id=1, source_target_pairs={{0,1},{1,2},{2,3},{3,4},{4,5},{5,6},{6,7},{7,0},{8,9},{9,10},{10,1... | collective-permute-start | bytes 12296 | tf_op jit(solution)/shard_map/ppermute | solution.py:563
  38.6 10.9 %copy-start.3 = (bf16[128,256]{1,0:T(8,128)(2,1)}, bf16[128,256]{1,0:T(8,128)(2,1)S(1)}, u32[]{:S(2)}) copy-start(bf16[128,256]{1,0:T(8,128)(2,1)S(1)} %collective-permute-done.3.right_ref) | copy-start | bytes 196612
  49.5 30.3 %all-to-all-start.1 = ((bf16[32,128,128]{2,1,0:T(8,128)(2,1)}), bf16[32,128,128]{2,1,0:T(8,128)(2,1)S(1)}, u32[]{:S(2)}, u32[]{:S(2)}) async-start(bf16[32,128,128]{2,1,0:T(8,128)(2,1)} %bitcast.7), calls=%async_computation.1 | async-start | bytes 2097152 | tf_op jit(solution)/shard_map/all_to_all | solution.py:644
  52.2 1.2 %copy-start.1 = (bf16[64,32,256]{2,1,0:T(8,128)(2,1)S(1)}, bf16[64,32,256]{2,1,0:T(8,128)(2,1)}, u32[]{:S(2)}) copy-start(bf16[64,32,256]{2,1,0:T(8,128)(2,1)} %get-tuple-element.43.grad_ref) | copy-start | bytes 3145732
  53.5 1.0 %copy-start.2 = (bf16[3,256,256]{2,1,0:T(8,128)(2,1)S(1)}, bf16[3,256,256]{2,1,0:T(8,128)(2,1)}, u32[]{:S(2)}) copy-start(bf16[3,256,256]{2,1,0:T(8,128)(2,1)} %mix_ref.1) | copy-start | bytes 1179652
  54.5 0.8 %copy-start.4 = (bf16[128,256]{1,0:T(8,128)(2,1)S(1)}, bf16[128,256]{1,0:T(8,128)(2,1)}, u32[]{:S(2)}) copy-start(bf16[128,256]{1,0:T(8,128)(2,1)} %copy-done.3) | copy-start | bytes 196612
  55.3 0.8 copy-start.6

commit v6 on v5

--- a/solution.py
+++ b/solution.py
@@ -381,7 +381,7 @@
     lines = pltpu.VMEM((tiles, local * (forward.shape[0] + PAD), LANES), F32)
     return pl.pallas_call(
         functools.partial(
-            spectral_kernel, group=group, q_count=q_count, unroll=math.gcd(block, 16), count=count
+            spectral_kernel, group=group, q_count=q_count, unroll=math.gcd(block, 32), count=count
         ),
         in_specs=[anywhere] + [vmem] * 4 + [anywhere] * count,
         out_specs=anywhere,

time: 82.5 us -> 81.6 us (0.989)
  Pallas kernels: 39.5 us -> 38.5 us
    pallas_call x1, Pallas kernels: 7.71 us -> 6.75 us  [spectral(): pl.pallas_call(functools.partial(spectral_kernel, group=group, q_count=q_...]
where the time goes in v6:
time: 81.6 us; the launch traced here: 81.1 us
  Pallas kernels  38.5 us (47%)
  starting transfers between devices  18.6 us (23%)
  waiting for transfers between devices  17 us (21%)
  local copies, waits for them, and re-layouts  4.4 us (5%)
  other arithmetic  2.2 us (3%)
    pallas_call x1, Pallas kernels, disco(): pl.pallas_call(disco_kernel, grid=(steps,), in_specs=[pl.BlockSpec(memory...  15.8 us
    ppermute x6, starting transfers between devices, shifted(): lax.ppermute(block, axis, [(i, (i + step) % count) for i in range(count)])  8.6 us
    pallas_call x1, Pallas kernels, legendre(): pl.pallas_call(functools.partial(legendre_kernel, degrees=degrees, span=8...  8.44 us
    all_to_all x1, waiting for transfers between devices, shards(): lax.all_to_all(back.reshape(devices, local * q_count, LANES), ('lat', 'lo...  7.84 us
    all_to_all x1, starting transfers between devices, shards(): received = lax.all_to_all(to_send, ('lat', 'lon'), 0, 0, tiled=True)  7.38 us
    pallas_call x1, Pallas kernels, spectral(): pl.pallas_call(functools.partial(spectral_kernel, group=group, q_count=q_...  6.75 us
    ppermute x6, waiting for transfers between devices, shifted(): lax.ppermute(block, axis, [(i, (i + step) % count) for i in range(count)])  6.04 us
    pallas_call x1, Pallas kernels, gradient(): pl.pallas_call(functools.partial(grad_kernel, group=group, q_count=q_coun...  5.25 us
  transfers between devices with their start and end apart: 8, of which 4 were waited for; matrix products, arithmetic and copies ran while one was open for 3% of the time, Pallas kernels for 30%

profile of v6, /device:TPU:0, one launch (start us, length us, event | category | flops | bytes accessed | tf_op | source)
XLA Modules:
  0.0 81.1 jit_solution(10431076078447942084)
XLA Ops:
  0.0 0.0 copy-start
  0.0 0.0 copy-start.10
  0.0 5.2 %gradient.1 = (bf16[64,32,256]{2,1,0:T(8,128)(2,1)}, bf16[32,128,128]{2,1,0:T(8,128)(2,1)}, bf16[64,256]{1,0:T(8,128)(2,1)}, bf16[64,256]{1,0:T(8,128)(2,1)}, bf...) custom-call(s32[1]{0:T(128)} %bitcast.flip_ref, bf16[64,32,256]{2,1,0:T(8,128)(2,1)} %pre_hbm.1, bf16[64,32,256]{2,1,0:T(8,128)(2,1)} %cot_hbm.1), custom_call_target="tpu_custom_call" | custom-call | tf_op jit(solution)/shard_map/gradient/pallas_call | solution.py:99
  5.3 7.4 %all-to-all-start = ((bf16[32,128,128]{2,1,0:T(8,128)(2,1)}), bf16[32,128,128]{2,1,0:T(8,128)(2,1)S(1)}, u32[]{:S(2)}, u32[]{:S(2)}) async-start(bf16[32,128,128]{2,1,0:T(8,128)(2,1)} %get-tuple-element.27), calls=%async_computation | async-start | bytes 2097152 | tf_op jit(solution)/shard_map/all_to_all | solution.py:600
  12.7 0.1 fusion.21
  12.7 0.6 pad_maximum_fusion.4.norm_ref
  13.4 0.0 copy-done.10
  13.4 0.7 multiply_add_fusion.start_ref
  14.1 0.0 copy-start.13
  14.1 0.0 copy-start.14
  14.1 0.0 copy-start.12
  14.1 0.0 copy-start.11
  14.1 0.0 copy-start.9
  14.1 0.0 copy-start.8
  14.1 0.0 copy-start.7
  14.1 8.4 %legendre.1 = (bf16[128,128,128]{2,1,0:T(8,128)(2,1)}, bf16[128,128,128]{2,1,0:T(8,128)(2,1)}) custom-call(f32[2,128]{1,0:T(2,128)} %pad_maximum_fusion.4.norm_ref, f32[1,128]{1,0:T(1,128)} %constant.119.cos_ref, f32[128,128]{1,0:T(8,128)} %multiply_add_fusion.start_ref), custom_call_target="tpu_custom_call" | custom-call | flops 8388608000 | bytes 8388608 | tf_op jit(solution)/shard_map/legendre/pallas_call | solution.py:171
  22.6 0.0 copy-done.13
  22.6 0.3 collective-permute-start
  22.8 0.0 copy-done.14
  22.8 1.5 %collective-permute-start.1 = (bf16[64,256]{1,0:T(8,128)(2,1)S(1)}, bf16[64,256]{1,0:T(8,128)(2,1)S(1)}, u32[]{:S(2)}, u32[]{:S(2)}) collective-permute-start(bf16[64,256]{1,0:T(8,128)(2,1)S(1)} %copy-done.14), channel_id=1, source_target_pairs={{0,24},{8,0},{16,8},{24,16},{1,25},{9,1},{17,9},{25,17},{2,26},{10... | collective-permute-start | bytes 98312 | tf_op jit(solution)/shard_map/ppermute | solution.py:563
  24.3 0.0 copy-done.12
  24.3 1.8 %collective-permute-start.2 = (bf16[128,256]{1,0:T(8,128)(2,1)S(1)}, bf16[128,256]{1,0:T(8,128)(2,1)S(1)}, u32[]{:S(2)}, u32[]{:S(2)}) collective-permute-start(bf16[128,256]{1,0:T(8,128)(2,1)S(1)} %copy-done.12), channel_id=1, source_target_pairs={{0,1},{1,2},{2,3},{3,4},{4,5},{5,6},{6,7},{7,0},{8,9},{9,10},{10,1... | collective-permute-start | bytes 196616 | tf_op jit(solution)/shard_map/ppermute | solution.py:563
  26.1 0.0 copy-done.11
  26.1 3.0 %collective-permute-start.3 = (bf16[128,256]{1,0:T(8,128)(2,1)S(1)}, bf16[128,256]{1,0:T(8,128)(2,1)S(1)}, u32[]{:S(2)}, u32[]{:S(2)}) collective-permute-start(bf16[128,256]{1,0:T(8,128)(2,1)S(1)} %copy-done.11), channel_id=1, source_target_pairs={{0,7},{1,0},{2,1},{3,2},{4,3},{5,4},{6,5},{7,6},{8,15},{9,8},{10,9... | collective-permute-start | bytes 196616 | tf_op jit(solution)/shard_map/ppermute | solution.py:563
  29.1 0.5 sine_negate_fusion
  29.6 0.0 copy-done.9
  29.6 0.1 compare_convert_fusion
  29.7 0.1 multiply_convert_fusion.forward_ref
  29.8 0.0 copy-done.8
  29.9 0.0 copy-done
  29.9 0.2 constant_dynamic-slice_fusion
  30.1 0.0 collective-permute-done.1.high_ref
  30.1 0.0 copy-start.5
  30.1 0.0 collective-permute-done.low_ref
  30.2 1.9 %collective-permute-start.5 = (bf16[8,256]{1,0:T(8,128)(2,1)S(1)}, bf16[8,256]{1,0:T(8,128)(2,1)S(1)}, u32[]{:S(2)}, u32[]{:S(2)}) collective-permute-start(bf16[8,256]{1,0:T(8,128)(2,1)S(1)} %reshape.338), channel_id=1, source_target_pairs={{0,7},{1,0},{2,1},{3,2},{4,3},{5,4},{6,5},{7,6},{8,15},{9,8},{10,9... | collective-permute-start | bytes 12296 | tf_op jit(solution)/shard_map/ppermute | solution.py:563
  32.1 0.2 collective-permute-start.4
  32.3 0.1 fusion.8
  32.4 0.1 copy.13
  32.5 1.3 %collective-permute-done.5 = bf16[8,256]{1,0:T(8,128)(2,1)S(1)} collective-permute-done((bf16[8,256]{1,0:T(8,128)(2,1)S(1)}, bf16[8,256]{1,0:T(8,128)(2,1)S(1)}, u32[]{:S(2)}, u32[]{:S(2)}) %collective-permute-start.5) | collective-permute-done | bytes 4128 | tf_op jit(solution)/shard_map/ppermute | solution.py:563
  33.8 4.7 %collective-permute-done.4 = bf16[8,256]{1,0:T(8,128)(2,1)S(1)} collective-permute-done((bf16[8,256]{1,0:T(8,128)(2,1)S(1)}, bf16[8,256]{1,0:T(8,128)(2,1)S(1)}, u32[]{:S(2)}, u32[]{:S(2)}) %collective-permute-start.4) | collective-permute-done | bytes 4128 | tf_op jit(solution)/shard_map/ppermute | solution.py:563
  38.6 0.0 collective-permute-done.2.left_ref
  38.6 0.0 collective-permute-done.3.right_ref
  38.6 0.0 copy-start.3
  38.6 3.1 %all-to-all-done = bf16[32,128,128]{2,1,0:T(8,128)(2,1)S(1)} async-done(((bf16[32,128,128]{2,1,0:T(8,128)(2,1)}), bf16[32,128,128]{2,1,0:T(8,128)(2,1)S(1)}, u32[]{:S(2)}, u32[]{:S(2)}) %all-to-all-start) | async-done | bytes 1048608 | tf_op jit(solution)/shard_map/all_to_all | solution.py:600
  41.7 0.0 copy-done.7
  41.7 6.8 %spectral.1 = bf16[4,8,128,128]{3,2,1,0:T(8,128)(2,1)} custom-call(bf16[4,8,128,128]{3,2,1,0:T(8,128)(2,1)S(1)} %bitcast.11, bf16[256,256]{1,0:T(8,128)(2,1)S(1)} %multiply_convert_fusion.forward_ref, bf16[256,256]{1,0:T(8,128)(2,1)S(1)} %fusion.inverse_ref, f32[2,8,128]{2,1,0:T(8,128)S(1)} %bitcast.14, f32[1,128]{1,0:T(1,128)S(1)} %copy-done.7, ...), custom_call_target="tpu_custom_call" | custom-call | flops 8589934592 | bytes 8388608 | tf_op jit(solution)/shard_map/spectral/pallas_call | solution.py:382
  48.5 0.0 copy-done.5
  48.5 0.0 copy-done.3
  48.5 2.7 %all-to-all-start.1 = ((bf16[32,128,128]{2,1,0:T(8,128)(2,1)}), bf16[32,128,128]{2,1,0:T(8,128)(2,1)S(1)}, u32[]{:S(2)}, u32[]{:S(2)}) async-start(bf16[32,128,128]{2,1,0:T(8,128)(2,1)} %bitcast.7), calls=%async_computation.1 | async-start | bytes 2097152 | tf_op jit(solution)/shard_map/all_to_all | solution.py:644
  51.2 0.1 copy.12.tap_ref
  51.3 0.0 copy-start.1
  51.3 1.2 %copy-done.1 = bf16[64,32,256]{2,1,0:T(8,128)(2,1)S(1)} copy-done((bf16[64,32,256]{2,1,0:T(8,128)(2,1)S(1)}, bf16[64,32,256]{2,1,0:T(8,128)(2,1)}, u32[]{:S(2)}) %copy-start.1) | copy-done | bytes 1048600
  52.5 0.0 copy-start.2
  52.5 1.0 %copy-done.2 = bf16[3,256,256]{2,1,0:T(8,128)(2,1)S(1)} copy-done((bf16[3,256,256]{2,1,0:T(8,128)(2,1)S(1)}, bf16[3,256,256]{2,1,0:T(8,128)(2,1)}, u32[]{:S(2)}) %copy-start.2) | copy-done | bytes 393240
  53.5 0.0 copy-start.4
  53.5 0.8 %copy-done.4 = bf16[128,256]{1,0:T(8,128)(2,1)S(1)} copy-done((bf16[128,256]{1,0:T(8,128)(2,1)S(1)}, bf16[128,256]{1,0:T(8,128)(2,1)}, u32[]{:S(2)}) %copy-start.4) | copy-done | bytes 65560
  54.3 0.0 copy-start.6
  54.3 0.8 copy-done.6
  55.1 15.8 %disco.1.disco_ref = f32[64,32,256]{2,1,0:T(8,128)S(1)} custom-call(f32[68,75]{1,0:T(8,128)S(1)} %copy.12.tap_ref, bf16[64,32,256]{2,1,0:T(8,128)(2,1)S(1)} %copy-done.1, bf16[64,256]{1,0:T(8,128)(2,1)S(1)} %collective-permute-done.low_ref, bf16[64,256]{1,0:T(8,128)(2,1)S(1)} %copy-done.6, bf16[128,256]{1,0:T(8,128)(2,1)S(1)} %collective-permute-done.2.left_ref, ...), custom_call_target="tpu_custom_call" | custom-call | flops 524288000 | bytes 4194304 | tf_op jit(solution)/shard_map/disco/pallas_call | solution.py:477
  70.9 7.8 %all-to-all-done.1.back_hbm = bf16[32,128,128]{2,1,0:T(8,128)(2,1)S(1)} async-done(((bf16[32,128,128]{2,1,0:T(8,128)(2,1)}), bf16[32,128,128]{2,1,0:T(8,128)(2,1)S(1)}, u32[]{:S(2)}, u32[]{:S(2)}) %all-to-all-start.1) | async-done | bytes 1048608 | tf_op jit(solution)/shard_map/all_to_all | solution.py:644
  78.8 2.3 %combine.1 = bf16[64,32,256]{2,1,0:T(8,128)(2,1)} custom-call(s32[1]{0:T(128)} %bitcast.flip_ref, bf16[32,128,128]{2,1,0:T(8,128)(2,1)S(1)} %all-to-all-done.1.back_hbm, f32[64,32,256]{2,1,0:T(8,128)S(1)} %disco.1.disco_ref), custom_call_target="tpu_custom_call" | custom-call | tf_op jit(solution)/shard_map/combine/pallas_call | solution.py:540
  (15 shorter events, 0.2 us)
Async XLA Ops:
  0.0 29.9 %copy-start = (f32[128,2,256]{2,1,0:T(2,128)S(1)}, f32[128,2,256]{2,1,0:T(2,128)}, u32[]{:S(2)}) copy-start(f32[128,2,256]{2,1,0:T(2,128)} %param.9) | copy-start | bytes 786436
  0.0 13.4 %copy-start.10 = (f32[128]{0:T(128)S(1)}, f32[128]{0:T(128)}, u32[]{:S(2)}) copy-start(f32[128]{0:T(128)} %constant.121) | copy-start | bytes 1540
  5.3 36.5 %all-to-all-start = ((bf16[32,128,128]{2,1,0:T(8,128)(2,1)}), bf16[32,128,128]{2,1,0:T(8,128)(2,1)S(1)}, u32[]{:S(2)}, u32[]{:S(2)}) async-start(bf16[32,128,128]{2,1,0:T(8,128)(2,1)} %get-tuple-element.27), calls=%async_computation | async-start | bytes 2097152 | tf_op jit(solution)/shard_map/all_to_all | solution.py:600
  14.1 8.5 %copy-start.13 = (bf16[64,256]{1,0:T(8,128)(2,1)S(1)}, bf16[64,256]{1,0:T(8,128)(2,1)}, u32[]{:S(2)}) copy-start(bf16[64,256]{1,0:T(8,128)(2,1)} %get-tuple-element.34) | copy-start | bytes 98308
  14.1 8.7 %copy-start.14 = (bf16[64,256]{1,0:T(8,128)(2,1)S(1)}, bf16[64,256]{1,0:T(8,128)(2,1)}, u32[]{:S(2)}) copy-start(bf16[64,256]{1,0:T(8,128)(2,1)} %get-tuple-element.35) | copy-start | bytes 98308
  14.1 10.2 %copy-start.12 = (bf16[128,256]{1,0:T(8,128)(2,1)S(1)}, bf16[128,256]{1,0:T(8,128)(2,1)}, u32[]{:S(2)}) copy-start(bf16[128,256]{1,0:T(8,128)(2,1)} %get-tuple-element.36) | copy-start | bytes 196612
  14.1 12.0 %copy-start.11 = (bf16[128,256]{1,0:T(8,128)(2,1)S(1)}, bf16[128,256]{1,0:T(8,128)(2,1)}, u32[]{:S(2)}) copy-start(bf16[128,256]{1,0:T(8,128)(2,1)} %get-tuple-element.37) | copy-start | bytes 196612
  14.1 15.5 %copy-start.9 = (s32[256,5]{0,1:T(8,128)S(1)}, s32[256,5]{0,1:T(8,128)}, u32[]{:S(2)}) copy-start(s32[256,5]{0,1:T(8,128)} %param.12) | copy-start | bytes 15364
  14.1 15.7 %copy-start.8 = (f32[3,256,5,5]{1,0,3,2:T(4,128)S(1)}, f32[3,256,5,5]{1,0,3,2:T(4,128)}, u32[]{:S(2)}) copy-start(f32[3,256,5,5]{1,0,3,2:T(4,128)} %param.11) | copy-start | bytes 230404
  14.1 27.6 %copy-start.7 = (f32[1,128]{1,0:T(1,128)S(1)}, f32[1,128]{1,0:T(1,128)}, u32[]{:S(2)}) copy-start(f32[1,128]{1,0:T(1,128)} %constant.123.quad_ref) | copy-start | bytes 1540
  22.6 7.5 %collective-permute-start = (bf16[64,256]{1,0:T(8,128)(2,1)S(1)}, bf16[64,256]{1,0:T(8,128)(2,1)S(1)}, u32[]{:S(2)}, u32[]{:S(2)}) collective-permute-start(bf16[64,256]{1,0:T(8,128)(2,1)S(1)} %copy-done.13), channel_id=1, source_target_pairs={{0,8},{8,16},{16,24},{24,0},{1,9},{9,17},{17,25},{25,1},{2,10},{10... | collective-permute-start | bytes 98312 | tf_op jit(solution)/shard_map/ppermute | solution.py:563
  22.8 7.3 %collective-permute-start.1 = (bf16[64,256]{1,0:T(8,128)(2,1)S(1)}, bf16[64,256]{1,0:T(8,128)(2,1)S(1)}, u32[]{:S(2)}, u32[]{:S(2)}) collective-permute-start(bf16[64,256]{1,0:T(8,128)(2,1)S(1)} %copy-done.14), channel_id=1, source_target_pairs={{0,24},{8,0},{16,8},{24,16},{1,25},{9,1},{17,9},{25,17},{2,26},{10... | collective-permute-start | bytes 98312 | tf_op jit(solution)/shard_map/ppermute | solution.py:563
  24.3 14.3 %collective-permute-start.2 = (bf16[128,256]{1,0:T(8,128)(2,1)S(1)}, bf16[128,256]{1,0:T(8,128)(2,1)S(1)}, u32[]{:S(2)}, u32[]{:S(2)}) collective-permute-start(bf16[128,256]{1,0:T(8,128)(2,1)S(1)} %copy-done.12), channel_id=1, source_target_pairs={{0,1},{1,2},{2,3},{3,4},{4,5},{5,6},{6,7},{7,0},{8,9},{9,10},{10,1... | collective-permute-start | bytes 196616 | tf_op jit(solution)/shard_map/ppermute | solution.py:563
  26.1 12.5 %collective-permute-start.3 = (bf16[128,256]{1,0:T(8,128)(2,1)S(1)}, bf16[128,256]{1,0:T(8,128)(2,1)S(1)}, u32[]{:S(2)}, u32[]{:S(2)}) collective-permute-start(bf16[128,256]{1,0:T(8,128)(2,1)S(1)} %copy-done.11), channel_id=1, source_target_pairs={{0,7},{1,0},{2,1},{3,2},{4,3},{5,4},{6,5},{7,6},{8,15},{9,8},{10,9... | collective-permute-start | bytes 196616 | tf_op jit(solution)/shard_map/ppermute | solution.py:563
  30.1 18.4 %copy-start.5 = (bf16[64,256]{1,0:T(8,128)(2,1)}, bf16[64,256]{1,0:T(8,128)(2,1)S(1)}, u32[]{:S(2)}) copy-start(bf16[64,256]{1,0:T(8,128)(2,1)S(1)} %collective-permute-done.1.high_ref) | copy-start | bytes 98308
  30.2 3.7 %collective-permute-start.5 = (bf16[8,256]{1,0:T(8,128)(2,1)S(1)}, bf16[8,256]{1,0:T(8,128)(2,1)S(1)}, u32[]{:S(2)}, u32[]{:S(2)}) collective-permute-start(bf16[8,256]{1,0:T(8,128)(2,1)S(1)} %reshape.338), channel_id=1, source_target_pairs={{0,7},{1,0},{2,1},{3,2},{4,3},{5,4},{6,5},{7,6},{8,15},{9,8},{10,9... | collective-permute-start | bytes 12296 | tf_op jit(solution)/shard_map/ppermute | solution.py:563
  32.1 6.5 %collective-permute-start.4 = (bf16[8,256]{1,0:T(8,128)(2,1)S(1)}, bf16[8,256]{1,0:T(8,128)(2,1)S(1)}, u32[]{:S(2)}, u32[]{:S(2)}) collective-permute-start(bf16[8,256]{1,0:T(8,128)(2,1)S(1)} %reshape.337), channel_id=1, source_target_pairs={{0,1},{1,2},{2,3},{3,4},{4,5},{5,6},{6,7},{7,0},{8,9},{9,10},{10,1... | collective-permute-start | bytes 12296 | tf_op jit(solution)/shard_map/ppermute | solution.py:563
  38.6 9.9 %copy-start.3 = (bf16[128,256]{1,0:T(8,128)(2,1)}, bf16[128,256]{1,0:T(8,128)(2,1)S(1)}, u32[]{:S(2)}) copy-start(bf16[128,256]{1,0:T(8,128)(2,1)S(1)} %collective-permute-done.3.right_ref) | copy-start | bytes 196612
  48.5 30.3 %all-to-all-start.1 = ((bf16[32,128,128]{2,1,0:T(8,128)(2,1)}), bf16[32,128,128]{2,1,0:T(8,128)(2,1)S(1)}, u32[]{:S(2)}, u32[]{:S(2)}) async-start(bf16[32,128,128]{2,1,0:T(8,128)(2,1)} %bitcast.7), calls=%async_computation.1 | async-start | bytes 2097152 | tf_op jit(solution)/shard_map/all_to_all | solution.py:644
  51.3 1.2 %copy-start.1 = (bf16[64,32,256]{2,1,0:T(8,128)(2,1)S(1)}, bf16[64,32,256]{2,1,0:T(8,128)(2,1)}, u32[]{:S(2)}) copy-start(bf16[64,32,256]{2,1,0:T(8,128)(2,1)} %get-tuple-element.43.grad_ref) | copy-start | bytes 3145732
  52.5 1.0 %copy-start.2 = (bf16[3,256,256]{2,1,0:T(8,128)(2,1)S(1)}, bf16[3,256,256]{2,1,0:T(8,128)(2,1)}, u32[]{:S(2)}) copy-start(bf16[3,256,256]{2,1,0:T(8,128)(2,1)} %mix_ref.1) | copy-start | bytes 1179652
  53.5 0.8 %copy-start.4 = (bf16[128,256]{1,0:T(8,128)(2,1)S(1)}, bf16[128,256]{1,0:T(8,128)(2,1)}, u32[]{:S(2)}) copy-start(bf16[128,256]{1,0:T(8,128)(2,1)} %copy-done.3) | copy-start | bytes 196612
  54.3 0.8 copy-start.6

commit v7 on v6

--- a/solution.py
+++ b/solution.py
@@ -202,7 +202,7 @@
     back_hbm, recv_ref, back_ref, grid_scr, even_scr, odd_scr, north_scr, south_scr = refs[count : count + 8]
     slots = refs[count + 8 : 2 * count + 8]
     recv_sem, table_sems, back_sems = refs[2 * count + 8 :]
-    bands, sectors = recv_ref.shape[:2]
+    sectors, bands = recv_ref.shape[:2]
     local, lats, lons = grid_scr.shape
     slot_count, orders_here, degrees, half = slots[0].shape
     tiles = half // LANES
@@ -246,7 +246,7 @@
         for band in range(bands):
             for unit in range(sectors // group):
                 pieces = [
-                    recv_ref[band, unit * group + k, at : at + q_count, :].astype(F32) for k in range(group)
+                    recv_ref[unit * group + k, band, at : at + q_count, :].astype(F32) for k in range(group)
                 ]
                 for r in range(group):
                     value = rolled(pieces[0], -r)
@@ -360,14 +360,14 @@
                     value = rolled(pieces[0], -k)
                     for r in range(1, group):
                         value = jnp.where(lane_group == r, rolled(pieces[r], r - k), value)
-                    back_ref[band, unit * group + k, at : at + q_count, :] = value.astype(BF16)
+                    back_ref[unit * group + k, band, at : at + q_count, :] = value.astype(BF16)
         give(chan).start()
     for chan in range(local):
         give(chan).wait()
 
 
 def spectral(received, forward, inverse, tables, weights, quad, group):
-    bands, sectors, rows, _ = received.shape
+    rows = received.shape[2]
     local = weights.shape[1]
     q_count = rows // local
     orders, degrees, half = tables[0].shape
@@ -587,7 +587,7 @@
     lon_count = lax.axis_size("lon")
     devices = lat_count * lon_count
     band_index = lax.axis_index("lat")
-    device_id = band_index * lon_count + lax.axis_index("lon")
+    device_id = lax.axis_index("lon") * lat_count + band_index
     total_lat = lat_rows * lat_count
     total_lon = lon_cols * lon_count
     mode_count = spec_weight.shape[0]
@@ -597,7 +597,7 @@
     flip = (2 * band_index >= lat_count).astype(jnp.int32).reshape(1)
 
     grad_pre, to_send, *edges = gradient(pre_act, cotangent, flip, devices, group)
-    received = lax.all_to_all(to_send, ("lat", "lon"), 0, 0, tiled=True)
+    received = lax.all_to_all(to_send, ("lon", "lat"), 0, 0, tiled=True)
 
     lane = np.arange(total_lat // 2)
     lats = lane // lat_rows * lat_rows + lane % q_count * group + lane % lat_rows // q_count
@@ -638,11 +638,11 @@
     )
     corners = corners_of(sides[0], sides[1], channels)
     received, sides = lax.optimization_barrier((received, sides))
-    blocks = received.reshape(lat_count, lon_count, local * q_count, LANES)
+    blocks = received.reshape(lon_count, lat_count, local * q_count, LANES)
     back = spectral(blocks, forward, inverse, tables, weights, quad, group)
     back, taps, corners = lax.optimization_barrier((back, taps, corners))
     returned = lax.all_to_all(
-        back.reshape(devices, local * q_count, LANES), ("lat", "lon"), 0, 0, tiled=True
+        back.reshape(devices, local * q_count, LANES), ("lon", "lat"), 0, 0, tiled=True
     )
     local_part = disco(taps, grad_pre, *sides, corners, disco_weight)
     return combine(returned, local_part, flip, group)

time: 81.6 us -> 79 us (0.968)
  waiting for transfers between devices: 17 us -> 13.3 us
  starting transfers between devices: 18.6 us -> 19.8 us
    all_to_all x2, waiting for transfers between devices: 11 us -> 7.36 us  [the longest x1 6.49 us: shards(): lax.all_to_all(back.reshape(devices, local * q_count, LANES), ('lon', 'la...]
    all_to_all x2, starting transfers between devices: 10 us -> 11.2 us  [the longest x1 7.38 us: shards(): received = lax.all_to_all(to_send, ('lon', 'lat'), 0, 0, tiled=True)]
  transfers between devices with their start and end apart: 8 -> 8, of which waited for: 4 -> 4; matrix products, arithmetic and copies ran while one was open for 3% -> 3% of each run, Pallas kernels for 30% -> 31%
where the time goes in v7:
time: 79 us; the launch traced here: 78.5 us
  Pallas kernels  38.5 us (49%)
  starting transfers between devices  19.8 us (25%)
  waiting for transfers between devices  13.3 us (17%)
  local copies, waits for them, and re-layouts  4.4 us (6%)
  other arithmetic  2.2 us (3%)
    pallas_call x1, Pallas kernels, disco(): pl.pallas_call(disco_kernel, grid=(steps,), in_specs=[pl.BlockSpec(memory...  15.8 us
    ppermute x6, starting transfers between devices, shifted(): lax.ppermute(block, axis, [(i, (i + step) % count) for i in range(count)])  8.6 us
    pallas_call x1, Pallas kernels, legendre(): pl.pallas_call(functools.partial(legendre_kernel, degrees=degrees, span=8...  8.44 us
    all_to_all x1, starting transfers between devices, shards(): received = lax.all_to_all(to_send, ('lon', 'lat'), 0, 0, tiled=True)  7.38 us
    pallas_call x1, Pallas kernels, spectral(): pl.pallas_call(functools.partial(spectral_kernel, group=group, q_count=q_...  6.75 us
    all_to_all x1, waiting for transfers between devices, shards(): lax.all_to_all(back.reshape(devices, local * q_count, LANES), ('lon', 'la...  6.49 us
    ppermute x6, waiting for transfers between devices, shifted(): lax.ppermute(block, axis, [(i, (i + step) % count) for i in range(count)])  5.95 us
    pallas_call x1, Pallas kernels, gradient(): pl.pallas_call(functools.partial(grad_kernel, group=group, q_count=q_coun...  5.25 us
  transfers between devices with their start and end apart: 8, of which 4 were waited for; matrix products, arithmetic and copies ran while one was open for 3% of the time, Pallas kernels for 31%

profile of v7, /device:TPU:0, one launch (start us, length us, event | category | flops | bytes accessed | tf_op | source)
XLA Modules:
  0.0 78.5 jit_solution(16364011110271383131)
XLA Ops:
  0.0 0.0 copy-start
  0.0 0.0 copy-start.10
  0.0 5.2 %gradient.1 = (bf16[64,32,256]{2,1,0:T(8,128)(2,1)}, bf16[32,128,128]{2,1,0:T(8,128)(2,1)}, bf16[64,256]{1,0:T(8,128)(2,1)}, bf16[64,256]{1,0:T(8,128)(2,1)}, bf...) custom-call(s32[1]{0:T(128)} %bitcast.flip_ref, bf16[64,32,256]{2,1,0:T(8,128)(2,1)} %pre_hbm.1, bf16[64,32,256]{2,1,0:T(8,128)(2,1)} %cot_hbm.1), custom_call_target="tpu_custom_call" | custom-call | tf_op jit(solution)/shard_map/gradient/pallas_call | solution.py:99
  5.3 7.4 %all-to-all-start = ((bf16[32,128,128]{2,1,0:T(8,128)(2,1)}), bf16[32,128,128]{2,1,0:T(8,128)(2,1)S(1)}, u32[]{:S(2)}, u32[]{:S(2)}) async-start(bf16[32,128,128]{2,1,0:T(8,128)(2,1)} %get-tuple-element.27), calls=%async_computation | async-start | bytes 2097152 | tf_op jit(solution)/shard_map/all_to_all | solution.py:600
  12.7 0.1 fusion.21
  12.7 0.6 pad_maximum_fusion.4.norm_ref
  13.4 0.0 copy-done.10
  13.4 0.7 multiply_add_fusion.start_ref
  14.1 0.0 copy-start.13
  14.1 0.0 copy-start.14
  14.1 0.0 copy-start.12
  14.1 0.0 copy-start.11
  14.1 0.0 copy-start.9
  14.1 0.0 copy-start.8
  14.1 0.0 copy-start.7
  14.1 8.4 %legendre.1 = (bf16[128,128,128]{2,1,0:T(8,128)(2,1)}, bf16[128,128,128]{2,1,0:T(8,128)(2,1)}) custom-call(f32[2,128]{1,0:T(2,128)} %pad_maximum_fusion.4.norm_ref, f32[1,128]{1,0:T(1,128)} %constant.119.cos_ref, f32[128,128]{1,0:T(8,128)} %multiply_add_fusion.start_ref), custom_call_target="tpu_custom_call" | custom-call | flops 8388608000 | bytes 8388608 | tf_op jit(solution)/shard_map/legendre/pallas_call | solution.py:171
  22.6 0.0 copy-done.13
  22.6 0.3 collective-permute-start
  22.8 0.0 copy-done.14
  22.8 1.5 %collective-permute-start.1 = (bf16[64,256]{1,0:T(8,128)(2,1)S(1)}, bf16[64,256]{1,0:T(8,128)(2,1)S(1)}, u32[]{:S(2)}, u32[]{:S(2)}) collective-permute-start(bf16[64,256]{1,0:T(8,128)(2,1)S(1)} %copy-done.14), channel_id=1, source_target_pairs={{0,24},{8,0},{16,8},{24,16},{1,25},{9,1},{17,9},{25,17},{2,26},{10... | collective-permute-start | bytes 98312 | tf_op jit(solution)/shard_map/ppermute | solution.py:563
  24.3 0.0 copy-done.12
  24.3 1.8 %collective-permute-start.2 = (bf16[128,256]{1,0:T(8,128)(2,1)S(1)}, bf16[128,256]{1,0:T(8,128)(2,1)S(1)}, u32[]{:S(2)}, u32[]{:S(2)}) collective-permute-start(bf16[128,256]{1,0:T(8,128)(2,1)S(1)} %copy-done.12), channel_id=1, source_target_pairs={{0,1},{1,2},{2,3},{3,4},{4,5},{5,6},{6,7},{7,0},{8,9},{9,10},{10,1... | collective-permute-start | bytes 196616 | tf_op jit(solution)/shard_map/ppermute | solution.py:563
  26.1 0.0 copy-done.11
  26.1 3.0 %collective-permute-start.3 = (bf16[128,256]{1,0:T(8,128)(2,1)S(1)}, bf16[128,256]{1,0:T(8,128)(2,1)S(1)}, u32[]{:S(2)}, u32[]{:S(2)}) collective-permute-start(bf16[128,256]{1,0:T(8,128)(2,1)S(1)} %copy-done.11), channel_id=1, source_target_pairs={{0,7},{1,0},{2,1},{3,2},{4,3},{5,4},{6,5},{7,6},{8,15},{9,8},{10,9... | collective-permute-start | bytes 196616 | tf_op jit(solution)/shard_map/ppermute | solution.py:563
  29.1 0.5 sine_negate_fusion
  29.6 0.0 copy-done.9
  29.6 0.1 compare_convert_fusion
  29.7 0.1 multiply_convert_fusion.forward_ref
  29.8 0.0 copy-done.8
  29.9 0.0 copy-done
  29.9 0.2 constant_dynamic-slice_fusion
  30.1 0.0 collective-permute-done.1.high_ref
  30.1 0.0 copy-start.5
  30.1 0.0 collective-permute-done.low_ref
  30.2 1.9 %collective-permute-start.5 = (bf16[8,256]{1,0:T(8,128)(2,1)S(1)}, bf16[8,256]{1,0:T(8,128)(2,1)S(1)}, u32[]{:S(2)}, u32[]{:S(2)}) collective-permute-start(bf16[8,256]{1,0:T(8,128)(2,1)S(1)} %reshape.338), channel_id=1, source_target_pairs={{0,7},{1,0},{2,1},{3,2},{4,3},{5,4},{6,5},{7,6},{8,15},{9,8},{10,9... | collective-permute-start | bytes 12296 | tf_op jit(solution)/shard_map/ppermute | solution.py:563
  32.1 0.2 collective-permute-start.4
  32.3 0.1 fusion.8
  32.4 0.1 copy.13
  32.5 1.3 %collective-permute-done.5 = bf16[8,256]{1,0:T(8,128)(2,1)S(1)} collective-permute-done((bf16[8,256]{1,0:T(8,128)(2,1)S(1)}, bf16[8,256]{1,0:T(8,128)(2,1)S(1)}, u32[]{:S(2)}, u32[]{:S(2)}) %collective-permute-start.5) | collective-permute-done | bytes 4128 | tf_op jit(solution)/shard_map/ppermute | solution.py:563
  33.9 4.6 %collective-permute-done.4 = bf16[8,256]{1,0:T(8,128)(2,1)S(1)} collective-permute-done((bf16[8,256]{1,0:T(8,128)(2,1)S(1)}, bf16[8,256]{1,0:T(8,128)(2,1)S(1)}, u32[]{:S(2)}, u32[]{:S(2)}) %collective-permute-start.4) | collective-permute-done | bytes 4128 | tf_op jit(solution)/shard_map/ppermute | solution.py:563
  38.5 0.0 collective-permute-done.2.left_ref
  38.5 0.0 collective-permute-done.3.right_ref
  38.5 0.0 copy-start.3
  38.5 0.9 %all-to-all-done = bf16[32,128,128]{2,1,0:T(8,128)(2,1)S(1)} async-done(((bf16[32,128,128]{2,1,0:T(8,128)(2,1)}), bf16[32,128,128]{2,1,0:T(8,128)(2,1)S(1)}, u32[]{:S(2)}, u32[]{:S(2)}) %all-to-all-start) | async-done | bytes 1048608 | tf_op jit(solution)/shard_map/all_to_all | solution.py:600
  39.4 0.0 copy-done.7
  39.4 6.8 %spectral.1 = bf16[8,4,128,128]{3,2,1,0:T(8,128)(2,1)} custom-call(bf16[8,4,128,128]{3,2,1,0:T(8,128)(2,1)S(1)} %bitcast.11, bf16[256,256]{1,0:T(8,128)(2,1)S(1)} %multiply_convert_fusion.forward_ref, bf16[256,256]{1,0:T(8,128)(2,1)S(1)} %fusion.inverse_ref, f32[2,8,128]{2,1,0:T(8,128)S(1)} %bitcast.14, f32[1,128]{1,0:T(1,128)S(1)} %copy-done.7, ...), custom_call_target="tpu_custom_call" | custom-call | flops 8589934592 | bytes 8388608 | tf_op jit(solution)/shard_map/spectral/pallas_call | solution.py:382
  46.1 0.0 copy-done.5
  46.1 0.0 copy-done.3
  46.1 3.9 %all-to-all-start.1 = ((bf16[32,128,128]{2,1,0:T(8,128)(2,1)}), bf16[32,128,128]{2,1,0:T(8,128)(2,1)S(1)}, u32[]{:S(2)}, u32[]{:S(2)}) async-start(bf16[32,128,128]{2,1,0:T(8,128)(2,1)} %bitcast.7), calls=%async_computation.1 | async-start | bytes 2097152 | tf_op jit(solution)/shard_map/all_to_all | solution.py:644
  50.0 0.1 copy.12.tap_ref
  50.1 0.0 copy-start.1
  50.1 1.2 %copy-done.1 = bf16[64,32,256]{2,1,0:T(8,128)(2,1)S(1)} copy-done((bf16[64,32,256]{2,1,0:T(8,128)(2,1)S(1)}, bf16[64,32,256]{2,1,0:T(8,128)(2,1)}, u32[]{:S(2)}) %copy-start.1) | copy-done | bytes 1048600
  51.3 0.0 copy-start.2
  51.3 1.0 %copy-done.2 = bf16[3,256,256]{2,1,0:T(8,128)(2,1)S(1)} copy-done((bf16[3,256,256]{2,1,0:T(8,128)(2,1)S(1)}, bf16[3,256,256]{2,1,0:T(8,128)(2,1)}, u32[]{:S(2)}) %copy-start.2) | copy-done | bytes 393240
  52.3 0.0 copy-start.4
  52.3 0.8 %copy-done.4 = bf16[128,256]{1,0:T(8,128)(2,1)S(1)} copy-done((bf16[128,256]{1,0:T(8,128)(2,1)S(1)}, bf16[128,256]{1,0:T(8,128)(2,1)}, u32[]{:S(2)}) %copy-start.4) | copy-done | bytes 65560
  53.2 0.0 copy-start.6
  53.2 0.8 copy-done.6
  53.9 15.8 %disco.1.disco_ref = f32[64,32,256]{2,1,0:T(8,128)S(1)} custom-call(f32[68,75]{1,0:T(8,128)S(1)} %copy.12.tap_ref, bf16[64,32,256]{2,1,0:T(8,128)(2,1)S(1)} %copy-done.1, bf16[64,256]{1,0:T(8,128)(2,1)S(1)} %collective-permute-done.low_ref, bf16[64,256]{1,0:T(8,128)(2,1)S(1)} %copy-done.6, bf16[128,256]{1,0:T(8,128)(2,1)S(1)} %collective-permute-done.2.left_ref, ...), custom_call_target="tpu_custom_call" | custom-call | flops 524288000 | bytes 4194304 | tf_op jit(solution)/shard_map/disco/pallas_call | solution.py:477
  69.8 6.5 %all-to-all-done.1.back_hbm = bf16[32,128,128]{2,1,0:T(8,128)(2,1)S(1)} async-done(((bf16[32,128,128]{2,1,0:T(8,128)(2,1)}), bf16[32,128,128]{2,1,0:T(8,128)(2,1)S(1)}, u32[]{:S(2)}, u32[]{:S(2)}) %all-to-all-start.1) | async-done | bytes 1048608 | tf_op jit(solution)/shard_map/all_to_all | solution.py:644
  76.2 2.3 %combine.1 = bf16[64,32,256]{2,1,0:T(8,128)(2,1)} custom-call(s32[1]{0:T(128)} %bitcast.flip_ref, bf16[32,128,128]{2,1,0:T(8,128)(2,1)S(1)} %all-to-all-done.1.back_hbm, f32[64,32,256]{2,1,0:T(8,128)S(1)} %disco.1.disco_ref), custom_call_target="tpu_custom_call" | custom-call | tf_op jit(solution)/shard_map/combine/pallas_call | solution.py:540
  (15 shorter events, 0.2 us)
Async XLA Ops:
  0.0 29.9 %copy-start = (f32[128,2,256]{2,1,0:T(2,128)S(1)}, f32[128,2,256]{2,1,0:T(2,128)}, u32[]{:S(2)}) copy-start(f32[128,2,256]{2,1,0:T(2,128)} %param.9) | copy-start | bytes 786436
  0.0 13.4 %copy-start.10 = (f32[128]{0:T(128)S(1)}, f32[128]{0:T(128)}, u32[]{:S(2)}) copy-start(f32[128]{0:T(128)} %constant.121) | copy-start | bytes 1540
  5.3 34.1 %all-to-all-start = ((bf16[32,128,128]{2,1,0:T(8,128)(2,1)}), bf16[32,128,128]{2,1,0:T(8,128)(2,1)S(1)}, u32[]{:S(2)}, u32[]{:S(2)}) async-start(bf16[32,128,128]{2,1,0:T(8,128)(2,1)} %get-tuple-element.27), calls=%async_computation | async-start | bytes 2097152 | tf_op jit(solution)/shard_map/all_to_all | solution.py:600
  14.1 8.5 %copy-start.13 = (bf16[64,256]{1,0:T(8,128)(2,1)S(1)}, bf16[64,256]{1,0:T(8,128)(2,1)}, u32[]{:S(2)}) copy-start(bf16[64,256]{1,0:T(8,128)(2,1)} %get-tuple-element.34) | copy-start | bytes 98308
  14.1 8.7 %copy-start.14 = (bf16[64,256]{1,0:T(8,128)(2,1)S(1)}, bf16[64,256]{1,0:T(8,128)(2,1)}, u32[]{:S(2)}) copy-start(bf16[64,256]{1,0:T(8,128)(2,1)} %get-tuple-element.35) | copy-start | bytes 98308
  14.1 10.2 %copy-start.12 = (bf16[128,256]{1,0:T(8,128)(2,1)S(1)}, bf16[128,256]{1,0:T(8,128)(2,1)}, u32[]{:S(2)}) copy-start(bf16[128,256]{1,0:T(8,128)(2,1)} %get-tuple-element.36) | copy-start | bytes 196612
  14.1 12.0 %copy-start.11 = (bf16[128,256]{1,0:T(8,128)(2,1)S(1)}, bf16[128,256]{1,0:T(8,128)(2,1)}, u32[]{:S(2)}) copy-start(bf16[128,256]{1,0:T(8,128)(2,1)} %get-tuple-element.37) | copy-start | bytes 196612
  14.1 15.5 %copy-start.9 = (s32[256,5]{0,1:T(8,128)S(1)}, s32[256,5]{0,1:T(8,128)}, u32[]{:S(2)}) copy-start(s32[256,5]{0,1:T(8,128)} %param.12) | copy-start | bytes 15364
  14.1 15.7 %copy-start.8 = (f32[3,256,5,5]{1,0,3,2:T(4,128)S(1)}, f32[3,256,5,5]{1,0,3,2:T(4,128)}, u32[]{:S(2)}) copy-start(f32[3,256,5,5]{1,0,3,2:T(4,128)} %param.11) | copy-start | bytes 230404
  14.1 25.3 %copy-start.7 = (f32[1,128]{1,0:T(1,128)S(1)}, f32[1,128]{1,0:T(1,128)}, u32[]{:S(2)}) copy-start(f32[1,128]{1,0:T(1,128)} %constant.123.quad_ref) | copy-start | bytes 1540
  22.6 7.5 %collective-permute-start = (bf16[64,256]{1,0:T(8,128)(2,1)S(1)}, bf16[64,256]{1,0:T(8,128)(2,1)S(1)}, u32[]{:S(2)}, u32[]{:S(2)}) collective-permute-start(bf16[64,256]{1,0:T(8,128)(2,1)S(1)} %copy-done.13), channel_id=1, source_target_pairs={{0,8},{8,16},{16,24},{24,0},{1,9},{9,17},{17,25},{25,1},{2,10},{10... | collective-permute-start | bytes 98312 | tf_op jit(solution)/shard_map/ppermute | solution.py:563
  22.8 7.3 %collective-permute-start.1 = (bf16[64,256]{1,0:T(8,128)(2,1)S(1)}, bf16[64,256]{1,0:T(8,128)(2,1)S(1)}, u32[]{:S(2)}, u32[]{:S(2)}) collective-permute-start(bf16[64,256]{1,0:T(8,128)(2,1)S(1)} %copy-done.14), channel_id=1, source_target_pairs={{0,24},{8,0},{16,8},{24,16},{1,25},{9,1},{17,9},{25,17},{2,26},{10... | collective-permute-start | bytes 98312 | tf_op jit(solution)/shard_map/ppermute | solution.py:563
  24.3 14.2 %collective-permute-start.2 = (bf16[128,256]{1,0:T(8,128)(2,1)S(1)}, bf16[128,256]{1,0:T(8,128)(2,1)S(1)}, u32[]{:S(2)}, u32[]{:S(2)}) collective-permute-start(bf16[128,256]{1,0:T(8,128)(2,1)S(1)} %copy-done.12), channel_id=1, source_target_pairs={{0,1},{1,2},{2,3},{3,4},{4,5},{5,6},{6,7},{7,0},{8,9},{9,10},{10,1... | collective-permute-start | bytes 196616 | tf_op jit(solution)/shard_map/ppermute | solution.py:563
  26.1 12.4 %collective-permute-start.3 = (bf16[128,256]{1,0:T(8,128)(2,1)S(1)}, bf16[128,256]{1,0:T(8,128)(2,1)S(1)}, u32[]{:S(2)}, u32[]{:S(2)}) collective-permute-start(bf16[128,256]{1,0:T(8,128)(2,1)S(1)} %copy-done.11), channel_id=1, source_target_pairs={{0,7},{1,0},{2,1},{3,2},{4,3},{5,4},{6,5},{7,6},{8,15},{9,8},{10,9... | collective-permute-start | bytes 196616 | tf_op jit(solution)/shard_map/ppermute | solution.py:563
  30.1 16.0 %copy-start.5 = (bf16[64,256]{1,0:T(8,128)(2,1)}, bf16[64,256]{1,0:T(8,128)(2,1)S(1)}, u32[]{:S(2)}) copy-start(bf16[64,256]{1,0:T(8,128)(2,1)S(1)} %collective-permute-done.1.high_ref) | copy-start | bytes 98308
  30.2 3.7 %collective-permute-start.5 = (bf16[8,256]{1,0:T(8,128)(2,1)S(1)}, bf16[8,256]{1,0:T(8,128)(2,1)S(1)}, u32[]{:S(2)}, u32[]{:S(2)}) collective-permute-start(bf16[8,256]{1,0:T(8,128)(2,1)S(1)} %reshape.338), channel_id=1, source_target_pairs={{0,7},{1,0},{2,1},{3,2},{4,3},{5,4},{6,5},{7,6},{8,15},{9,8},{10,9... | collective-permute-start | bytes 12296 | tf_op jit(solution)/shard_map/ppermute | solution.py:563
  32.1 6.4 %collective-permute-start.4 = (bf16[8,256]{1,0:T(8,128)(2,1)S(1)}, bf16[8,256]{1,0:T(8,128)(2,1)S(1)}, u32[]{:S(2)}, u32[]{:S(2)}) collective-permute-start(bf16[8,256]{1,0:T(8,128)(2,1)S(1)} %reshape.337), channel_id=1, source_target_pairs={{0,1},{1,2},{2,3},{3,4},{4,5},{5,6},{6,7},{7,0},{8,9},{9,10},{10,1... | collective-permute-start | bytes 12296 | tf_op jit(solution)/shard_map/ppermute | solution.py:563
  38.5 7.7 %copy-start.3 = (bf16[128,256]{1,0:T(8,128)(2,1)}, bf16[128,256]{1,0:T(8,128)(2,1)S(1)}, u32[]{:S(2)}) copy-start(bf16[128,256]{1,0:T(8,128)(2,1)S(1)} %collective-permute-done.3.right_ref) | copy-start | bytes 196612
  46.1 30.1 %all-to-all-start.1 = ((bf16[32,128,128]{2,1,0:T(8,128)(2,1)}), bf16[32,128,128]{2,1,0:T(8,128)(2,1)S(1)}, u32[]{:S(2)}, u32[]{:S(2)}) async-start(bf16[32,128,128]{2,1,0:T(8,128)(2,1)} %bitcast.7), calls=%async_computation.1 | async-start | bytes 2097152 | tf_op jit(solution)/shard_map/all_to_all | solution.py:644
  50.1 1.2 %copy-start.1 = (bf16[64,32,256]{2,1,0:T(8,128)(2,1)S(1)}, bf16[64,32,256]{2,1,0:T(8,128)(2,1)}, u32[]{:S(2)}) copy-start(bf16[64,32,256]{2,1,0:T(8,128)(2,1)} %get-tuple-element.43.grad_ref) | copy-start | bytes 3145732
  51.3 1.0 %copy-start.2 = (bf16[3,256,256]{2,1,0:T(8,128)(2,1)S(1)}, bf16[3,256,256]{2,1,0:T(8,128)(2,1)}, u32[]{:S(2)}) copy-start(bf16[3,256,256]{2,1,0:T(8,128)(2,1)} %mix_ref.1) | copy-start | bytes 1179652
  52.3 0.8 %copy-start.4 = (bf16[128,256]{1,0:T(8,128)(2,1)S(1)}, bf16[128,256]{1,0:T(8,128)(2,1)}, u32[]{:S(2)}) copy-start(bf16[128,256]{1,0:T(8,128)(2,1)} %copy-done.3) | copy-start | bytes 196612
  53.2 0.8 copy-start.6

commit v8 on v7

--- a/solution.py
+++ b/solution.py
@@ -30,8 +30,9 @@
 
 
 def grad_kernel(
-    flip_ref, pre_hbm, cot_hbm, grad_hbm, send_hbm, first_ref, last_ref, west_ref, east_ref,
-    pre_ref, cot_ref, grad_ref, send_ref, rows_scr, chan_scr, in_sems, out_sems, *, group, q_count,
+    flip_ref, pre_hbm, cot_hbm, grad_hbm, send_hbm, first_hbm, last_hbm, west_hbm, east_hbm,
+    pre_ref, cot_ref, grad_ref, send_ref, first_ref, last_ref, west_ref, east_ref, rows_scr, chan_scr,
+    in_sems, out_sems, edge_sems, *, group, q_count,
 ):
     rows, cols, channels = pre_ref.shape
     part = rows // CHUNKS
@@ -73,20 +74,26 @@
             for tile in range(channels // LANES):
                 turned = stacked[:, tile * LANES : (tile + 1) * LANES].T
                 chan_scr[pl.ds(tile * LANES * q_count + q_out, LANES, stride=q_count), :] = turned
-    dests, count = send_ref.shape[:2]
-    for chunk in range(CHUNKS):
-        for dest in range(chunk * dests // CHUNKS, (chunk + 1) * dests // CHUNKS):
-            send_ref[dest] = chan_scr[dest * count : (dest + 1) * count, :].astype(BF16)
-        send(chunk).start()
     for row in range(REACH):
         first_ref[row * cols : (row + 1) * cols, :] = grad_ref[row]
         last_ref[row * cols : (row + 1) * cols, :] = grad_ref[rows - REACH + row]
     for side in range(REACH):
         west_ref[side * rows : (side + 1) * rows, :] = rows_scr[:, side, :].astype(BF16)
         east_ref[side * rows : (side + 1) * rows, :] = rows_scr[:, cols - REACH + side, :].astype(BF16)
+    pairs = ((first_ref, first_hbm), (last_ref, last_hbm), (west_ref, west_hbm), (east_ref, east_hbm))
+    edges = [pltpu.make_async_copy(ref, hbm, edge_sems.at[at]) for at, (ref, hbm) in enumerate(pairs)]
+    for edge in edges:
+        edge.start()
+    dests, count = send_ref.shape[:2]
+    for chunk in range(CHUNKS):
+        for dest in range(chunk * dests // CHUNKS, (chunk + 1) * dests // CHUNKS):
+            send_ref[dest] = chan_scr[dest * count : (dest + 1) * count, :].astype(BF16)
+        send(chunk).start()
     for chunk in range(CHUNKS):
         keep(chunk).wait()
         send(chunk).wait()
+    for edge in edges:
+        edge.wait()
 
 
 def gradient(pre_act, cotangent, flip, devices, group):
@@ -95,21 +102,22 @@
     send = (devices, channels // devices * q_count, LANES)
     edges = [(REACH * cols, channels)] * 2 + [(REACH * rows, channels)] * 2
     anywhere = pl.BlockSpec(memory_space=pl.ANY)
-    vmem = pl.BlockSpec(memory_space=pltpu.VMEM)
     return pl.pallas_call(
         functools.partial(grad_kernel, group=group, q_count=q_count),
         in_specs=[pl.BlockSpec(memory_space=pltpu.SMEM), anywhere, anywhere],
-        out_specs=[anywhere, anywhere] + [vmem] * len(edges),
+        out_specs=[anywhere] * (2 + len(edges)),
         out_shape=[jax.ShapeDtypeStruct(shape, BF16) for shape in (pre_act.shape, send, *edges)],
         scratch_shapes=[
             pltpu.VMEM(pre_act.shape, BF16),
             pltpu.VMEM(pre_act.shape, BF16),
             pltpu.VMEM(pre_act.shape, BF16),
             pltpu.VMEM(send, BF16),
+            *[pltpu.VMEM(edge, BF16) for edge in edges],
             pltpu.VMEM(pre_act.shape, F32),
             pltpu.VMEM((channels * q_count, LANES), F32),
             pltpu.SemaphoreType.DMA((2, CHUNKS)),
             pltpu.SemaphoreType.DMA((2, CHUNKS)),
+            pltpu.SemaphoreType.DMA((4,)),
         ],
         compiler_params=params(60 * MIB),
         name="gradient",

time: 79 us -> 78.2 us (0.990)
  Pallas kernels: 38.5 us -> 37.7 us
    pallas_call x1, Pallas kernels: 5.25 us -> 4.43 us  [gradient(): pl.pallas_call(functools.partial(grad_kernel, group=group, q_count=q_coun...]
  transfers between devices with their start and end apart: 8 -> 8, of which waited for: 4 -> 4; matrix products, arithmetic and copies ran while one was open for 3% -> 4% of each run, Pallas kernels for 31% -> 31%
where the time goes in v8:
time: 78.2 us; the launch traced here: 77.7 us
  Pallas kernels  37.7 us (48%)
  starting transfers between devices  19.8 us (25%)
  waiting for transfers between devices  13.3 us (17%)
  local copies, waits for them, and re-layouts  4.4 us (6%)
  other arithmetic  2.2 us (3%)
    pallas_call x1, Pallas kernels, disco(): pl.pallas_call(disco_kernel, grid=(steps,), in_specs=[pl.BlockSpec(memory...  15.8 us
    ppermute x6, starting transfers between devices, shifted(): lax.ppermute(block, axis, [(i, (i + step) % count) for i in range(count)])  8.6 us
    pallas_call x1, Pallas kernels, legendre(): pl.pallas_call(functools.partial(legendre_kernel, degrees=degrees, span=8...  8.44 us
    all_to_all x1, starting transfers between devices, shards(): received = lax.all_to_all(to_send, ('lon', 'lat'), 0, 0, tiled=True)  7.38 us
    pallas_call x1, Pallas kernels, spectral(): pl.pallas_call(functools.partial(spectral_kernel, group=group, q_count=q_...  6.76 us
    all_to_all x1, waiting for transfers between devices, shards(): lax.all_to_all(back.reshape(devices, local * q_count, LANES), ('lon', 'la...  6.49 us
    ppermute x6, waiting for transfers between devices, shifted(): lax.ppermute(block, axis, [(i, (i + step) % count) for i in range(count)])  5.95 us
    pallas_call x1, Pallas kernels, gradient(): pl.pallas_call(functools.partial(grad_kernel, group=group, q_count=q_coun...  4.43 us
  transfers between devices with their start and end apart: 8, of which 4 were waited for; matrix products, arithmetic and copies ran while one was open for 4% of the time, Pallas kernels for 31%

profile of v8, /device:TPU:0, one launch (start us, length us, event | category | flops | bytes accessed | tf_op | source)
XLA Modules:
  0.0 77.7 jit_solution(17751809653991096418)
XLA Ops:
  0.0 0.0 copy-start
  0.0 0.0 copy-start.10
  0.0 4.4 %gradient.1 = (bf16[64,32,256]{2,1,0:T(8,128)(2,1)}, bf16[32,128,128]{2,1,0:T(8,128)(2,1)}, bf16[64,256]{1,0:T(8,128)(2,1)}, bf16[64,256]{1,0:T(8,128)(2,1)}, bf...) custom-call(s32[1]{0:T(128)} %bitcast.flip_ref, bf16[64,32,256]{2,1,0:T(8,128)(2,1)} %pre_hbm.1, bf16[64,32,256]{2,1,0:T(8,128)(2,1)} %cot_hbm.1), custom_call_target="tpu_custom_call" | custom-call | tf_op jit(solution)/shard_map/gradient/pallas_call | solution.py:105
  4.4 7.4 %all-to-all-start = ((bf16[32,128,128]{2,1,0:T(8,128)(2,1)}), bf16[32,128,128]{2,1,0:T(8,128)(2,1)S(1)}, u32[]{:S(2)}, u32[]{:S(2)}) async-start(bf16[32,128,128]{2,1,0:T(8,128)(2,1)} %get-tuple-element.27), calls=%async_computation | async-start | bytes 2097152 | tf_op jit(solution)/shard_map/all_to_all | solution.py:608
  11.9 0.1 fusion.21
  11.9 0.6 pad_maximum_fusion.4.norm_ref
  12.5 0.0 copy-done.10
  12.5 0.7 multiply_add_fusion.start_ref
  13.3 0.0 copy-start.13
  13.3 0.0 copy-start.14
  13.3 0.0 copy-start.12
  13.3 0.0 copy-start.11
  13.3 0.0 copy-start.9
  13.3 0.0 copy-start.8
  13.3 0.0 copy-start.7
  13.3 8.4 %legendre.1 = (bf16[128,128,128]{2,1,0:T(8,128)(2,1)}, bf16[128,128,128]{2,1,0:T(8,128)(2,1)}) custom-call(f32[2,128]{1,0:T(2,128)} %pad_maximum_fusion.4.norm_ref, f32[1,128]{1,0:T(1,128)} %constant.119.cos_ref, f32[128,128]{1,0:T(8,128)} %multiply_add_fusion.start_ref), custom_call_target="tpu_custom_call" | custom-call | flops 8388608000 | bytes 8388608 | tf_op jit(solution)/shard_map/legendre/pallas_call | solution.py:179
  21.7 0.0 copy-done.13
  21.7 0.3 collective-permute-start
  22.0 0.0 copy-done.14
  22.0 1.5 %collective-permute-start.1 = (bf16[64,256]{1,0:T(8,128)(2,1)S(1)}, bf16[64,256]{1,0:T(8,128)(2,1)S(1)}, u32[]{:S(2)}, u32[]{:S(2)}) collective-permute-start(bf16[64,256]{1,0:T(8,128)(2,1)S(1)} %copy-done.14), channel_id=1, source_target_pairs={{0,24},{8,0},{16,8},{24,16},{1,25},{9,1},{17,9},{25,17},{2,26},{10... | collective-permute-start | bytes 98312 | tf_op jit(solution)/shard_map/ppermute | solution.py:571
  23.5 0.0 copy-done.12
  23.5 1.8 %collective-permute-start.2 = (bf16[128,256]{1,0:T(8,128)(2,1)S(1)}, bf16[128,256]{1,0:T(8,128)(2,1)S(1)}, u32[]{:S(2)}, u32[]{:S(2)}) collective-permute-start(bf16[128,256]{1,0:T(8,128)(2,1)S(1)} %copy-done.12), channel_id=1, source_target_pairs={{0,1},{1,2},{2,3},{3,4},{4,5},{5,6},{6,7},{7,0},{8,9},{9,10},{10,1... | collective-permute-start | bytes 196616 | tf_op jit(solution)/shard_map/ppermute | solution.py:571
  25.3 0.0 copy-done.11
  25.3 3.0 %collective-permute-start.3 = (bf16[128,256]{1,0:T(8,128)(2,1)S(1)}, bf16[128,256]{1,0:T(8,128)(2,1)S(1)}, u32[]{:S(2)}, u32[]{:S(2)}) collective-permute-start(bf16[128,256]{1,0:T(8,128)(2,1)S(1)} %copy-done.11), channel_id=1, source_target_pairs={{0,7},{1,0},{2,1},{3,2},{4,3},{5,4},{6,5},{7,6},{8,15},{9,8},{10,9... | collective-permute-start | bytes 196616 | tf_op jit(solution)/shard_map/ppermute | solution.py:571
  28.2 0.5 sine_negate_fusion
  28.8 0.0 copy-done.9
  28.8 0.1 compare_convert_fusion
  28.9 0.1 multiply_convert_fusion.forward_ref
  29.0 0.0 copy-done.8
  29.0 0.0 copy-done
  29.0 0.2 constant_dynamic-slice_fusion
  29.3 0.0 collective-permute-done.1.high_ref
  29.3 0.0 copy-start.5
  29.3 0.0 collective-permute-done.low_ref
  29.3 1.9 %collective-permute-start.5 = (bf16[8,256]{1,0:T(8,128)(2,1)S(1)}, bf16[8,256]{1,0:T(8,128)(2,1)S(1)}, u32[]{:S(2)}, u32[]{:S(2)}) collective-permute-start(bf16[8,256]{1,0:T(8,128)(2,1)S(1)} %reshape.338), channel_id=1, source_target_pairs={{0,7},{1,0},{2,1},{3,2},{4,3},{5,4},{6,5},{7,6},{8,15},{9,8},{10,9... | collective-permute-start | bytes 12296 | tf_op jit(solution)/shard_map/ppermute | solution.py:571
  31.3 0.2 collective-permute-start.4
  31.5 0.1 fusion.8
  31.6 0.1 copy.13
  31.7 1.3 %collective-permute-done.5 = bf16[8,256]{1,0:T(8,128)(2,1)S(1)} collective-permute-done((bf16[8,256]{1,0:T(8,128)(2,1)S(1)}, bf16[8,256]{1,0:T(8,128)(2,1)S(1)}, u32[]{:S(2)}, u32[]{:S(2)}) %collective-permute-start.5) | collective-permute-done | bytes 4128 | tf_op jit(solution)/shard_map/ppermute | solution.py:571
  33.0 4.6 %collective-permute-done.4 = bf16[8,256]{1,0:T(8,128)(2,1)S(1)} collective-permute-done((bf16[8,256]{1,0:T(8,128)(2,1)S(1)}, bf16[8,256]{1,0:T(8,128)(2,1)S(1)}, u32[]{:S(2)}, u32[]{:S(2)}) %collective-permute-start.4) | collective-permute-done | bytes 4128 | tf_op jit(solution)/shard_map/ppermute | solution.py:571
  37.7 0.0 collective-permute-done.2.left_ref
  37.7 0.0 collective-permute-done.3.right_ref
  37.7 0.0 copy-start.3
  37.7 0.9 %all-to-all-done = bf16[32,128,128]{2,1,0:T(8,128)(2,1)S(1)} async-done(((bf16[32,128,128]{2,1,0:T(8,128)(2,1)}), bf16[32,128,128]{2,1,0:T(8,128)(2,1)S(1)}, u32[]{:S(2)}, u32[]{:S(2)}) %all-to-all-start) | async-done | bytes 1048608 | tf_op jit(solution)/shard_map/all_to_all | solution.py:608
  38.5 0.0 copy-done.7
  38.5 6.8 %spectral.1 = bf16[8,4,128,128]{3,2,1,0:T(8,128)(2,1)} custom-call(bf16[8,4,128,128]{3,2,1,0:T(8,128)(2,1)S(1)} %bitcast.11, bf16[256,256]{1,0:T(8,128)(2,1)S(1)} %multiply_convert_fusion.forward_ref, bf16[256,256]{1,0:T(8,128)(2,1)S(1)} %fusion.inverse_ref, f32[2,8,128]{2,1,0:T(8,128)S(1)} %bitcast.14, f32[1,128]{1,0:T(1,128)S(1)} %copy-done.7, ...), custom_call_target="tpu_custom_call" | custom-call | flops 8589934592 | bytes 8388608 | tf_op jit(solution)/shard_map/spectral/pallas_call | solution.py:390
  45.3 0.0 copy-done.5
  45.3 0.0 copy-done.3
  45.3 3.9 %all-to-all-start.1 = ((bf16[32,128,128]{2,1,0:T(8,128)(2,1)}), bf16[32,128,128]{2,1,0:T(8,128)(2,1)S(1)}, u32[]{:S(2)}, u32[]{:S(2)}) async-start(bf16[32,128,128]{2,1,0:T(8,128)(2,1)} %bitcast.7), calls=%async_computation.1 | async-start | bytes 2097152 | tf_op jit(solution)/shard_map/all_to_all | solution.py:652
  49.2 0.1 copy.12.tap_ref
  49.3 0.0 copy-start.1
  49.3 1.2 %copy-done.1 = bf16[64,32,256]{2,1,0:T(8,128)(2,1)S(1)} copy-done((bf16[64,32,256]{2,1,0:T(8,128)(2,1)S(1)}, bf16[64,32,256]{2,1,0:T(8,128)(2,1)}, u32[]{:S(2)}) %copy-start.1) | copy-done | bytes 1048600
  50.5 0.0 copy-start.2
  50.5 1.0 %copy-done.2 = bf16[3,256,256]{2,1,0:T(8,128)(2,1)S(1)} copy-done((bf16[3,256,256]{2,1,0:T(8,128)(2,1)S(1)}, bf16[3,256,256]{2,1,0:T(8,128)(2,1)}, u32[]{:S(2)}) %copy-start.2) | copy-done | bytes 393240
  51.5 0.0 copy-start.4
  51.5 0.8 %copy-done.4 = bf16[128,256]{1,0:T(8,128)(2,1)S(1)} copy-done((bf16[128,256]{1,0:T(8,128)(2,1)S(1)}, bf16[128,256]{1,0:T(8,128)(2,1)}, u32[]{:S(2)}) %copy-start.4) | copy-done | bytes 65560
  52.4 0.0 copy-start.6
  52.4 0.8 copy-done.6
  53.1 15.8 %disco.1.disco_ref = f32[64,32,256]{2,1,0:T(8,128)S(1)} custom-call(f32[68,75]{1,0:T(8,128)S(1)} %copy.12.tap_ref, bf16[64,32,256]{2,1,0:T(8,128)(2,1)S(1)} %copy-done.1, bf16[64,256]{1,0:T(8,128)(2,1)S(1)} %collective-permute-done.low_ref, bf16[64,256]{1,0:T(8,128)(2,1)S(1)} %copy-done.6, bf16[128,256]{1,0:T(8,128)(2,1)S(1)} %collective-permute-done.2.left_ref, ...), custom_call_target="tpu_custom_call" | custom-call | flops 524288000 | bytes 4194304 | tf_op jit(solution)/shard_map/disco/pallas_call | solution.py:485
  68.9 6.5 %all-to-all-done.1.back_hbm = bf16[32,128,128]{2,1,0:T(8,128)(2,1)S(1)} async-done(((bf16[32,128,128]{2,1,0:T(8,128)(2,1)}), bf16[32,128,128]{2,1,0:T(8,128)(2,1)S(1)}, u32[]{:S(2)}, u32[]{:S(2)}) %all-to-all-start.1) | async-done | bytes 1048608 | tf_op jit(solution)/shard_map/all_to_all | solution.py:652
  75.4 2.3 %combine.1 = bf16[64,32,256]{2,1,0:T(8,128)(2,1)} custom-call(s32[1]{0:T(128)} %bitcast.flip_ref, bf16[32,128,128]{2,1,0:T(8,128)(2,1)S(1)} %all-to-all-done.1.back_hbm, f32[64,32,256]{2,1,0:T(8,128)S(1)} %disco.1.disco_ref), custom_call_target="tpu_custom_call" | custom-call | tf_op jit(solution)/shard_map/combine/pallas_call | solution.py:548
  (15 shorter events, 0.2 us)
Async XLA Ops:
  0.0 29.0 %copy-start = (f32[128,2,256]{2,1,0:T(2,128)S(1)}, f32[128,2,256]{2,1,0:T(2,128)}, u32[]{:S(2)}) copy-start(f32[128,2,256]{2,1,0:T(2,128)} %param.9) | copy-start | bytes 786436
  0.0 12.5 %copy-start.10 = (f32[128]{0:T(128)S(1)}, f32[128]{0:T(128)}, u32[]{:S(2)}) copy-start(f32[128]{0:T(128)} %constant.121) | copy-start | bytes 1540
  4.4 34.1 %all-to-all-start = ((bf16[32,128,128]{2,1,0:T(8,128)(2,1)}), bf16[32,128,128]{2,1,0:T(8,128)(2,1)S(1)}, u32[]{:S(2)}, u32[]{:S(2)}) async-start(bf16[32,128,128]{2,1,0:T(8,128)(2,1)} %get-tuple-element.27), calls=%async_computation | async-start | bytes 2097152 | tf_op jit(solution)/shard_map/all_to_all | solution.py:608
  13.3 8.5 %copy-start.13 = (bf16[64,256]{1,0:T(8,128)(2,1)S(1)}, bf16[64,256]{1,0:T(8,128)(2,1)}, u32[]{:S(2)}) copy-start(bf16[64,256]{1,0:T(8,128)(2,1)} %get-tuple-element.34) | copy-start | bytes 98308
  13.3 8.7 %copy-start.14 = (bf16[64,256]{1,0:T(8,128)(2,1)S(1)}, bf16[64,256]{1,0:T(8,128)(2,1)}, u32[]{:S(2)}) copy-start(bf16[64,256]{1,0:T(8,128)(2,1)} %get-tuple-element.35) | copy-start | bytes 98308
  13.3 10.2 %copy-start.12 = (bf16[128,256]{1,0:T(8,128)(2,1)S(1)}, bf16[128,256]{1,0:T(8,128)(2,1)}, u32[]{:S(2)}) copy-start(bf16[128,256]{1,0:T(8,128)(2,1)} %get-tuple-element.36) | copy-start | bytes 196612
  13.3 12.0 %copy-start.11 = (bf16[128,256]{1,0:T(8,128)(2,1)S(1)}, bf16[128,256]{1,0:T(8,128)(2,1)}, u32[]{:S(2)}) copy-start(bf16[128,256]{1,0:T(8,128)(2,1)} %get-tuple-element.37) | copy-start | bytes 196612
  13.3 15.5 %copy-start.9 = (s32[256,5]{0,1:T(8,128)S(1)}, s32[256,5]{0,1:T(8,128)}, u32[]{:S(2)}) copy-start(s32[256,5]{0,1:T(8,128)} %param.12) | copy-start | bytes 15364
  13.3 15.7 %copy-start.8 = (f32[3,256,5,5]{1,0,3,2:T(4,128)S(1)}, f32[3,256,5,5]{1,0,3,2:T(4,128)}, u32[]{:S(2)}) copy-start(f32[3,256,5,5]{1,0,3,2:T(4,128)} %param.11) | copy-start | bytes 230404
  13.3 25.3 %copy-start.7 = (f32[1,128]{1,0:T(1,128)S(1)}, f32[1,128]{1,0:T(1,128)}, u32[]{:S(2)}) copy-start(f32[1,128]{1,0:T(1,128)} %constant.123.quad_ref) | copy-start | bytes 1540
  21.7 7.5 %collective-permute-start = (bf16[64,256]{1,0:T(8,128)(2,1)S(1)}, bf16[64,256]{1,0:T(8,128)(2,1)S(1)}, u32[]{:S(2)}, u32[]{:S(2)}) collective-permute-start(bf16[64,256]{1,0:T(8,128)(2,1)S(1)} %copy-done.13), channel_id=1, source_target_pairs={{0,8},{8,16},{16,24},{24,0},{1,9},{9,17},{17,25},{25,1},{2,10},{10... | collective-permute-start | bytes 98312 | tf_op jit(solution)/shard_map/ppermute | solution.py:571
  22.0 7.3 %collective-permute-start.1 = (bf16[64,256]{1,0:T(8,128)(2,1)S(1)}, bf16[64,256]{1,0:T(8,128)(2,1)S(1)}, u32[]{:S(2)}, u32[]{:S(2)}) collective-permute-start(bf16[64,256]{1,0:T(8,128)(2,1)S(1)} %copy-done.14), channel_id=1, source_target_pairs={{0,24},{8,0},{16,8},{24,16},{1,25},{9,1},{17,9},{25,17},{2,26},{10... | collective-permute-start | bytes 98312 | tf_op jit(solution)/shard_map/ppermute | solution.py:571
  23.5 14.2 %collective-permute-start.2 = (bf16[128,256]{1,0:T(8,128)(2,1)S(1)}, bf16[128,256]{1,0:T(8,128)(2,1)S(1)}, u32[]{:S(2)}, u32[]{:S(2)}) collective-permute-start(bf16[128,256]{1,0:T(8,128)(2,1)S(1)} %copy-done.12), channel_id=1, source_target_pairs={{0,1},{1,2},{2,3},{3,4},{4,5},{5,6},{6,7},{7,0},{8,9},{9,10},{10,1... | collective-permute-start | bytes 196616 | tf_op jit(solution)/shard_map/ppermute | solution.py:571
  25.3 12.4 %collective-permute-start.3 = (bf16[128,256]{1,0:T(8,128)(2,1)S(1)}, bf16[128,256]{1,0:T(8,128)(2,1)S(1)}, u32[]{:S(2)}, u32[]{:S(2)}) collective-permute-start(bf16[128,256]{1,0:T(8,128)(2,1)S(1)} %copy-done.11), channel_id=1, source_target_pairs={{0,7},{1,0},{2,1},{3,2},{4,3},{5,4},{6,5},{7,6},{8,15},{9,8},{10,9... | collective-permute-start | bytes 196616 | tf_op jit(solution)/shard_map/ppermute | solution.py:571
  29.3 16.0 %copy-start.5 = (bf16[64,256]{1,0:T(8,128)(2,1)}, bf16[64,256]{1,0:T(8,128)(2,1)S(1)}, u32[]{:S(2)}) copy-start(bf16[64,256]{1,0:T(8,128)(2,1)S(1)} %collective-permute-done.1.high_ref) | copy-start | bytes 98308
  29.3 3.7 %collective-permute-start.5 = (bf16[8,256]{1,0:T(8,128)(2,1)S(1)}, bf16[8,256]{1,0:T(8,128)(2,1)S(1)}, u32[]{:S(2)}, u32[]{:S(2)}) collective-permute-start(bf16[8,256]{1,0:T(8,128)(2,1)S(1)} %reshape.338), channel_id=1, source_target_pairs={{0,7},{1,0},{2,1},{3,2},{4,3},{5,4},{6,5},{7,6},{8,15},{9,8},{10,9... | collective-permute-start | bytes 12296 | tf_op jit(solution)/shard_map/ppermute | solution.py:571
  31.3 6.4 %collective-permute-start.4 = (bf16[8,256]{1,0:T(8,128)(2,1)S(1)}, bf16[8,256]{1,0:T(8,128)(2,1)S(1)}, u32[]{:S(2)}, u32[]{:S(2)}) collective-permute-start(bf16[8,256]{1,0:T(8,128)(2,1)S(1)} %reshape.337), channel_id=1, source_target_pairs={{0,1},{1,2},{2,3},{3,4},{4,5},{5,6},{6,7},{7,0},{8,9},{9,10},{10,1... | collective-permute-start | bytes 12296 | tf_op jit(solution)/shard_map/ppermute | solution.py:571
  37.7 7.7 %copy-start.3 = (bf16[128,256]{1,0:T(8,128)(2,1)}, bf16[128,256]{1,0:T(8,128)(2,1)S(1)}, u32[]{:S(2)}) copy-start(bf16[128,256]{1,0:T(8,128)(2,1)S(1)} %collective-permute-done.3.right_ref) | copy-start | bytes 196612
  45.3 30.1 %all-to-all-start.1 = ((bf16[32,128,128]{2,1,0:T(8,128)(2,1)}), bf16[32,128,128]{2,1,0:T(8,128)(2,1)S(1)}, u32[]{:S(2)}, u32[]{:S(2)}) async-start(bf16[32,128,128]{2,1,0:T(8,128)(2,1)} %bitcast.7), calls=%async_computation.1 | async-start | bytes 2097152 | tf_op jit(solution)/shard_map/all_to_all | solution.py:652
  49.3 1.2 %copy-start.1 = (bf16[64,32,256]{2,1,0:T(8,128)(2,1)S(1)}, bf16[64,32,256]{2,1,0:T(8,128)(2,1)}, u32[]{:S(2)}) copy-start(bf16[64,32,256]{2,1,0:T(8,128)(2,1)} %get-tuple-element.43.grad_ref) | copy-start | bytes 3145732
  50.5 1.0 %copy-start.2 = (bf16[3,256,256]{2,1,0:T(8,128)(2,1)S(1)}, bf16[3,256,256]{2,1,0:T(8,128)(2,1)}, u32[]{:S(2)}) copy-start(bf16[3,256,256]{2,1,0:T(8,128)(2,1)} %mix_ref.1) | copy-start | bytes 1179652
  51.5 0.8 %copy-start.4 = (bf16[128,256]{1,0:T(8,128)(2,1)S(1)}, bf16[128,256]{1,0:T(8,128)(2,1)}, u32[]{:S(2)}) copy-start(bf16[128,256]{1,0:T(8,128)(2,1)} %copy-done.3) | copy-start | bytes 196612
  52.4 0.8 copy-start.6
